TPU v7x, 512 devices: a whole 4x8x8 slice. The times are simulated.
512 devices in a mesh: xy: 32 (over y, x), gz: 16 (over z, core).
Axes of the slice: x: 4, y: 8, z: 8, core: 2. Of those that a mesh axis runs over, the one named last changes fastest.
Arguments:
- volume: float32 [1536, 32768], P('gz', 'xy'), may hold values from 0 to 1
- sinogram: float32 [1536, 8192], P('gz', 'xy'), may hold values from 100 to 2000
- ray_mats: bfloat16 [32, 16, 256, 256], P('xy'), may hold values from 0.049804688 to 1
- offsets: int32 [32, 16], P('xy'), may hold values from 0 to 768
- ray_lists: int32 [32, 16], replicated, may hold values from 0 to 31, all different within a row
- owner_map: int32 [32], replicated, may hold values from 0 to 31, each once
Outputs:
- new_volume: float32 [1536, 32768], P('gz', 'xy')
- weighted: float32 [1536, 8192], P('gz', 'xy')
Inputs may be any that keep to these rules, and one draw needn't show every extreme that they name: `ray_lists`: the 16 entries of a row are distinct, and every ray block is named by some row. `owner_map`: each owner appears once.
All inputs are finite; a program needn't handle non-finite values.
Results may differ from a plain program's by a relative error of at most 0.0003.
Values sent between devices are 32-bit elements; how exact they have to be, the bound alone decides.
No kernel may reach another device: no remote copies, remote signals or barrier semaphores. Data moves between devices by JAX's collectives and lax.ppermute only.
A program may use at most 64 MiB of HBM per device.

v0:
```python
import jax
import jax.numpy as jnp
from jax import lax
from jax.sharding import PartitionSpec as P

relax = 1.0
tv_weight = 0.2
smooth_sq = 0.01


def padded_2(cells, sides, width):
    for axis, dim in sides:
        count = lax.axis_size(axis)
        ends = count - 1
        head = lax.slice_in_dim(cells, 0, width, axis=dim)
        tail = lax.slice_in_dim(cells, cells.shape[dim] - width, cells.shape[dim], axis=dim)
        cells = jnp.concatenate(
            [
                lax.ppermute(tail, axis, [(i, (i + 1) % count) for i in range(ends)]),
                cells,
                lax.ppermute(head, axis, [((i + 1) % count, i) for i in range(ends)]),
            ],
            axis=dim,
        )
    return cells


def cut_windows(field, starts, width):
    return jax.vmap(lambda start: lax.dynamic_slice_in_dim(field, start, width, 1))(starts)


def spread_back(smeared, column_terms, starts, vxy):
    depth = smeared.shape[1]
    width = smeared.shape[2]

    def add_one(index, carry):
        update, column = carry
        start = starts[index]
        piece = lax.dynamic_slice_in_dim(update, start, width, 1) + smeared[index]
        update = lax.dynamic_update_slice_in_dim(update, piece, start, 1)
        col_piece = lax.dynamic_slice_in_dim(column, start, width, 0) + column_terms[index]
        column = lax.dynamic_update_slice_in_dim(column, col_piece, start, 0)
        return (update, column)

    init = (jnp.zeros((depth, vxy), jnp.float32), jnp.zeros((vxy,), jnp.float32))
    return lax.fori_loop(0, smeared.shape[0], add_one, init)


def total_variation(padded):
    diffs = padded[1:] - padded[:-1]
    slopes = diffs / jnp.sqrt(diffs * diffs + smooth_sq)
    return slopes[:-1] - slopes[1:]


def per_device(volume, sinogram, ray_mats, offsets, ray_lists, owner_map):
    faces = padded_2(volume, (("gz", 0),), 1)
    count = lax.axis_size("xy")
    myself = lax.axis_index("xy")
    labels = jnp.arange(count, dtype=jnp.int32)
    mine = lax.dynamic_index_in_dim(ray_lists, myself, 0, keepdims=False)
    owners = jnp.sum(jnp.where(mine[:, None] == labels[None, :], owner_map[None, :], 0), axis=1)
    matrix = ray_mats[0].astype(jnp.float32)
    starts = offsets[0]
    windows = cut_windows(volume, starts, matrix.shape[1])
    partial_value = jnp.einsum("kzw,kwr->kzr", windows, matrix, precision=lax.Precision.HIGHEST)
    row_terms = jnp.sum(matrix, axis=1)
    outgoing = (
        jnp.zeros((count,) + partial_value.shape[1:], jnp.float32).at[owners].set(partial_value)
    )
    out_rows = jnp.zeros((count, 1, row_terms.shape[1]), jnp.float32).at[owners, 0].set(row_terms)
    arrived, arrived_rows = (
        lax.all_to_all(outgoing, "xy", split_axis=0, concat_axis=0, tiled=True),
        lax.all_to_all(out_rows, "xy", split_axis=0, concat_axis=0, tiled=True),
    )
    projection = jnp.sum(arrived, axis=0)
    rowsum = jnp.sum(arrived_rows, axis=0)[0]
    weighted = (sinogram - projection) / rowsum[None, :]
    all_owners = jnp.sum(
        jnp.where(ray_lists[:, :, None] == labels[None, None, :], owner_map[None, None, :], 0),
        axis=2,
    )
    helpers = jnp.any(all_owners == myself, axis=1)
    returning = jnp.where(helpers[:, None, None], weighted[None], 0.0)
    returned = lax.all_to_all(returning, "xy", split_axis=0, concat_axis=0, tiled=True)
    needed = returned[owners]
    smeared = jnp.einsum("kzr,kwr->kzw", needed, matrix, precision=lax.Precision.HIGHEST)
    update, column = spread_back(smeared, jnp.sum(matrix, axis=2), starts, volume.shape[1])
    update = update / jnp.maximum(column, 1.0)[None, :]
    new_volume = volume + relax * update - tv_weight * total_variation(faces)
    return (new_volume, weighted)


def solution(mesh):
    in_specs = (P("gz", "xy"), P("gz", "xy"), P("xy", None, None, None), P("xy", None), P(), P())
    out_specs = (P("gz", "xy"), P("gz", "xy"))
    return jax.shard_map(
        per_device, mesh=mesh, in_specs=in_specs, out_specs=out_specs, check_vma=False
    )
```

profile of v0, /device:TPU:1, one launch (start us, length us, event | category | flops | bytes accessed | tf_op | source)
XLA Modules:
  0.0 303.2 jit_solution(2269196420937081070)
XLA Ops:
  2.4 2.6 convert_reduce_fusion
  6.3 10.5 %all-to-all-start.1 = ((f32[32,1,256]{2,1,0:T(1,128)}), f32[32,1,256]{2,1,0:T(1,128)S(1)}, u32[]{:S(2)}, u32[]{:S(2)}) async-start(f32[32,1,256]{2,1,0:T(1,128)} %reshape.91), calls=%async_computation.1 | async-start | bytes 65536 | tf_op jit(solution)/shard_map/all_to_all | solution.py:73
  16.9 31.2 %while.17 = (s32[]{:T(128)}, f32[96,1024]{1,0:T(8,128)S(1)}, s32[16,2]{0,1:T(2,128)S(1)}, f32[16,96,256]{2,1,0:T(8,128)}, s32[]{:T(128)}) while((s32[]{:T(128)}, f32[96,1024]{1,0:T(8,128)S(1)}, s32[16,2]{0,1:T(2,128)S(1)}, f32[16,96,256]{2,1,0:T(8,128)}, s32[]{:T(128)}) %tuple.51), condition=%wide.while_cond, body=%wide.while_body.sunk | while | flops 2 | bytes 197721 | solution.py:29
  17.5 1.3 bitcast_dynamic-update-slice_fusion.2
  19.5 1.3 bitcast_dynamic-update-slice_fusion.2
  21.4 1.3 bitcast_dynamic-update-slice_fusion.2
  23.4 1.4 bitcast_dynamic-update-slice_fusion.2
  25.3 1.3 bitcast_dynamic-update-slice_fusion.2
  27.3 1.3 bitcast_dynamic-update-slice_fusion.2
  29.2 1.3 bitcast_dynamic-update-slice_fusion.2
  31.2 1.3 bitcast_dynamic-update-slice_fusion.2
  33.1 1.3 bitcast_dynamic-update-slice_fusion.2
  35.1 1.3 bitcast_dynamic-update-slice_fusion.2
  37.0 1.3 bitcast_dynamic-update-slice_fusion.2
  39.0 1.3 bitcast_dynamic-update-slice_fusion.2
  40.9 1.3 bitcast_dynamic-update-slice_fusion.2
  42.9 1.3 bitcast_dynamic-update-slice_fusion.2
  44.8 1.3 bitcast_dynamic-update-slice_fusion.2
  46.8 1.3 bitcast_dynamic-update-slice_fusion.2
  48.1 3.7 %fusion.2 = f32[16,96,256]{2,1,0:T(8,128)} fusion(f32[16,96,256]{2,1,0:T(8,128)} %get-tuple-element.121, bf16[1,16,256,256]{3,2,1,0:T(8,128)(2,1)S(1)} %copy-done), kind=kOutput, calls=%fused_computation.12 | convolution fusion | flops 1207959552 | bytes 5242880 | tf_op jit(solution)/shard_map/kzw,kwr->kzr/dot_general | solution.py:65
  51.9 2.0 broadcast_in_dim.72
  53.9 3.9 %scatter_fusion = f32[32,96,256]{2,1,0:T(8,128)} fusion(f32[32,96,256]{2,1,0:T(8,128)} %broadcast_in_dim.72, s32[16]{0:T(128)S(1)} %fusion.8, f32[16,96,256]{2,1,0:T(8,128)} %fusion.2), kind=kCustom, calls=%fused_computation.1 | custom fusion | bytes 4718656 | tf_op jit(solution)/shard_map/scatter | solution.py:68
  57.9 9.5 %all-to-all-start = ((f32[32,96,256]{2,1,0:T(8,128)}), f32[32,96,256]{2,1,0:T(8,128)}, u32[]{:S(2)}, u32[]{:S(2)}) async-start(f32[32,96,256]{2,1,0:T(8,128)} %scatter_fusion), calls=%async_computation | async-start | bytes 6291456 | tf_op jit(solution)/shard_map/all_to_all | solution.py:72
  68.3 69.8 %all-to-all-done = f32[32,96,256]{2,1,0:T(8,128)} async-done(((f32[32,96,256]{2,1,0:T(8,128)}), f32[32,96,256]{2,1,0:T(8,128)}, u32[]{:S(2)}, u32[]{:S(2)}) %all-to-all-start) | async-done | bytes 3145760 | tf_op jit(solution)/shard_map/all_to_all | solution.py:72
  138.1 2.1 reduce_sum.59
  140.2 2.1 broadcast_select_fusion
  142.3 6.7 %all-to-all-start.2 = ((f32[32,96,256]{2,1,0:T(8,128)}), f32[32,96,256]{2,1,0:T(8,128)}, u32[]{:S(2)}, u32[]{:S(2)}) async-start(f32[32,96,256]{2,1,0:T(8,128)} %broadcast_select_fusion), calls=%async_computation.2 | async-start | bytes 6291456 | tf_op jit(solution)/shard_map/all_to_all | solution.py:84
  149.0 4.4 %collective-permute-start = (f32[1,1024]{1,0:T(1,128)S(1)}, f32[1,1024]{1,0:T(1,128)S(1)}, u32[]{:S(2)}, u32[]{:S(2)}) collective-permute-start(f32[1,1024]{1,0:T(1,128)S(1)} %get-tuple-element.144), channel_id=1, source_target_pairs={{1,0},{2,1},{3,2},{4,3},{5,4},{6,5},{7,6},{8,7},{9,8},{10,9},{11,1... | collective-permute-start | bytes 12296 | tf_op jit(solution)/shard_map/ppermute | solution.py:21
  153.4 3.9 %collective-permute-start.1 = (f32[1,1024]{1,0:T(1,128)S(1)}, f32[1,1024]{1,0:T(1,128)S(1)}, u32[]{:S(2)}, u32[]{:S(2)}) collective-permute-start(f32[1,1024]{1,0:T(1,128)S(1)} %get-tuple-element.145), channel_id=1, source_target_pairs={{0,1},{1,2},{2,3},{3,4},{4,5},{5,6},{6,7},{7,8},{8,9},{9,10},{10,1... | collective-permute-start | bytes 12296 | tf_op jit(solution)/shard_map/ppermute | solution.py:19
  158.2 60.3 %all-to-all-done.2 = f32[32,96,256]{2,1,0:T(8,128)} async-done(((f32[32,96,256]{2,1,0:T(8,128)}), f32[32,96,256]{2,1,0:T(8,128)}, u32[]{:S(2)}, u32[]{:S(2)}) %all-to-all-start.2) | async-done | bytes 3145760 | tf_op jit(solution)/shard_map/all_to_all | solution.py:84
  218.5 3.7 %gather_fusion = f32[16,96,256]{2,1,0:T(8,128)} fusion(f32[32,96,256]{2,1,0:T(8,128)} %all-to-all-done.2, s32[1024]{0:T(1024)S(1)} %pad_clamp_fusion), kind=kCustom, calls=%fused_computation | custom fusion | bytes 3145792 | tf_op jit(solution)/shard_map/gather | solution.py:85
  222.2 4.6 %fusion = f32[16,96,256]{2,1,0:T(8,128)} fusion(f32[16,96,256]{2,1,0:T(8,128)} %gather_fusion, bf16[1,16,256,256]{3,2,1,0:T(8,128)(2,1)S(1)} %copy-done), kind=kOutput, calls=%fused_computation.10 | convolution fusion | flops 1207959552 | bytes 5242880 | tf_op jit(solution)/shard_map/kzr,kwr->kzw/dot_general | solution.py:86
  226.8 75.5 %while.16 = (s32[]{:T(128)}, f32[96,1024]{1,0:T(8,128)S(1)}, f32[1024]{0:T(1024)S(1)}, s32[16]{0:T(128)S(1)}, f32[16,96,256]{2,1,0:T(8,128)}, /*index=5*/f32[16,256]{1,0:T(8,128)S(1)}, s32[]{:T(128)}, s32[]{:T(128)}, s32[]{:T(128)}) while((s32[]{:T(128)}, f32[96,1024]{1,0:T(8,128)S(1)}, f32[1024]{0:T(1024)S(1)}, s32[16]{0:T(128)S(1)}, ...), condition=%wide.region_10.11_spmd, body=%wide.region_9.10_spmd.sunk | while | flops 24837 | bytes 496799 | solution.py:46
  229.3 1.0 bitcast_add_fusion.2
  230.3 1.1 dynamic_update_slice.18
  234.0 1.0 bitcast_add_fusion.2
  235.0 1.1 dynamic_update_slice.18
  238.7 1.0 bitcast_add_fusion.2
  239.7 1.1 dynamic_update_slice.18
  243.5 1.0 bitcast_add_fusion.2
  244.5 1.1 dynamic_update_slice.18
  248.2 1.0 bitcast_add_fusion.2
  249.2 1.1 dynamic_update_slice.18
  252.9 1.0 bitcast_add_fusion.2
  253.9 1.1 dynamic_update_slice.18
  257.7 1.0 bitcast_add_fusion.2
  258.7 1.1 dynamic_update_slice.18
  262.4 1.0 bitcast_add_fusion.2
  263.4 1.1 dynamic_update_slice.18
  267.1 1.0 bitcast_add_fusion.2
  268.1 1.1 dynamic_update_slice.18
  271.8 1.0 bitcast_add_fusion.2
  272.8 1.1 dynamic_update_slice.18
  276.6 1.0 bitcast_add_fusion.2
  281.1 1.0 bitcast_add_fusion.2
  282.1 1.1 dynamic_update_slice.18
  285.9 1.0 bitcast_add_fusion.2
  286.9 1.1 dynamic_update_slice.18
  290.6 1.0 bitcast_add_fusion.2
  291.6 1.1 dynamic_update_slice.18
  295.3 1.0 bitcast_add_fusion.2
  296.3 1.1 dynamic_update_slice.18
  300.0 1.0 bitcast_add_fusion.2
  301.0 1.1 dynamic_update_slice.18
  (119 shorter events, 29.5 us)
Async XLA Ops:
  0.6 16.2 %copy-start.6 = (s32[1,16]{1,0:T(1,128)S(1)}, s32[1,16]{1,0:T(1,128)}, u32[]{:S(2)}) copy-start(s32[1,16]{1,0:T(1,128)} %param.11) | copy-start | bytes 196
  0.6 16.2 %copy-start.1 = (f32[96,1024]{1,0:T(8,128)S(1)}, f32[96,1024]{1,0:T(8,128)}, u32[]{:S(2)}) copy-start(f32[96,1024]{1,0:T(8,128)} %param.8) | copy-start | bytes 1179652
  2.4 45.7 %copy-start = (bf16[1,16,256,256]{3,2,1,0:T(8,128)(2,1)S(1)}, bf16[1,16,256,256]{3,2,1,0:T(8,128)(2,1)}, u32[]{:S(2)}) copy-start(bf16[1,16,256,256]{3,2,1,0:T(8,128)(2,1)} %param.10) | copy-start | bytes 6291460
  6.3 51.5 %all-to-all-start.1 = ((f32[32,1,256]{2,1,0:T(1,128)}), f32[32,1,256]{2,1,0:T(1,128)S(1)}, u32[]{:S(2)}, u32[]{:S(2)}) async-start(f32[32,1,256]{2,1,0:T(1,128)} %reshape.91), calls=%async_computation.1 | async-start | bytes 65536 | tf_op jit(solution)/shard_map/all_to_all | solution.py:73
  57.9 9.5 %copy-start.4 = (s32[32,16]{0,1:T(8,128)S(1)}, s32[32,16]{0,1:T(8,128)}, u32[]{:S(2)}) copy-start(s32[32,16]{0,1:T(8,128)} %param.12) | copy-start | bytes 6148
  57.9 9.6 %copy-start.5 = (s32[32]{0:T(128)S(1)}, s32[32]{0:T(128)}, u32[]{:S(2)}) copy-start(s32[32]{0:T(128)} %param.13) | copy-start | bytes 388
  57.9 80.2 %all-to-all-start = ((f32[32,96,256]{2,1,0:T(8,128)}), f32[32,96,256]{2,1,0:T(8,128)}, u32[]{:S(2)}, u32[]{:S(2)}) async-start(f32[32,96,256]{2,1,0:T(8,128)} %scatter_fusion), calls=%async_computation | async-start | bytes 6291456 | tf_op jit(solution)/shard_map/all_to_all | solution.py:72
  68.3 71.9 %copy-start.3 = (f32[96,256]{1,0:T(8,128)S(1)}, f32[96,256]{1,0:T(8,128)}, u32[]{:S(2)}) copy-start(f32[96,256]{1,0:T(8,128)} %param.9) | copy-start | bytes 294916
  140.2 2.1 copy-start.2
  142.3 76.2 %all-to-all-start.2 = ((f32[32,96,256]{2,1,0:T(8,128)}), f32[32,96,256]{2,1,0:T(8,128)}, u32[]{:S(2)}, u32[]{:S(2)}) async-start(f32[32,96,256]{2,1,0:T(8,128)} %broadcast_select_fusion), calls=%async_computation.2 | async-start | bytes 6291456 | tf_op jit(solution)/shard_map/all_to_all | solution.py:84
  149.0 8.3 %collective-permute-start = (f32[1,1024]{1,0:T(1,128)S(1)}, f32[1,1024]{1,0:T(1,128)S(1)}, u32[]{:S(2)}, u32[]{:S(2)}) collective-permute-start(f32[1,1024]{1,0:T(1,128)S(1)} %get-tuple-element.144), channel_id=1, source_target_pairs={{1,0},{2,1},{3,2},{4,3},{5,4},{6,5},{7,6},{8,7},{9,8},{10,9},{11,1... | collective-permute-start | bytes 12296 | tf_op jit(solution)/shard_map/ppermute | solution.py:21
  153.4 4.7 %collective-permute-start.1 = (f32[1,1024]{1,0:T(1,128)S(1)}, f32[1,1024]{1,0:T(1,128)S(1)}, u32[]{:S(2)}, u32[]{:S(2)}) collective-permute-start(f32[1,1024]{1,0:T(1,128)S(1)} %get-tuple-element.145), channel_id=1, source_target_pairs={{0,1},{1,2},{2,3},{3,4},{4,5},{5,6},{6,7},{7,8},{8,9},{9,10},{10,1... | collective-permute-start | bytes 12296 | tf_op jit(solution)/shard_map/ppermute | solution.py:19
where the time goes:
time: 308 us; the launch traced here: 303 us
  waiting for transfers between devices  131 us (43%)
  local copies, waits for them, and re-layouts  70.4 us (23%)
  starting transfers between devices  35 us (11%)
  loops' own time  29.6 us (10%)
  other arithmetic  28.3 us (9%)
  matrix products  8.33 us (3%)
    all_to_all x1, waiting for transfers between devices, per_device(): lax.all_to_all(outgoing, 'xy', split_axis=0, concat_axis=0, tiled=True)  69.8 us
    all_to_all x1, waiting for transfers between devices, per_device(): lax.all_to_all(returning, 'xy', split_axis=0, concat_axis=0, tiled=True)  60.3 us
    gather x48, local copies, waits for them, and re-layouts  31.2 us
    another operation x1, loops' own time, spread_back(): return lax.fori_loop(0, smeared.shape[0], add_one, init)  29.6 us
    dynamic_update_slice x16, local copies, waits for them, and re-layouts, add_one(): update = lax.dynamic_update_slice_in_dim(update, piece, start, 1)  17.1 us
    add x16, other arithmetic, add_one(): piece = lax.dynamic_slice_in_dim(update, start, width, 1) + smeared[index]  15.9 us
    all_to_all x1, starting transfers between devices, per_device(): lax.all_to_all(out_rows, 'xy', split_axis=0, concat_axis=0, tiled=True)  10.5 us
    dynamic_slice x16, local copies, waits for them, and re-layouts, add_one(): start = starts[index]  9.77 us
  transfers between devices with their start and end apart: 5, of which 3 were waited for; matrix products, arithmetic and copies ran while one was open for 14% of the time, Pallas kernels for 0%

commit v1 on v0

v1 whole, which is shorter than its diff:
```python
import jax
import jax.numpy as jnp
from jax import lax
from jax.experimental import pallas as pl
from jax.experimental.pallas import tpu as pltpu
from jax.sharding import PartitionSpec as P

relax = 1.0
tv_weight = 0.2
smooth_sq = 0.01

NX, NY = 4, 8
PAIRS = NY // 2
W = 256
LANES = 128
VMEM_LIMIT = 40 * 1024 * 1024


def device_of(pair, odd, x):
    return (2 * pair + odd) * NX + x


NEAR = [[device_of(p, q, x) for q in range(2) for x in range(NX)] for p in range(PAIRS)]
FAR = [[device_of(p, q, x) for p in range(PAIRS)] for q in range(2) for x in range(NX)]


def exchange(value, groups):
    return lax.all_to_all(
        value, "xy", split_axis=0, concat_axis=0, axis_index_groups=groups, tiled=True
    )


def split3(value):
    high = value.astype(jnp.bfloat16)
    rest = value - high.astype(jnp.float32)
    mid = rest.astype(jnp.bfloat16)
    low = (rest - mid.astype(jnp.float32)).astype(jnp.bfloat16)
    return [high, mid, low]


def with_ones(value):
    ones = jnp.ones((16, value.shape[1]), jnp.bfloat16)
    return jnp.concatenate(split3(value) + [ones], axis=0)


def near_far(owner):
    y, x = owner // NX, owner % NX
    return (y % 2) * NX + x, y // 2


def project_kernel(me_ref, lists_ref, owners_ref, starts_ref, vol_ref, mats_ref, out_ref, wide):
    rows = vol_ref.shape[0]
    count = starts_ref.shape[1]
    wide[:, : vol_ref.shape[1]] = vol_ref[...]
    wide[:, vol_ref.shape[1] :] = jnp.zeros((rows, LANES), jnp.float32)
    out_ref[...] = jnp.zeros(out_ref.shape, jnp.float32)
    me = me_ref[0]

    def step(k, carry):
        start = starts_ref[0, k]
        near, far = near_far(owners_ref[lists_ref[me, k]])
        base = pl.multiple_of((start // LANES) * LANES, LANES)
        window = wide[:, pl.ds(base, W + LANES)]
        window = pltpu.roll(window, (W + LANES) - start % LANES, 1)[:, :W]
        product = jnp.dot(
            with_ones(window), mats_ref[0, k], preferred_element_type=jnp.float32
        )
        value = product[2 * rows : 3 * rows] + product[rows : 2 * rows] + product[:rows]
        out_ref[near, pl.ds(pl.multiple_of(far * rows, 8), rows), :] = value
        out_ref[near, pl.ds(PAIRS * rows + far, 1), :] = product[3 * rows : 3 * rows + 1]
        return carry

    lax.fori_loop(0, count, step, 0, unroll=2)


def project(me, lists, owners, starts, volume, mats):
    rows, cols = volume.shape
    smem = pl.BlockSpec(memory_space=pltpu.SMEM)
    vmem = pl.BlockSpec(memory_space=pltpu.VMEM)
    return pl.pallas_call(
        project_kernel,
        out_shape=jax.ShapeDtypeStruct((2 * NX, PAIRS * rows + 8, W), jnp.float32),
        in_specs=[smem] * 4 + [vmem] * 2,
        out_specs=vmem,
        scratch_shapes=[pltpu.VMEM((rows, cols + LANES), jnp.float32)],
        compiler_params=pltpu.CompilerParams(vmem_limit_bytes=VMEM_LIMIT),
    )(me, lists, owners, starts, volume, mats)


def back_kernel(
    me_ref, lists_ref, owners_ref, starts_ref, base_ref, mats_ref, got_ref, out_ref, total
):
    rows, cols = base_ref.shape
    count = starts_ref.shape[1]
    total[...] = jnp.zeros(total.shape, jnp.float32)
    me = me_ref[0]

    def step(k, carry):
        start = starts_ref[0, k]
        near, far = near_far(owners_ref[lists_ref[me, k]])
        base = pl.multiple_of((start // LANES) * LANES, LANES)
        product = lax.dot_general(
            with_ones(got_ref[near, far]),
            mats_ref[0, k],
            (((1,), (1,)), ((), ())),
            preferred_element_type=jnp.float32,
        )
        value = product[2 * rows : 3 * rows] + product[rows : 2 * rows] + product[:rows]
        value = jnp.concatenate([value, product[3 * rows : 3 * rows + 8]], axis=0)
        value = jnp.concatenate([value, jnp.zeros((rows + 8, LANES), jnp.float32)], axis=1)
        total[:, pl.ds(base, W + LANES)] += pltpu.roll(value, start % LANES, 1)
        return carry

    lax.fori_loop(0, count, step, 0, unroll=2)
    column = jnp.maximum(total[rows : rows + 1, :cols], 1.0)
    out_ref[...] = base_ref[...] + relax * (total[:rows, :cols] / column)


def back_project(me, lists, owners, starts, base, mats, got):
    rows, cols = base.shape
    smem = pl.BlockSpec(memory_space=pltpu.SMEM)
    vmem = pl.BlockSpec(memory_space=pltpu.VMEM)
    return pl.pallas_call(
        back_kernel,
        out_shape=jax.ShapeDtypeStruct((rows, cols), jnp.float32),
        in_specs=[smem] * 4 + [vmem] * 3,
        out_specs=vmem,
        scratch_shapes=[pltpu.VMEM((rows + 8, cols + LANES), jnp.float32)],
        compiler_params=pltpu.CompilerParams(vmem_limit_bytes=VMEM_LIMIT),
    )(me, lists, owners, starts, base, mats, got)


def with_faces(volume):
    count = lax.axis_size("gz")
    up = [(i, i + 1) for i in range(count - 1)]
    down = [(i + 1, i) for i in range(count - 1)]
    return jnp.concatenate(
        [
            lax.ppermute(volume[-1:], "gz", up),
            volume,
            lax.ppermute(volume[:1], "gz", down),
        ],
        axis=0,
    )


def total_variation(padded):
    diffs = padded[1:] - padded[:-1]
    slopes = diffs / jnp.sqrt(diffs * diffs + smooth_sq)
    return slopes[:-1] - slopes[1:]


def per_device(volume, sinogram, ray_mats, offsets, ray_lists, owner_map):
    rows = volume.shape[0]
    me = lax.axis_index("xy").astype(jnp.int32).reshape(1)
    outgoing = project(me, ray_lists, owner_map, offsets, volume, ray_mats)
    arrived = jnp.sum(exchange(outgoing, NEAR), axis=0)
    values = arrived[: PAIRS * rows].reshape(PAIRS, rows, W)
    sums = arrived[PAIRS * rows : PAIRS * rows + PAIRS].reshape(PAIRS, 1, W)
    outgoing = jnp.concatenate([values, jnp.pad(sums, ((0, 0), (0, 7), (0, 0)))], axis=1)
    arrived = jnp.sum(exchange(outgoing, FAR), axis=0)
    weighted = (sinogram - arrived[:rows]) / arrived[rows : rows + 1]
    spread = jnp.broadcast_to(weighted[None], (PAIRS, rows, W))
    column = exchange(spread, FAR)
    spread = jnp.broadcast_to(column[None], (2 * NX, PAIRS, rows, W))
    got = exchange(spread, NEAR)
    base = volume - tv_weight * total_variation(with_faces(volume))
    new_volume = back_project(me, ray_lists, owner_map, offsets, base, ray_mats, got)
    return (new_volume, weighted)


def solution(mesh):
    in_specs = (P("gz", "xy"), P("gz", "xy"), P("xy", None, None, None), P("xy", None), P(), P())
    out_specs = (P("gz", "xy"), P("gz", "xy"))
    return jax.shard_map(
        per_device, mesh=mesh, in_specs=in_specs, out_specs=out_specs, check_vma=False
    )
```

time: 308 us -> 142 us (0.46); the launches traced: 303 us -> 141 us
  waiting for transfers between devices: 131 us -> 26.7 us
  blocking collectives: 0 us -> 76.8 us
  local copies, waits for them, and re-layouts: 70.4 us -> 13 us
  loops' own time: 29.6 us -> 0 us
  other arithmetic: 28.3 us -> 1.97 us
  starting transfers between devices: 35 us -> 13.3 us
  Pallas kernels: 0 us -> 8.61 us
  matrix products: 8.33 us -> 0 us
    all_to_all x3 -> x1, waiting for transfers between devices: 130 us -> 26 us  [exchange(): lax.all_to_all(value, 'xy', split_axis=0, concat_axis=0, axis_index_group...]
    all_to_all x0 -> x3, blocking collectives: none -> 76.8 us  [exchange(): lax.all_to_all(value, 'xy', split_axis=0, concat_axis=0, axis_index_group...]
    gather x49 -> x0, local copies, waits for them, and re-layouts: 34.9 us -> none
    another operation x2 -> x0, loops' own time: 29.6 us -> none  [the longest x1 29.6 us: spread_back(): return lax.fori_loop(0, smeared.shape[0], add_one, init)]
    all_to_all x3 -> x1, starting transfers between devices: 26.7 us -> 3.78 us  [exchange(): lax.all_to_all(value, 'xy', split_axis=0, concat_axis=0, axis_index_group...]
    dynamic_update_slice x16 -> x0, local copies, waits for them, and re-layouts: 17.1 us -> none  [add_one(): update = lax.dynamic_update_slice_in_dim(update, piece, start, 1)]
    add x16 -> x0, other arithmetic: 15.9 us -> none  [add_one(): piece = lax.dynamic_slice_in_dim(update, start, width, 1) + smeared[index]]
    dynamic_slice x33 -> x0, local copies, waits for them, and re-layouts: 10.9 us -> none  [the longest x16 9.77 us: add_one(): start = starts[index]]
  transfers between devices with their start and end apart: 5 -> 3, of which waited for: 3 -> 2; matrix products, arithmetic and copies ran while one was open for 14% -> 1% of each run, Pallas kernels for 0% -> 0%
where the time goes in v1:
time: 142 us; the launch traced here: 141 us
  blocking collectives  76.8 us (54%)
  waiting for transfers between devices  26.7 us (19%)
  starting transfers between devices  13.3 us (9%)
  local copies, waits for them, and re-layouts  13 us (9%)
  Pallas kernels  8.61 us (6%)
  other arithmetic  1.97 us (1%)
    all_to_all x3, blocking collectives, exchange(): lax.all_to_all(value, 'xy', split_axis=0, concat_axis=0, axis_index_group...  76.8 us
    all_to_all x1, waiting for transfers between devices, exchange(): lax.all_to_all(value, 'xy', split_axis=0, concat_axis=0, axis_index_group...  26 us
    unnamed x23, local copies, waits for them, and re-layouts  9.21 us
    ppermute x1, starting transfers between devices, with_faces(): lax.ppermute(volume[:1], 'gz', down)  5.66 us
    pallas_call x1, Pallas kernels, back_project(): pl.pallas_call(back_kernel, out_shape=jax.ShapeDtypeStruct((rows, cols),...  4.81 us
    ppermute x1, starting transfers between devices, with_faces(): lax.ppermute(volume[-1:], 'gz', up)  3.9 us
    pallas_call x1, Pallas kernels, project(): pl.pallas_call(project_kernel, out_shape=jax.ShapeDtypeStruct((2 * NX, PA...  3.8 us
    all_to_all x1, starting transfers between devices, exchange(): lax.all_to_all(value, 'xy', split_axis=0, concat_axis=0, axis_index_group...  3.78 us
  transfers between devices with their start and end apart: 3, of which 2 were waited for; matrix products, arithmetic and copies ran while one was open for 1% of the time, Pallas kernels for 0%

profile of v1, /device:TPU:1, one launch (start us, length us, event | category | flops | bytes accessed | tf_op | source)
XLA Modules:
  0.0 141.2 jit_solution(10281893938052842379)
XLA Ops:
  0.6 0.8 copy.12.lists_ref
  1.4 0.0 copy-start
  1.4 1.6 %copy-done = bf16[1,16,256,256]{3,2,1,0:T(8,128)(2,1)S(1)} copy-done((bf16[1,16,256,256]{3,2,1,0:T(8,128)(2,1)S(1)}, bf16[1,16,256,256]{3,2,1,0:T(8,128)(2,1)}, u32[]{:S(2)}) %copy-start) | copy-done | bytes 2097176
  3.0 0.0 copy-start.2
  3.0 1.0 copy-done.2
  4.0 0.0 copy-start.5
  4.0 0.7 copy-done.5
  4.6 0.0 copy-start.7
  4.7 0.7 copy-done.7
  5.3 3.8 %shard_map.77 = f32[8,392,256]{2,1,0:T(8,128)S(1)} custom-call(s32[1]{0:T(128)} %bitcast.me_ref, s32[32,16]{1,0:T(8,128)S(1)} %copy.12.lists_ref, s32[32]{0:T(128)S(1)} %copy-done.5, s32[1,16]{1,0:T(1,128)S(1)} %copy-done.7, f32[96,1024]{1,0:T(8,128)S(1)} %copy-done.2, bf16[1,16,256,256]{3,2,1,0:T(8,128)(2,1)S(1)} %copy-done), custom_call_target="tpu_custom_call" | custom-call | tf_op jit(solution)/shard_map/pallas_call | solution.py:80
  9.1 40.9 %all_to_all.20 = f32[8,392,256]{2,1,0:T(8,128)S(1)} all-to-all(f32[8,392,256]{2,1,0:T(8,128)S(1)} %shard_map.77), channel_id=1, replica_groups={{0,16,32,48,64,80,96,112},{128,144,160,176,192,208,224,240},{256,272,28..., dimensions={0} | all-to-all | bytes 6422528 | tf_op jit(solution)/shard_map/all_to_all | solution.py:28
  50.0 0.0 copy-start.10
  50.0 1.0 reduce_sum.18
  51.0 1.0 slice.38
  52.0 0.7 slice.39
  52.8 20.1 %all_to_all.21 = f32[4,104,256]{2,1,0:T(8,128)S(1)} all-to-all(f32[4,104,256]{2,1,0:T(8,128)S(1)} %select_maximum_fusion), channel_id=1, replica_groups={{0,128,256,384},{16,144,272,400},{32,160,288,416},{48,176,304,432},{64,..., dimensions={0} | all-to-all | bytes 851968 | tf_op jit(solution)/shard_map/all_to_all | solution.py:28
  73.0 0.0 copy-done.10
  73.0 0.0 copy-start.9
  73.0 0.6 copy-done.9
  73.7 15.7 %all_to_all.22 = f32[4,96,256]{2,1,0:T(8,128)S(1)} all-to-all(f32[4,96,256]{2,1,0:T(8,128)S(1)} %broadcast_in_dim.4), channel_id=1, replica_groups={{0,128,256,384},{16,144,272,400},{32,160,288,416},{48,176,304,432},{64,..., dimensions={0} | all-to-all | bytes 786432 | tf_op jit(solution)/shard_map/all_to_all | solution.py:28
  89.4 2.0 %broadcast_in_dim.5 = f32[8,4,96,256]{3,2,1,0:T(8,128)} broadcast(f32[4,96,256]{2,1,0:T(8,128)S(1)} %all_to_all.22), dimensions={1,2,3} | broadcast | bytes 3538944 | tf_op jit(solution)/shard_map/broadcast_in_dim | solution.py:165
  91.4 0.0 copy-start.3
  91.4 3.8 %all-to-all-start.3 = ((f32[8,4,96,256]{3,2,1,0:T(8,128)}), f32[8,4,96,256]{3,2,1,0:T(8,128)S(1)}, u32[]{:S(2)}, u32[]{:S(2)}) async-start(f32[8,4,96,256]{3,2,1,0:T(8,128)} %broadcast_in_dim.5), calls=%async_computation.3 | async-start | bytes 6291456 | tf_op jit(solution)/shard_map/all_to_all | solution.py:28
  95.2 0.0 copy-done.3
  95.2 5.7 %collective-permute-start = (f32[1,1024]{1,0:T(1,128)S(1)}, f32[1,1024]{1,0:T(1,128)S(1)}, u32[]{:S(2)}, u32[]{:S(2)}) collective-permute-start(f32[1,1024]{1,0:T(1,128)S(1)} %get-tuple-element.2), channel_id=1, source_target_pairs={{1,0},{2,1},{3,2},{4,3},{5,4},{6,5},{7,6},{8,7},{9,8},{10,9},{11,1... | collective-permute-start | bytes 12296 | tf_op jit(solution)/shard_map/ppermute | solution.py:141
  100.9 3.9 %collective-permute-start.1 = (f32[1,1024]{1,0:T(1,128)S(1)}, f32[1,1024]{1,0:T(1,128)S(1)}, u32[]{:S(2)}, u32[]{:S(2)}) collective-permute-start(f32[1,1024]{1,0:T(1,128)S(1)} %get-tuple-element.3), channel_id=1, source_target_pairs={{0,1},{1,2},{2,3},{3,4},{4,5},{5,6},{6,7},{7,8},{8,9},{9,10},{10,1... | collective-permute-start | bytes 12296 | tf_op jit(solution)/shard_map/ppermute | solution.py:139
  104.8 0.0 collective-permute-done
  104.8 0.7 collective-permute-done.1
  105.5 0.1 rsqrt_multiply_fusion
  105.6 0.8 fusion.1.base_ref
  106.5 26.0 %all-to-all-done.3.got_ref = f32[8,4,96,256]{3,2,1,0:T(8,128)S(1)} async-done(((f32[8,4,96,256]{3,2,1,0:T(8,128)}), f32[8,4,96,256]{3,2,1,0:T(8,128)S(1)}, u32[]{:S(2)}, u32[]{:S(2)}) %all-to-all-start.3) | async-done | bytes 3145760 | tf_op jit(solution)/shard_map/all_to_all | solution.py:28
  132.5 0.0 copy-start.1
  132.5 1.6 %copy-done.1 = bf16[1,16,256,256]{3,2,1,0:T(8,128)(2,1)S(1)} copy-done((bf16[1,16,256,256]{3,2,1,0:T(8,128)(2,1)S(1)}, bf16[1,16,256,256]{3,2,1,0:T(8,128)(2,1)}, u32[]{:S(2)}) %copy-start.1) | copy-done | bytes 2097176
  134.1 0.0 copy-start.4
  134.1 1.0 copy-done.4
  135.1 0.0 copy-start.6
  135.1 0.7 copy-done.6
  135.7 0.0 copy-start.8
  135.7 0.7 copy-done.8
  136.4 4.8 %shard_map.78 = f32[96,1024]{1,0:T(8,128)} custom-call(s32[1]{0:T(128)} %bitcast.me_ref, s32[32,16]{1,0:T(8,128)S(1)} %copy.12.lists_ref, s32[32]{0:T(128)S(1)} %copy-done.6, s32[1,16]{1,0:T(1,128)S(1)} %copy-done.8, f32[96,1024]{1,0:T(8,128)S(1)} %copy-done.4, bf16[1,16,256,256]{3,2,1,0:T(8,128)(2,1)S(1)} %copy-done.1, ...), custom_call_target="tpu_custom_call" | custom-call | tf_op jit(solution)/shard_map/pallas_call | solution.py:123
  (7 shorter events, 0.1 us)
Async XLA Ops:
  1.4 1.6 %copy-start = (bf16[1,16,256,256]{3,2,1,0:T(8,128)(2,1)S(1)}, bf16[1,16,256,256]{3,2,1,0:T(8,128)(2,1)}, u32[]{:S(2)}) copy-start(bf16[1,16,256,256]{3,2,1,0:T(8,128)(2,1)} %mats_ref.3) | copy-start | bytes 6291460
  3.0 1.0 copy-start.2
  4.0 0.7 copy-start.5
  4.6 0.7 copy-start.7
  50.0 22.9 %copy-start.10 = (f32[96,256]{1,0:T(8,128)S(1)}, f32[96,256]{1,0:T(8,128)}, u32[]{:S(2)}) copy-start(f32[96,256]{1,0:T(8,128)} %param.7) | copy-start | bytes 294916
  73.0 0.6 copy-start.9
  91.4 3.8 %copy-start.3 = (f32[96,1024]{1,0:T(8,128)S(1)}, f32[96,1024]{1,0:T(8,128)}, u32[]{:S(2)}) copy-start(f32[96,1024]{1,0:T(8,128)} %vol_ref.1) | copy-start | bytes 1179652
  91.4 41.1 %all-to-all-start.3 = ((f32[8,4,96,256]{3,2,1,0:T(8,128)}), f32[8,4,96,256]{3,2,1,0:T(8,128)S(1)}, u32[]{:S(2)}, u32[]{:S(2)}) async-start(f32[8,4,96,256]{3,2,1,0:T(8,128)} %broadcast_in_dim.5), calls=%async_computation.3 | async-start | bytes 6291456 | tf_op jit(solution)/shard_map/all_to_all | solution.py:28
  95.2 9.6 %collective-permute-start = (f32[1,1024]{1,0:T(1,128)S(1)}, f32[1,1024]{1,0:T(1,128)S(1)}, u32[]{:S(2)}, u32[]{:S(2)}) collective-permute-start(f32[1,1024]{1,0:T(1,128)S(1)} %get-tuple-element.2), channel_id=1, source_target_pairs={{1,0},{2,1},{3,2},{4,3},{5,4},{6,5},{7,6},{8,7},{9,8},{10,9},{11,1... | collective-permute-start | bytes 12296 | tf_op jit(solution)/shard_map/ppermute | solution.py:141
  100.9 4.6 %collective-permute-start.1 = (f32[1,1024]{1,0:T(1,128)S(1)}, f32[1,1024]{1,0:T(1,128)S(1)}, u32[]{:S(2)}, u32[]{:S(2)}) collective-permute-start(f32[1,1024]{1,0:T(1,128)S(1)} %get-tuple-element.3), channel_id=1, source_target_pairs={{0,1},{1,2},{2,3},{3,4},{4,5},{5,6},{6,7},{7,8},{8,9},{9,10},{10,1... | collective-permute-start | bytes 12296 | tf_op jit(solution)/shard_map/ppermute | solution.py:139
  132.5 1.6 %copy-start.1 = (bf16[1,16,256,256]{3,2,1,0:T(8,128)(2,1)S(1)}, bf16[1,16,256,256]{3,2,1,0:T(8,128)(2,1)}, u32[]{:S(2)}) copy-start(bf16[1,16,256,256]{3,2,1,0:T(8,128)(2,1)} %mats_ref.3) | copy-start | bytes 6291460
  134.1 1.0 copy-start.4
  135.1 0.7 copy-start.6
  135.7 0.7 copy-start.8

commit v2 on v1

v2 whole, which is shorter than its diff:
```python
import functools

import jax
import jax.numpy as jnp
from jax import lax
from jax.experimental import pallas as pl
from jax.experimental.pallas import tpu as pltpu
from jax.sharding import PartitionSpec as P

relax = 1.0
tv_weight = 0.2
smooth_sq = 0.01

NX, NY = 4, 8
PAIRS = NY // 2
NEAR_SIZE = 2 * NX
W = 256
LANES = 128
HALVES = 2
FAR_STEPS = (1, 3, 2)
VMEM_LIMIT = 40 * 1024 * 1024
VMEM_MOST = 60 * 1024 * 1024


def device_of(pair, odd, x):
    return (2 * (pair % PAIRS) + odd) * NX + x


NEAR = [[device_of(p, q, x) for q in range(2) for x in range(NX)] for p in range(PAIRS)]


def near_exchange(value):
    return lax.all_to_all(
        value, "xy", split_axis=0, concat_axis=0, axis_index_groups=NEAR, tiled=True
    )


def far_send(value, step):
    moves = [
        (device_of(p, q, x), device_of(p + step, q, x))
        for p in range(PAIRS)
        for q in range(2)
        for x in range(NX)
    ]
    return lax.ppermute(value, "xy", moves)


def split3(value):
    high = value.astype(jnp.bfloat16)
    rest = value - high.astype(jnp.float32)
    mid = rest.astype(jnp.bfloat16)
    low = (rest - mid.astype(jnp.float32)).astype(jnp.bfloat16)
    return [high, mid, low]


def with_ones(value):
    ones = jnp.ones((16, value.shape[1]), jnp.bfloat16)
    return jnp.concatenate(split3(value) + [ones], axis=0)


def join3(product, rows):
    return product[2 * rows : 3 * rows] + product[rows : 2 * rows] + product[:rows]


def near_far(owner, me, sign):
    y, x = owner // NX, owner % NX
    apart = sign * (y // 2 - me // (2 * NX)) + PAIRS
    return (y % 2) * NX + x, apart % PAIRS


def fetch_all(pairs, sems):
    copies = [pltpu.make_async_copy(src, dst, sems.at[i]) for i, (src, dst) in enumerate(pairs)]
    for copy in copies:
        copy.start()
    return copies


def project_kernel(
    first, rows, sums, me_ref, lists_hbm, owners_hbm, starts_hbm, vol_hbm, mats_hbm, out_ref,
    lists, owners, starts, wide, mats, sems, mat_sems,
):
    count = mats.shape[0]
    cols = vol_hbm.shape[1]
    small = fetch_all(
        [
            (lists_hbm, lists),
            (owners_hbm, owners),
            (starts_hbm, starts),
            (vol_hbm.at[pl.ds(first, rows)], wide.at[:, pl.ds(0, cols)]),
        ],
        sems,
    )
    big = fetch_all([(mats_hbm.at[0, k], mats.at[k]) for k in range(count)], mat_sems)
    out_ref[...] = jnp.zeros(out_ref.shape, jnp.float32)
    wide[:, cols:] = jnp.zeros((rows, LANES), jnp.float32)
    for copy in small:
        copy.wait()
    me = me_ref[0]
    for k in range(count):
        start = starts[0, k]
        near, far = near_far(owners[0, lists[k, me]], me, 1)
        base = pl.multiple_of((start // LANES) * LANES, LANES)
        window = wide[:, pl.ds(base, W + LANES)]
        window = pltpu.roll(window, (W + LANES) - start % LANES, 1)[:, :W]
        left = with_ones(window)
        big[k].wait()
        product = jnp.dot(left, mats[k], preferred_element_type=jnp.float32)
        out_ref[near, pl.ds(pl.multiple_of(far * rows, 8), rows), :] = join3(product, rows)
        if sums:
            out_ref[near, pl.ds(PAIRS * rows + far, 1), :] = product[3 * rows : 3 * rows + 1]


HBM = pl.BlockSpec(memory_space=pl.ANY)
SMEM = pl.BlockSpec(memory_space=pltpu.SMEM)
VMEM = pl.BlockSpec(memory_space=pltpu.VMEM)


def small_scratch(lists, owners, starts):
    return [pltpu.SMEM(a.shape, jnp.int32) for a in (lists, owners, starts)]


def project(first, rows, sums, me, lists, owners, starts, volume, mats):
    cols = volume.shape[1]
    count = mats.shape[1]
    out_rows = PAIRS * rows + (8 if sums else 0)
    return pl.pallas_call(
        functools.partial(project_kernel, first, rows, sums),
        out_shape=jax.ShapeDtypeStruct((NEAR_SIZE, out_rows, W), jnp.float32),
        in_specs=[SMEM] + [HBM] * 5,
        out_specs=VMEM,
        scratch_shapes=small_scratch(lists, owners, starts)
        + [
            pltpu.VMEM((rows, cols + LANES), jnp.float32),
            pltpu.VMEM(mats.shape[1:], jnp.bfloat16),
            pltpu.SemaphoreType.DMA((4,)),
            pltpu.SemaphoreType.DMA((count,)),
        ],
        compiler_params=pltpu.CompilerParams(vmem_limit_bytes=VMEM_MOST if sums else VMEM_LIMIT),
        cost_estimate=pl.CostEstimate(
            flops=2 * 3 * count * rows * W * W, bytes_accessed=6 << 20, transcendentals=0
        ),
    )(me, lists, owners, starts, volume, mats)


def gather_kernel(rows, sums, in_ref, *outs):
    outs = outs[-PAIRS:]
    total = in_ref[0]
    for i in range(1, NEAR_SIZE):
        total = total + in_ref[i]
    for far in range(PAIRS):
        outs[far][:rows] = total[far * rows : (far + 1) * rows]
        if sums:
            outs[far][rows:] = jnp.broadcast_to(
                total[PAIRS * rows + far : PAIRS * rows + far + 1], (8, W)
            )


def gather_near(rows, sums, arrived, after):
    out = jax.ShapeDtypeStruct((rows + (8 if sums else 0), W), jnp.float32)
    return pl.pallas_call(
        functools.partial(gather_kernel, rows, sums),
        out_shape=[out] * PAIRS,
        in_specs=[VMEM] + [HBM] * len(after),
        out_specs=[VMEM] * PAIRS,
        compiler_params=pltpu.CompilerParams(vmem_limit_bytes=VMEM_LIMIT),
    )(arrived, *after)


def spread_kernel(*refs):
    parts = refs[:PAIRS]
    out_hbm, token_ref, column, sems = refs[PAIRS:]
    for far in range(PAIRS):
        column[far] = parts[far][...]
    copies = fetch_all([(column, out_hbm.at[i]) for i in range(NEAR_SIZE)], sems)
    token_ref[...] = column[0, :8, :LANES]
    for copy in copies:
        copy.wait()


def spread_near(parts):
    rows = parts[0].shape[0]
    return pl.pallas_call(
        spread_kernel,
        out_shape=[
            jax.ShapeDtypeStruct((NEAR_SIZE, PAIRS, rows, W), jnp.float32),
            jax.ShapeDtypeStruct((8, LANES), jnp.float32),
        ],
        in_specs=[VMEM] * PAIRS,
        out_specs=[HBM, VMEM],
        scratch_shapes=[
            pltpu.VMEM((PAIRS, rows, W), jnp.float32),
            pltpu.SemaphoreType.DMA((NEAR_SIZE,)),
        ],
        compiler_params=pltpu.CompilerParams(vmem_limit_bytes=VMEM_LIMIT),
    )(*parts)


def back_kernel(
    first, rows, has_old, me_ref, lists_hbm, owners_hbm, starts_hbm, base_hbm, mats_hbm, got_ref, *rest
):
    if has_old:
        rest = rest[1:]
    out_hbm, lists, owners, starts, base_v, mats, total, result, sems, mat_sems, out_sem = rest
    count = mats.shape[0]
    cols = base_hbm.shape[1]
    small = fetch_all(
        [
            (lists_hbm, lists),
            (owners_hbm, owners),
            (starts_hbm, starts),
            (base_hbm.at[pl.ds(first, rows)], base_v),
        ],
        sems,
    )
    big = fetch_all([(mats_hbm.at[0, k], mats.at[k]) for k in range(count)], mat_sems)
    total[...] = jnp.zeros(total.shape, jnp.float32)
    for copy in small:
        copy.wait()
    me = me_ref[0]
    for k in range(count):
        start = starts[0, k]
        near, far = near_far(owners[0, lists[k, me]], me, -1)
        base = pl.multiple_of((start // LANES) * LANES, LANES)
        left = with_ones(got_ref[near, far])
        big[k].wait()
        product = lax.dot_general(
            left, mats[k], (((1,), (1,)), ((), ())), preferred_element_type=jnp.float32
        )
        value = jnp.concatenate([join3(product, rows), product[3 * rows : 3 * rows + 8]], axis=0)
        value = jnp.concatenate([value, jnp.zeros((rows + 8, LANES), jnp.float32)], axis=1)
        total[:, pl.ds(base, W + LANES)] += pltpu.roll(value, start % LANES, 1)
    column = jnp.maximum(total[rows : rows + 1, :cols], 1.0)
    result[...] = base_v[...] + relax * (total[:rows, :cols] / column)
    out = pltpu.make_async_copy(result, out_hbm.at[pl.ds(first, rows)], out_sem.at[0])
    out.start()
    out.wait()


def back_project(first, rows, old, me, lists, owners, starts, base, mats, got):
    cols = base.shape[1]
    count = mats.shape[1]
    more = [] if old is None else [old]
    return pl.pallas_call(
        functools.partial(back_kernel, first, rows, bool(more)),
        out_shape=jax.ShapeDtypeStruct(base.shape, jnp.float32),
        in_specs=[SMEM] + [HBM] * 5 + [VMEM] + [HBM] * len(more),
        out_specs=HBM,
        scratch_shapes=small_scratch(lists, owners, starts)
        + [
            pltpu.VMEM((rows, cols), jnp.float32),
            pltpu.VMEM(mats.shape[1:], jnp.bfloat16),
            pltpu.VMEM((rows + 8, cols + LANES), jnp.float32),
            pltpu.VMEM((rows, cols), jnp.float32),
            pltpu.SemaphoreType.DMA((4,)),
            pltpu.SemaphoreType.DMA((count,)),
            pltpu.SemaphoreType.DMA((1,)),
        ],
        input_output_aliases={7: 0} if more else {},
        compiler_params=pltpu.CompilerParams(vmem_limit_bytes=VMEM_LIMIT),
        cost_estimate=pl.CostEstimate(
            flops=2 * 3 * count * rows * W * W, bytes_accessed=6 << 20, transcendentals=0
        ),
    )(me, lists, owners, starts, base, mats, got, *more)


def with_faces(volume):
    count = lax.axis_size("gz")
    up = [(i, i + 1) for i in range(count - 1)]
    down = [(i + 1, i) for i in range(count - 1)]
    return jnp.concatenate(
        [
            lax.ppermute(volume[-1:], "gz", up),
            volume,
            lax.ppermute(volume[:1], "gz", down),
        ],
        axis=0,
    )


def total_variation(padded):
    diffs = padded[1:] - padded[:-1]
    slopes = diffs / jnp.sqrt(diffs * diffs + smooth_sq)
    return slopes[:-1] - slopes[1:]


def per_device(volume, sinogram, ray_mats, offsets, ray_lists, owner_map):
    rows = volume.shape[0] // HALVES
    me = lax.axis_index("xy").astype(jnp.int32).reshape(1)
    common = (me, ray_lists.T, owner_map.reshape(1, -1), offsets)
    arrived = [
        near_exchange(project(h * rows, rows, h == 0, *common, volume, ray_mats))
        for h in range(HALVES)
    ]
    rowsum = None
    weighted = []
    got = []
    spreads = []
    for h in range(HALVES):
        parts = gather_near(rows, h == 0, arrived[h], spreads)
        total = parts[0] + sum(far_send(parts[step], step) for step in FAR_STEPS)
        if h == 0:
            rowsum = total[rows : rows + 1]
        mine = (sinogram[h * rows : (h + 1) * rows] - total[:rows]) / rowsum
        weighted.append(mine)
        far = {0: mine, **{step: far_send(mine, step) for step in FAR_STEPS}}
        spread, token = spread_near([far[i] for i in range(PAIRS)])
        spreads.append(token)
        got.append(near_exchange(spread))
    base = volume - tv_weight * total_variation(with_faces(volume))
    new_volume = None
    for h in range(HALVES):
        new_volume = back_project(h * rows, rows, new_volume, *common, base, ray_mats, got[h])
    return (new_volume, jnp.concatenate(weighted, axis=0))


def solution(mesh):
    in_specs = (P("gz", "xy"), P("gz", "xy"), P("xy", None, None, None), P("xy", None), P(), P())
    out_specs = (P("gz", "xy"), P("gz", "xy"))
    return jax.shard_map(
        per_device, mesh=mesh, in_specs=in_specs, out_specs=out_specs, check_vma=False
    )
```

time: 142 us -> 168 us (1.18)
  blocking collectives: 76.8 us -> 0 us
  starting transfers between devices: 13.3 us -> 87.3 us
  Pallas kernels: 8.61 us -> 40.6 us
  local copies, waits for them, and re-layouts: 13 us -> 3.53 us
  waiting for transfers between devices: 26.7 us -> 32.6 us
    all_to_all x3 -> x0, blocking collectives: 76.8 us -> none  [exchange(): lax.all_to_all(value, 'xy', split_axis=0, concat_axis=0, axis_index_group...]
    ppermute x0 -> x12, starting transfers between devices: none -> 50 us  [far_send(): return lax.ppermute(value, 'xy', moves)]
    pallas_call x2 -> x8, Pallas kernels: 8.61 us -> 40.6 us  [the longest x2 20.3 us: back_project(): pl.pallas_call(functools.partial(back_kernel, first, rows, bool(more)), o...]
    ppermute x0 -> x12, waiting for transfers between devices: none -> 22.9 us  [far_send(): return lax.ppermute(value, 'xy', moves)]
    all_to_all x1 -> x4, starting transfers between devices: 3.78 us -> 22.5 us  [near_exchange(): lax.all_to_all(value, 'xy', split_axis=0, concat_axis=0, axis_index_group...]
    all_to_all x1 -> x4, waiting for transfers between devices: 26 us -> 8.9 us  [near_exchange(): lax.all_to_all(value, 'xy', split_axis=0, concat_axis=0, axis_index_group...]
    unnamed x23 -> x18, local copies, waits for them, and re-layouts: 9.21 us -> 3.52 us
    ppermute x1, starting transfers between devices: 5.66 us -> 9.68 us  [with_faces(): lax.ppermute(volume[:1], 'gz', down)]
  transfers between devices with their start and end apart: 3 -> 18, of which waited for: 2 -> 9; matrix products, arithmetic and copies ran while one was open for 1% -> 1% of each run, Pallas kernels for 0% -> 15%
where the time goes in v2:
time: 168 us; the launch traced here: 166 us
  starting transfers between devices  87.3 us (52%)
  Pallas kernels  40.6 us (24%)
  waiting for transfers between devices  32.6 us (19%)
  local copies, waits for them, and re-layouts  3.53 us (2%)
    ppermute x12, starting transfers between devices, far_send(): return lax.ppermute(value, 'xy', moves)  50 us
    ppermute x12, waiting for transfers between devices, far_send(): return lax.ppermute(value, 'xy', moves)  22.9 us
    all_to_all x4, starting transfers between devices, near_exchange(): lax.all_to_all(value, 'xy', split_axis=0, concat_axis=0, axis_index_group...  22.5 us
    pallas_call x2, Pallas kernels, back_project(): pl.pallas_call(functools.partial(back_kernel, first, rows, bool(more)), o...  20.3 us
    pallas_call x2, Pallas kernels, project(): pl.pallas_call(functools.partial(project_kernel, first, rows, sums), out_...  12.4 us
    ppermute x1, starting transfers between devices, with_faces(): lax.ppermute(volume[:1], 'gz', down)  9.68 us
    all_to_all x4, waiting for transfers between devices, near_exchange(): lax.all_to_all(value, 'xy', split_axis=0, concat_axis=0, axis_index_group...  8.9 us
    ppermute x1, starting transfers between devices, with_faces(): lax.ppermute(volume[-1:], 'gz', up)  5.07 us
  transfers between devices with their start and end apart: 18, of which 9 were waited for; matrix products, arithmetic and copies ran while one was open for 1% of the time, Pallas kernels for 15%

profile of v2, /device:TPU:1, one launch (start us, length us, event | category | flops | bytes accessed | tf_op | source)
XLA Modules:
  0.0 165.8 jit_solution(10900480568825084021)
XLA Ops:
  0.6 6.1 %shard_map.78 = f32[8,200,256]{2,1,0:T(8,128)} custom-call(s32[1]{0:T(128)} %bitcast.me_ref, s32[16,32]{1,0:T(8,128)} %bitcast.4, s32[1,32]{1,0:T(1,128)} %bitcast.8, s32[1,16]{1,0:T(1,128)} %starts_hbm.7, f32[96,1024]{1,0:T(8,128)} %vol_hbm.3, bf16[1,16,256,256]{3,2,1,0:T(8,128)(2,1)} %mats_hbm.7), custom_call_target="tpu_custom_call" | custom-call | flops 301989888 | bytes 6291456 | tf_op jit(solution)/shard_map/pallas_call | solution.py:126
  6.8 0.0 copy-start
  6.8 0.0 copy-start.1
  6.8 0.0 copy-start.5
  6.8 0.0 copy-start.6
  6.8 0.0 copy-start.7
  6.8 6.0 %all-to-all-start.1 = ((f32[8,200,256]{2,1,0:T(8,128)}), f32[8,200,256]{2,1,0:T(8,128)}, u32[]{:S(2)}, u32[]{:S(2)}) async-start(f32[8,200,256]{2,1,0:T(8,128)} %shard_map.78), calls=%async_computation.1 | async-start | bytes 3276800 | tf_op jit(solution)/shard_map/all_to_all | solution.py:33
  12.8 0.0 copy-done
  12.8 0.0 copy-done.1
  12.9 0.0 copy-done.5
  12.9 0.0 copy-done.6
  12.9 0.0 copy-done.7
  12.9 6.2 %shard_map.77 = f32[8,192,256]{2,1,0:T(8,128)S(1)} custom-call(s32[1]{0:T(128)} %bitcast.me_ref, s32[16,32]{1,0:T(8,128)S(1)} %bitcast.5, s32[1,32]{1,0:T(1,128)S(1)} %bitcast.9, s32[1,16]{1,0:T(1,128)S(1)} %copy-done.7, f32[96,1024]{1,0:T(8,128)S(1)} %copy-done.1, bf16[1,16,256,256]{3,2,1,0:T(8,128)(2,1)S(1)} %copy-done), custom_call_target="tpu_custom_call" | custom-call | flops 301989888 | bytes 6291456 | tf_op jit(solution)/shard_map/pallas_call | solution.py:126
  19.1 0.0 copy-start.2
  19.1 1.1 copy-done.2
  20.3 8.9 %all-to-all-done.1.in_ref = f32[8,200,256]{2,1,0:T(8,128)} async-done(((f32[8,200,256]{2,1,0:T(8,128)}), f32[8,200,256]{2,1,0:T(8,128)}, u32[]{:S(2)}, u32[]{:S(2)}) %all-to-all-start.1) | async-done | bytes 1638432 | tf_op jit(solution)/shard_map/all_to_all | solution.py:33
  29.1 7.9 %all-to-all-start = ((f32[8,192,256]{2,1,0:T(8,128)}), f32[8,192,256]{2,1,0:T(8,128)}, u32[]{:S(2)}, u32[]{:S(2)}) async-start(f32[8,192,256]{2,1,0:T(8,128)} %copy-done.2), calls=%async_computation | async-start | bytes 3145728 | tf_op jit(solution)/shard_map/all_to_all | solution.py:33
  37.1 1.5 shard_map.79
  38.6 5.7 %collective-permute-start.2 = (f32[56,256]{1,0:T(8,128)S(1)}, f32[56,256]{1,0:T(8,128)S(1)}, u32[]{:S(2)}, u32[]{:S(2)}) collective-permute-start(f32[56,256]{1,0:T(8,128)S(1)} %get-tuple-element.14), channel_id=1, source_target_pairs={{0,128},{16,144},{32,160},{48,176},{64,192},{80,208},{96,224},{112... | collective-permute-start | bytes 172040 | tf_op jit(solution)/shard_map/ppermute | solution.py:45
  44.3 2.8 %collective-permute-start.3 = (f32[56,256]{1,0:T(8,128)S(1)}, f32[56,256]{1,0:T(8,128)S(1)}, u32[]{:S(2)}, u32[]{:S(2)}) collective-permute-start(f32[56,256]{1,0:T(8,128)S(1)} %get-tuple-element.15), channel_id=1, source_target_pairs={{0,384},{16,400},{32,416},{48,432},{64,448},{80,464},{96,480},{112... | collective-permute-start | bytes 172040 | tf_op jit(solution)/shard_map/ppermute | solution.py:45
  47.0 7.0 %collective-permute-start.4 = (f32[56,256]{1,0:T(8,128)S(1)}, f32[56,256]{1,0:T(8,128)S(1)}, u32[]{:S(2)}, u32[]{:S(2)}) collective-permute-start(f32[56,256]{1,0:T(8,128)S(1)} %get-tuple-element.16), channel_id=1, source_target_pairs={{0,256},{16,272},{32,288},{48,304},{64,320},{80,336},{96,352},{112... | collective-permute-start | bytes 172040 | tf_op jit(solution)/shard_map/ppermute | solution.py:45
  54.1 7.0 %collective-permute-done.2 = f32[56,256]{1,0:T(8,128)S(1)} collective-permute-done((f32[56,256]{1,0:T(8,128)S(1)}, f32[56,256]{1,0:T(8,128)S(1)}, u32[]{:S(2)}, u32[]{:S(2)}) %collective-permute-start.2) | collective-permute-done | bytes 57376 | tf_op jit(solution)/shard_map/ppermute | solution.py:45
  61.1 0.0 collective-permute-done.3
  61.1 2.8 %collective-permute-done.4 = f32[56,256]{1,0:T(8,128)S(1)} collective-permute-done((f32[56,256]{1,0:T(8,128)S(1)}, f32[56,256]{1,0:T(8,128)S(1)}, u32[]{:S(2)}, u32[]{:S(2)}) %collective-permute-start.4) | collective-permute-done | bytes 57376 | tf_op jit(solution)/shard_map/ppermute | solution.py:45
  64.0 0.0 copy-done.8
  64.0 2.4 %collective-permute-start.5 = (f32[48,256]{1,0:T(8,128)S(1)}, f32[48,256]{1,0:T(8,128)S(1)}, u32[]{:S(2)}, u32[]{:S(2)}) collective-permute-start(f32[48,256]{1,0:T(8,128)S(1)} %fusion.2.refs_0_), channel_id=1, source_target_pairs={{0,128},{16,144},{32,160},{48,176},{64,192},{80,208},{96,224},{112... | collective-permute-start | bytes 147464 | tf_op jit(solution)/shard_map/ppermute | solution.py:45
  66.4 5.6 %collective-permute-start.6 = (f32[48,256]{1,0:T(8,128)S(1)}, f32[48,256]{1,0:T(8,128)S(1)}, u32[]{:S(2)}, u32[]{:S(2)}) collective-permute-start(f32[48,256]{1,0:T(8,128)S(1)} %fusion.2.refs_0_), channel_id=1, source_target_pairs={{0,256},{16,272},{32,288},{48,304},{64,320},{80,336},{96,352},{112... | collective-permute-start | bytes 147464 | tf_op jit(solution)/shard_map/ppermute | solution.py:45
  72.0 2.2 %collective-permute-start.7 = (f32[48,256]{1,0:T(8,128)S(1)}, f32[48,256]{1,0:T(8,128)S(1)}, u32[]{:S(2)}, u32[]{:S(2)}) collective-permute-start(f32[48,256]{1,0:T(8,128)S(1)} %fusion.2.refs_0_), channel_id=1, source_target_pairs={{0,384},{16,400},{32,416},{48,432},{64,448},{80,464},{96,480},{112... | collective-permute-start | bytes 147464 | tf_op jit(solution)/shard_map/ppermute | solution.py:45
  74.2 0.0 collective-permute-done.5.refs_1_
  74.2 1.2 collective-permute-done.6.refs_2_
  75.3 3.2 %collective-permute-done.7.refs_3_ = f32[48,256]{1,0:T(8,128)S(1)} collective-permute-done((f32[48,256]{1,0:T(8,128)S(1)}, f32[48,256]{1,0:T(8,128)S(1)}, u32[]{:S(2)}, u32[]{:S(2)}) %collective-permute-start.7) | collective-permute-done | bytes 49184 | tf_op jit(solution)/shard_map/ppermute | solution.py:45
  78.5 2.1 %shard_map.80 = (f32[8,4,48,256]{3,2,1,0:T(8,128)S(1)}, f32[8,128]{1,0:T(8,128)S(1)}) custom-call(f32[48,256]{1,0:T(8,128)S(1)} %fusion.2.refs_0_, f32[48,256]{1,0:T(8,128)S(1)} %collective-permute-done.5.refs_1_, f32[48,256]{1,0:T(8,128)S(1)} %collective-permute-done.6.refs_2_, f32[48,256]{1,0:T(8,128)S(1)} %collective-permute-done.7.refs_3_), custom_call_target="tpu_custom_call" | custom-call | tf_op jit(solution)/shard_map/pallas_call | solution.py:182
  80.7 0.0 copy-start.3
  80.7 1.2 copy-done.3
  81.9 0.0 all-to-all-done.in_ref
  81.9 4.3 %all-to-all-start.3 = ((f32[8,4,48,256]{3,2,1,0:T(8,128)}), f32[8,4,48,256]{3,2,1,0:T(8,128)}, u32[]{:S(2)}, u32[]{:S(2)}) async-start(f32[8,4,48,256]{3,2,1,0:T(8,128)} %copy-done.3), calls=%async_computation.3 | async-start | bytes 3145728 | tf_op jit(solution)/shard_map/all_to_all | solution.py:33
  86.2 1.5 shard_map.81
  87.6 5.6 %collective-permute-start.10 = (f32[48,256]{1,0:T(8,128)S(1)}, f32[48,256]{1,0:T(8,128)S(1)}, u32[]{:S(2)}, u32[]{:S(2)}) collective-permute-start(f32[48,256]{1,0:T(8,128)S(1)} %get-tuple-element.21), channel_id=1, source_target_pairs={{0,256},{16,272},{32,288},{48,304},{64,320},{80,336},{96,352},{112... | collective-permute-start | bytes 147464 | tf_op jit(solution)/shard_map/ppermute | solution.py:45
  93.3 2.8 %collective-permute-start.8 = (f32[48,256]{1,0:T(8,128)S(1)}, f32[48,256]{1,0:T(8,128)S(1)}, u32[]{:S(2)}, u32[]{:S(2)}) collective-permute-start(f32[48,256]{1,0:T(8,128)S(1)} %get-tuple-element.19), channel_id=1, source_target_pairs={{0,128},{16,144},{32,160},{48,176},{64,192},{80,208},{96,224},{112... | collective-permute-start | bytes 147464 | tf_op jit(solution)/shard_map/ppermute | solution.py:45
  96.1 4.6 %collective-permute-start.9 = (f32[48,256]{1,0:T(8,128)S(1)}, f32[48,256]{1,0:T(8,128)S(1)}, u32[]{:S(2)}, u32[]{:S(2)}) collective-permute-start(f32[48,256]{1,0:T(8,128)S(1)} %get-tuple-element.20), channel_id=1, source_target_pairs={{0,384},{16,400},{32,416},{48,432},{64,448},{80,464},{96,480},{112... | collective-permute-start | bytes 147464 | tf_op jit(solution)/shard_map/ppermute | solution.py:45
  100.7 6.0 %collective-permute-done.10 = f32[48,256]{1,0:T(8,128)S(1)} collective-permute-done((f32[48,256]{1,0:T(8,128)S(1)}, f32[48,256]{1,0:T(8,128)S(1)}, u32[]{:S(2)}, u32[]{:S(2)}) %collective-permute-start.10) | collective-permute-done | bytes 49184 | tf_op jit(solution)/shard_map/ppermute | solution.py:45
  106.7 0.8 collective-permute-done.8
  107.5 0.0 collective-permute-done.9
  107.5 1.9 %collective-permute-start.11 = (f32[48,256]{1,0:T(8,128)S(1)}, f32[48,256]{1,0:T(8,128)S(1)}, u32[]{:S(2)}, u32[]{:S(2)}) collective-permute-start(f32[48,256]{1,0:T(8,128)S(1)} %subtract_divide_fusion.refs_0_), channel_id=1, source_target_pairs={{0,128},{16,144},{32,160},{48,176},{64,192},{80,208},{96,224},{112... | collective-permute-start | bytes 147464 | tf_op jit(solution)/shard_map/ppermute | solution.py:45
  109.4 5.3 %collective-permute-start.12 = (f32[48,256]{1,0:T(8,128)S(1)}, f32[48,256]{1,0:T(8,128)S(1)}, u32[]{:S(2)}, u32[]{:S(2)}) collective-permute-start(f32[48,256]{1,0:T(8,128)S(1)} %subtract_divide_fusion.refs_0_), channel_id=1, source_target_pairs={{0,256},{16,272},{32,288},{48,304},{64,320},{80,336},{96,352},{112... | collective-permute-start | bytes 147464 | tf_op jit(solution)/shard_map/ppermute | solution.py:45
  114.7 4.2 %collective-permute-start.13 = (f32[48,256]{1,0:T(8,128)S(1)}, f32[48,256]{1,0:T(8,128)S(1)}, u32[]{:S(2)}, u32[]{:S(2)}) collective-permute-start(f32[48,256]{1,0:T(8,128)S(1)} %subtract_divide_fusion.refs_0_), channel_id=1, source_target_pairs={{0,384},{16,400},{32,416},{48,432},{64,448},{80,464},{96,480},{112... | collective-permute-start | bytes 147464 | tf_op jit(solution)/shard_map/ppermute | solution.py:45
  118.9 0.0 collective-permute-done.11.refs_1_
  118.9 0.0 collective-permute-done.12.refs_2_
  118.9 2.0 %collective-permute-done.13.refs_3_ = f32[48,256]{1,0:T(8,128)S(1)} collective-permute-done((f32[48,256]{1,0:T(8,128)S(1)}, f32[48,256]{1,0:T(8,128)S(1)}, u32[]{:S(2)}, u32[]{:S(2)}) %collective-permute-start.13) | collective-permute-done | bytes 49184 | tf_op jit(solution)/shard_map/ppermute | solution.py:45
  120.9 2.7 %shard_map.82 = (f32[8,4,48,256]{3,2,1,0:T(8,128)S(1)}, f32[8,128]{1,0:T(8,128)}) custom-call(f32[48,256]{1,0:T(8,128)S(1)} %subtract_divide_fusion.refs_0_, f32[48,256]{1,0:T(8,128)S(1)} %collective-permute-done.11.refs_1_, f32[48,256]{1,0:T(8,128)S(1)} %collective-permute-done.12.refs_2_, f32[48,256]{1,0:T(8,128)S(1)} %collective-permute-done.13.refs_3_), custom_call_target="tpu_custom_call" | custom-call | tf_op jit(solution)/shard_map/pallas_call | solution.py:182
  123.6 0.0 copy-start.4
  123.6 1.1 copy-done.4
  124.8 0.0 all-to-all-done.3.got_ref
  124.8 4.3 %all-to-all-start.2 = ((f32[8,4,48,256]{3,2,1,0:T(8,128)}), f32[8,4,48,256]{3,2,1,0:T(8,128)}, u32[]{:S(2)}, u32[]{:S(2)}) async-start(f32[8,4,48,256]{3,2,1,0:T(8,128)} %copy-done.4), calls=%async_computation.2 | async-start | bytes 3145728 | tf_op jit(solution)/shard_map/all_to_all | solution.py:33
  129.1 9.7 %collective-permute-start = (f32[1,1024]{1,0:T(1,128)S(1)}, f32[1,1024]{1,0:T(1,128)S(1)}, u32[]{:S(2)}, u32[]{:S(2)}) collective-permute-start(f32[1,1024]{1,0:T(1,128)S(1)} %get-tuple-element.24), channel_id=1, source_target_pairs={{1,0},{2,1},{3,2},{4,3},{5,4},{6,5},{7,6},{8,7},{9,8},{10,9},{11,1... | collective-permute-start | bytes 12296 | tf_op jit(solution)/shard_map/ppermute | solution.py:274
  138.8 5.1 %collective-permute-start.1 = (f32[1,1024]{1,0:T(1,128)S(1)}, f32[1,1024]{1,0:T(1,128)S(1)}, u32[]{:S(2)}, u32[]{:S(2)}) collective-permute-start(f32[1,1024]{1,0:T(1,128)S(1)} %get-tuple-element.25), channel_id=1, source_target_pairs={{0,1},{1,2},{2,3},{3,4},{4,5},{5,6},{6,7},{7,8},{8,9},{9,10},{10,1... | collective-permute-start | bytes 12296 | tf_op jit(solution)/shard_map/ppermute | solution.py:272
  143.9 0.0 collective-permute-done
  143.9 0.7 collective-permute-done.1
  144.6 0.1 rsqrt_multiply_fusion
  144.7 0.1 fusion.1.base_hbm
  144.8 0.6 pad_maximum_fusion
  145.4 10.2 %shard_map.83.rest_0_ = f32[96,1024]{1,0:T(8,128)} custom-call(s32[1]{0:T(128)} %bitcast.me_ref, s32[16,32]{1,0:T(8,128)S(1)} %bitcast.6, s32[1,32]{1,0:T(1,128)S(1)} %bitcast.10, s32[1,16]{1,0:T(1,128)S(1)} %copy-done.7, f32[96,1024]{1,0:T(8,128)S(1)} %fusion.1.base_hbm, bf16[1,16,256,256]{3,2,1,0:T(8,128)(2,1)S(1)} %copy-done, ...), custom_call_target="tpu_custom_call" | custom-call | flops 301989888 | bytes 6291456 | tf_op jit(solution)/shard_map/pallas_call | solution.py:243
  155.6 0.0 all-to-all-done.2.got_ref
  155.6 10.2 %shard_map.84 = f32[96,1024]{1,0:T(8,128)} custom-call(s32[1]{0:T(128)} %bitcast.me_ref, s32[16,32]{1,0:T(8,128)S(1)} %bitcast.7, s32[1,32]{1,0:T(1,128)S(1)} %bitcast.11, s32[1,16]{1,0:T(1,128)S(1)} %copy-done.7, f32[96,1024]{1,0:T(8,128)S(1)} %fusion.1.base_hbm, bf16[1,16,256,256]{3,2,1,0:T(8,128)(2,1)S(1)} %copy-done, ...), custom_call_target="tpu_custom_call", output_to_operand_aliasing={{}: (7, {})} | custom-call | flops 301989888 | bytes 6291456 | tf_op jit(solution)/shard_map/pallas_call | solution.py:243
  (6 shorter events, 0.1 us)
Async XLA Ops:
  6.8 6.1 %copy-start = (bf16[1,16,256,256]{3,2,1,0:T(8,128)(2,1)S(1)}, bf16[1,16,256,256]{3,2,1,0:T(8,128)(2,1)}, u32[]{:S(2)}) copy-start(bf16[1,16,256,256]{3,2,1,0:T(8,128)(2,1)} %mats_hbm.7) | copy-start | bytes 6291460
  6.8 6.1 %copy-start.1 = (f32[96,1024]{1,0:T(8,128)S(1)}, f32[96,1024]{1,0:T(8,128)}, u32[]{:S(2)}) copy-start(f32[96,1024]{1,0:T(8,128)} %vol_hbm.3) | copy-start | bytes 1179652
  6.8 6.1 %copy-start.5 = (s32[32,16]{0,1:T(8,128)S(1)}, s32[32,16]{0,1:T(8,128)}, u32[]{:S(2)}) copy-start(s32[32,16]{0,1:T(8,128)} %param.10) | copy-start | bytes 6148
  6.8 6.1 %copy-start.6 = (s32[32]{0:T(128)S(1)}, s32[32]{0:T(128)}, u32[]{:S(2)}) copy-start(s32[32]{0:T(128)} %param.11) | copy-start | bytes 388
  6.8 6.1 %copy-start.7 = (s32[1,16]{1,0:T(1,128)S(1)}, s32[1,16]{1,0:T(1,128)}, u32[]{:S(2)}) copy-start(s32[1,16]{1,0:T(1,128)} %starts_hbm.7) | copy-start | bytes 196
  6.8 22.3 %all-to-all-start.1 = ((f32[8,200,256]{2,1,0:T(8,128)}), f32[8,200,256]{2,1,0:T(8,128)}, u32[]{:S(2)}, u32[]{:S(2)}) async-start(f32[8,200,256]{2,1,0:T(8,128)} %shard_map.78), calls=%async_computation.1 | async-start | bytes 3276800 | tf_op jit(solution)/shard_map/all_to_all | solution.py:33
  19.1 1.1 copy-start.2
  29.1 52.7 %all-to-all-start = ((f32[8,192,256]{2,1,0:T(8,128)}), f32[8,192,256]{2,1,0:T(8,128)}, u32[]{:S(2)}, u32[]{:S(2)}) async-start(f32[8,192,256]{2,1,0:T(8,128)} %copy-done.2), calls=%async_computation | async-start | bytes 3145728 | tf_op jit(solution)/shard_map/all_to_all | solution.py:33
  37.1 26.9 %copy-start.8 = (f32[96,256]{1,0:T(8,128)S(1)}, f32[96,256]{1,0:T(8,128)}, u32[]{:S(2)}) copy-start(f32[96,256]{1,0:T(8,128)} %param.7) | copy-start | bytes 294916
  38.6 22.5 %collective-permute-start.2 = (f32[56,256]{1,0:T(8,128)S(1)}, f32[56,256]{1,0:T(8,128)S(1)}, u32[]{:S(2)}, u32[]{:S(2)}) collective-permute-start(f32[56,256]{1,0:T(8,128)S(1)} %get-tuple-element.14), channel_id=1, source_target_pairs={{0,128},{16,144},{32,160},{48,176},{64,192},{80,208},{96,224},{112... | collective-permute-start | bytes 172040 | tf_op jit(solution)/shard_map/ppermute | solution.py:45
  44.3 16.8 %collective-permute-start.3 = (f32[56,256]{1,0:T(8,128)S(1)}, f32[56,256]{1,0:T(8,128)S(1)}, u32[]{:S(2)}, u32[]{:S(2)}) collective-permute-start(f32[56,256]{1,0:T(8,128)S(1)} %get-tuple-element.15), channel_id=1, source_target_pairs={{0,384},{16,400},{32,416},{48,432},{64,448},{80,464},{96,480},{112... | collective-permute-start | bytes 172040 | tf_op jit(solution)/shard_map/ppermute | solution.py:45
  47.0 16.9 %collective-permute-start.4 = (f32[56,256]{1,0:T(8,128)S(1)}, f32[56,256]{1,0:T(8,128)S(1)}, u32[]{:S(2)}, u32[]{:S(2)}) collective-permute-start(f32[56,256]{1,0:T(8,128)S(1)} %get-tuple-element.16), channel_id=1, source_target_pairs={{0,256},{16,272},{32,288},{48,304},{64,320},{80,336},{96,352},{112... | collective-permute-start | bytes 172040 | tf_op jit(solution)/shard_map/ppermute | solution.py:45
  64.0 10.2 %collective-permute-start.5 = (f32[48,256]{1,0:T(8,128)S(1)}, f32[48,256]{1,0:T(8,128)S(1)}, u32[]{:S(2)}, u32[]{:S(2)}) collective-permute-start(f32[48,256]{1,0:T(8,128)S(1)} %fusion.2.refs_0_), channel_id=1, source_target_pairs={{0,128},{16,144},{32,160},{48,176},{64,192},{80,208},{96,224},{112... | collective-permute-start | bytes 147464 | tf_op jit(solution)/shard_map/ppermute | solution.py:45
  66.4 9.0 %collective-permute-start.6 = (f32[48,256]{1,0:T(8,128)S(1)}, f32[48,256]{1,0:T(8,128)S(1)}, u32[]{:S(2)}, u32[]{:S(2)}) collective-permute-start(f32[48,256]{1,0:T(8,128)S(1)} %fusion.2.refs_0_), channel_id=1, source_target_pairs={{0,256},{16,272},{32,288},{48,304},{64,320},{80,336},{96,352},{112... | collective-permute-start | bytes 147464 | tf_op jit(solution)/shard_map/ppermute | solution.py:45
  72.0 6.6 %collective-permute-start.7 = (f32[48,256]{1,0:T(8,128)S(1)}, f32[48,256]{1,0:T(8,128)S(1)}, u32[]{:S(2)}, u32[]{:S(2)}) collective-permute-start(f32[48,256]{1,0:T(8,128)S(1)} %fusion.2.refs_0_), channel_id=1, source_target_pairs={{0,384},{16,400},{32,416},{48,432},{64,448},{80,464},{96,480},{112... | collective-permute-start | bytes 147464 | tf_op jit(solution)/shard_map/ppermute | solution.py:45
  80.7 1.2 copy-start.3
  81.9 42.9 %all-to-all-start.3 = ((f32[8,4,48,256]{3,2,1,0:T(8,128)}), f32[8,4,48,256]{3,2,1,0:T(8,128)}, u32[]{:S(2)}, u32[]{:S(2)}) async-start(f32[8,4,48,256]{3,2,1,0:T(8,128)} %copy-done.3), calls=%async_computation.3 | async-start | bytes 3145728 | tf_op jit(solution)/shard_map/all_to_all | solution.py:33
  87.6 19.0 %collective-permute-start.10 = (f32[48,256]{1,0:T(8,128)S(1)}, f32[48,256]{1,0:T(8,128)S(1)}, u32[]{:S(2)}, u32[]{:S(2)}) collective-permute-start(f32[48,256]{1,0:T(8,128)S(1)} %get-tuple-element.21), channel_id=1, source_target_pairs={{0,256},{16,272},{32,288},{48,304},{64,320},{80,336},{96,352},{112... | collective-permute-start | bytes 147464 | tf_op jit(solution)/shard_map/ppermute | solution.py:45
  93.3 14.2 %collective-permute-start.8 = (f32[48,256]{1,0:T(8,128)S(1)}, f32[48,256]{1,0:T(8,128)S(1)}, u32[]{:S(2)}, u32[]{:S(2)}) collective-permute-start(f32[48,256]{1,0:T(8,128)S(1)} %get-tuple-element.19), channel_id=1, source_target_pairs={{0,128},{16,144},{32,160},{48,176},{64,192},{80,208},{96,224},{112... | collective-permute-start | bytes 147464 | tf_op jit(solution)/shard_map/ppermute | solution.py:45
  96.1 11.4 %collective-permute-start.9 = (f32[48,256]{1,0:T(8,128)S(1)}, f32[48,256]{1,0:T(8,128)S(1)}, u32[]{:S(2)}, u32[]{:S(2)}) collective-permute-start(f32[48,256]{1,0:T(8,128)S(1)} %get-tuple-element.20), channel_id=1, source_target_pairs={{0,384},{16,400},{32,416},{48,432},{64,448},{80,464},{96,480},{112... | collective-permute-start | bytes 147464 | tf_op jit(solution)/shard_map/ppermute | solution.py:45
  107.5 11.4 %collective-permute-start.11 = (f32[48,256]{1,0:T(8,128)S(1)}, f32[48,256]{1,0:T(8,128)S(1)}, u32[]{:S(2)}, u32[]{:S(2)}) collective-permute-start(f32[48,256]{1,0:T(8,128)S(1)} %subtract_divide_fusion.refs_0_), channel_id=1, source_target_pairs={{0,128},{16,144},{32,160},{48,176},{64,192},{80,208},{96,224},{112... | collective-permute-start | bytes 147464 | tf_op jit(solution)/shard_map/ppermute | solution.py:45
  109.4 9.5 %collective-permute-start.12 = (f32[48,256]{1,0:T(8,128)S(1)}, f32[48,256]{1,0:T(8,128)S(1)}, u32[]{:S(2)}, u32[]{:S(2)}) collective-permute-start(f32[48,256]{1,0:T(8,128)S(1)} %subtract_divide_fusion.refs_0_), channel_id=1, source_target_pairs={{0,256},{16,272},{32,288},{48,304},{64,320},{80,336},{96,352},{112... | collective-permute-start | bytes 147464 | tf_op jit(solution)/shard_map/ppermute | solution.py:45
  114.7 6.2 %collective-permute-start.13 = (f32[48,256]{1,0:T(8,128)S(1)}, f32[48,256]{1,0:T(8,128)S(1)}, u32[]{:S(2)}, u32[]{:S(2)}) collective-permute-start(f32[48,256]{1,0:T(8,128)S(1)} %subtract_divide_fusion.refs_0_), channel_id=1, source_target_pairs={{0,384},{16,400},{32,416},{48,432},{64,448},{80,464},{96,480},{112... | collective-permute-start | bytes 147464 | tf_op jit(solution)/shard_map/ppermute | solution.py:45
  123.6 1.2 copy-start.4
  124.8 30.8 %all-to-all-start.2 = ((f32[8,4,48,256]{3,2,1,0:T(8,128)}), f32[8,4,48,256]{3,2,1,0:T(8,128)}, u32[]{:S(2)}, u32[]{:S(2)}) async-start(f32[8,4,48,256]{3,2,1,0:T(8,128)} %copy-done.4), calls=%async_computation.2 | async-start | bytes 3145728 | tf_op jit(solution)/shard_map/all_to_all | solution.py:33
  129.1 14.8 %collective-permute-start = (f32[1,1024]{1,0:T(1,128)S(1)}, f32[1,1024]{1,0:T(1,128)S(1)}, u32[]{:S(2)}, u32[]{:S(2)}) collective-permute-start(f32[1,1024]{1,0:T(1,128)S(1)} %get-tuple-element.24), channel_id=1, source_target_pairs={{1,0},{2,1},{3,2},{4,3},{5,4},{6,5},{7,6},{8,7},{9,8},{10,9},{11,1... | collective-permute-start | bytes 12296 | tf_op jit(solution)/shard_map/ppermute | solution.py:274
  138.8 5.8 %collective-permute-start.1 = (f32[1,1024]{1,0:T(1,128)S(1)}, f32[1,1024]{1,0:T(1,128)S(1)}, u32[]{:S(2)}, u32[]{:S(2)}) collective-permute-start(f32[1,1024]{1,0:T(1,128)S(1)} %get-tuple-element.25), channel_id=1, source_target_pairs={{0,1},{1,2},{2,3},{3,4},{4,5},{5,6},{6,7},{7,8},{8,9},{9,10},{10,1... | collective-permute-start | bytes 12296 | tf_op jit(solution)/shard_map/ppermute | solution.py:272

commit v3 on v2

--- a/solution.py
+++ b/solution.py
@@ -16,10 +16,12 @@
 NEAR_SIZE = 2 * NX
 W = 256
 LANES = 128
-HALVES = 2
+HALVES = 1
 FAR_STEPS = (1, 3, 2)
 VMEM_LIMIT = 40 * 1024 * 1024
 VMEM_MOST = 60 * 1024 * 1024
+VMEM_SPREAD = 52 * 1024 * 1024
+VMEM_BACK = 50 * 1024 * 1024
 
 
 def device_of(pair, odd, x):
@@ -73,6 +75,15 @@
     for copy in copies:
         copy.start()
     return copies
+
+
+def mat_copy(mats_hbm, mats, sems, k):
+    return pltpu.make_async_copy(mats_hbm.at[0, k], mats.at[k], sems.at[k])
+
+
+def start_mats(mats_hbm, mats, sems):
+    for k in range(mats.shape[0]):
+        mat_copy(mats_hbm, mats, sems, k).start()
 
 
 def project_kernel(
@@ -90,24 +101,28 @@
         ],
         sems,
     )
-    big = fetch_all([(mats_hbm.at[0, k], mats.at[k]) for k in range(count)], mat_sems)
+    start_mats(mats_hbm, mats, mat_sems)
     out_ref[...] = jnp.zeros(out_ref.shape, jnp.float32)
     wide[:, cols:] = jnp.zeros((rows, LANES), jnp.float32)
     for copy in small:
         copy.wait()
     me = me_ref[0]
-    for k in range(count):
+
+    def step(k, carry):
         start = starts[0, k]
         near, far = near_far(owners[0, lists[k, me]], me, 1)
         base = pl.multiple_of((start // LANES) * LANES, LANES)
         window = wide[:, pl.ds(base, W + LANES)]
         window = pltpu.roll(window, (W + LANES) - start % LANES, 1)[:, :W]
         left = with_ones(window)
-        big[k].wait()
+        mat_copy(mats_hbm, mats, mat_sems, k).wait()
         product = jnp.dot(left, mats[k], preferred_element_type=jnp.float32)
         out_ref[near, pl.ds(pl.multiple_of(far * rows, 8), rows), :] = join3(product, rows)
         if sums:
             out_ref[near, pl.ds(PAIRS * rows + far, 1), :] = product[3 * rows : 3 * rows + 1]
+        return carry
+
+    lax.fori_loop(0, count, step, 0, unroll=2)
 
 
 HBM = pl.BlockSpec(memory_space=pl.ANY)
@@ -191,16 +206,16 @@
             pltpu.VMEM((PAIRS, rows, W), jnp.float32),
             pltpu.SemaphoreType.DMA((NEAR_SIZE,)),
         ],
-        compiler_params=pltpu.CompilerParams(vmem_limit_bytes=VMEM_LIMIT),
+        compiler_params=pltpu.CompilerParams(vmem_limit_bytes=VMEM_SPREAD),
     )(*parts)
 
 
 def back_kernel(
-    first, rows, has_old, me_ref, lists_hbm, owners_hbm, starts_hbm, base_hbm, mats_hbm, got_ref, *rest
+    first, rows, has_old, me_ref, lists_hbm, owners_hbm, starts_hbm, base_hbm, mats_hbm, got_hbm, *rest
 ):
     if has_old:
         rest = rest[1:]
-    out_hbm, lists, owners, starts, base_v, mats, total, result, sems, mat_sems, out_sem = rest
+    out_hbm, lists, owners, starts, base_v, mats, got, total, result, sems, mat_sems, got_sems, out_sem = rest
     count = mats.shape[0]
     cols = base_hbm.shape[1]
     small = fetch_all(
@@ -212,23 +227,35 @@
         ],
         sems,
     )
-    big = fetch_all([(mats_hbm.at[0, k], mats.at[k]) for k in range(count)], mat_sems)
+    start_mats(mats_hbm, mats, mat_sems)
     total[...] = jnp.zeros(total.shape, jnp.float32)
-    for copy in small:
+    for copy in small[:-1]:
         copy.wait()
     me = me_ref[0]
+
+    def got_copy(k):
+        near, far = near_far(owners[0, lists[k, me]], me, -1)
+        return pltpu.make_async_copy(got_hbm.at[near, far], got.at[k], got_sems.at[k])
+
     for k in range(count):
+        got_copy(k).start()
+
+    def step(k, carry):
         start = starts[0, k]
-        near, far = near_far(owners[0, lists[k, me]], me, -1)
         base = pl.multiple_of((start // LANES) * LANES, LANES)
-        left = with_ones(got_ref[near, far])
-        big[k].wait()
+        got_copy(k).wait()
+        left = with_ones(got[k])
+        mat_copy(mats_hbm, mats, mat_sems, k).wait()
         product = lax.dot_general(
             left, mats[k], (((1,), (1,)), ((), ())), preferred_element_type=jnp.float32
         )
         value = jnp.concatenate([join3(product, rows), product[3 * rows : 3 * rows + 8]], axis=0)
         value = jnp.concatenate([value, jnp.zeros((rows + 8, LANES), jnp.float32)], axis=1)
         total[:, pl.ds(base, W + LANES)] += pltpu.roll(value, start % LANES, 1)
+        return carry
+
+    lax.fori_loop(0, count, step, 0, unroll=2)
+    small[-1].wait()
     column = jnp.maximum(total[rows : rows + 1, :cols], 1.0)
     result[...] = base_v[...] + relax * (total[:rows, :cols] / column)
     out = pltpu.make_async_copy(result, out_hbm.at[pl.ds(first, rows)], out_sem.at[0])
@@ -243,20 +270,22 @@
     return pl.pallas_call(
         functools.partial(back_kernel, first, rows, bool(more)),
         out_shape=jax.ShapeDtypeStruct(base.shape, jnp.float32),
-        in_specs=[SMEM] + [HBM] * 5 + [VMEM] + [HBM] * len(more),
+        in_specs=[SMEM] + [HBM] * (6 + len(more)),
         out_specs=HBM,
         scratch_shapes=small_scratch(lists, owners, starts)
         + [
             pltpu.VMEM((rows, cols), jnp.float32),
             pltpu.VMEM(mats.shape[1:], jnp.bfloat16),
+            pltpu.VMEM((count, rows, W), jnp.float32),
             pltpu.VMEM((rows + 8, cols + LANES), jnp.float32),
             pltpu.VMEM((rows, cols), jnp.float32),
             pltpu.SemaphoreType.DMA((4,)),
             pltpu.SemaphoreType.DMA((count,)),
+            pltpu.SemaphoreType.DMA((count,)),
             pltpu.SemaphoreType.DMA((1,)),
         ],
         input_output_aliases={7: 0} if more else {},
-        compiler_params=pltpu.CompilerParams(vmem_limit_bytes=VMEM_LIMIT),
+        compiler_params=pltpu.CompilerParams(vmem_limit_bytes=VMEM_BACK),
         cost_estimate=pl.CostEstimate(
             flops=2 * 3 * count * rows * W * W, bytes_accessed=6 << 20, transcendentals=0
         ),

time: 168 us -> 145 us (0.86)
  blocking collectives: 0 us -> 40.1 us
  starting transfers between devices: 87.3 us -> 47.5 us
  Pallas kernels: 40.6 us -> 21.9 us
  local copies, waits for them, and re-layouts: 3.53 us -> 0.06 us
    all_to_all x0 -> x1, blocking collectives: none -> 40.1 us  [near_exchange(): lax.all_to_all(value, 'xy', split_axis=0, concat_axis=0, axis_index_group...]
    all_to_all x4 -> x1, starting transfers between devices: 22.5 us -> 4.59 us  [near_exchange(): lax.all_to_all(value, 'xy', split_axis=0, concat_axis=0, axis_index_group...]
    ppermute x12 -> x6, starting transfers between devices: 50 us -> 32.2 us  [far_send(): return lax.ppermute(value, 'xy', moves)]
    ppermute x12 -> x6, waiting for transfers between devices: 22.9 us -> 6.03 us  [far_send(): return lax.ppermute(value, 'xy', moves)]
    all_to_all x4 -> x1, waiting for transfers between devices: 8.9 us -> 25.1 us  [near_exchange(): lax.all_to_all(value, 'xy', split_axis=0, concat_axis=0, axis_index_group...]
    pallas_call x2 -> x1, Pallas kernels: 20.3 us -> 11 us  [back_project(): pl.pallas_call(functools.partial(back_kernel, first, rows, bool(more)), o...]
    pallas_call x2 -> x1, Pallas kernels: 12.4 us -> 8.32 us  [project(): pl.pallas_call(functools.partial(project_kernel, first, rows, sums), out_...]
    unnamed x18 -> x14, local copies, waits for them, and re-layouts: 3.52 us -> 0.04 us
  transfers between devices with their start and end apart: 18 -> 9, of which waited for: 9 -> 5; matrix products, arithmetic and copies ran while one was open for 1% -> 0% of each run, Pallas kernels for 15% -> 0%
where the time goes in v3:
time: 145 us; the launch traced here: 142 us
  starting transfers between devices  47.5 us (33%)
  blocking collectives  40.1 us (28%)
  waiting for transfers between devices  31.8 us (22%)
  Pallas kernels  21.9 us (15%)
    all_to_all x1, blocking collectives, near_exchange(): lax.all_to_all(value, 'xy', split_axis=0, concat_axis=0, axis_index_group...  40.1 us
    ppermute x6, starting transfers between devices, far_send(): return lax.ppermute(value, 'xy', moves)  32.2 us
    all_to_all x1, waiting for transfers between devices, near_exchange(): lax.all_to_all(value, 'xy', split_axis=0, concat_axis=0, axis_index_group...  25.1 us
    pallas_call x1, Pallas kernels, back_project(): pl.pallas_call(functools.partial(back_kernel, first, rows, bool(more)), o...  11 us
    pallas_call x1, Pallas kernels, project(): pl.pallas_call(functools.partial(project_kernel, first, rows, sums), out_...  8.32 us
    ppermute x1, starting transfers between devices, with_faces(): lax.ppermute(volume[:1], 'gz', down)  6.71 us
    ppermute x6, waiting for transfers between devices, far_send(): return lax.ppermute(value, 'xy', moves)  6.03 us
    all_to_all x1, starting transfers between devices, near_exchange(): lax.all_to_all(value, 'xy', split_axis=0, concat_axis=0, axis_index_group...  4.59 us
  transfers between devices with their start and end apart: 9, of which 5 were waited for; matrix products, arithmetic and copies ran while one was open for 0% of the time, Pallas kernels for 0%

profile of v3, /device:TPU:1, one launch (start us, length us, event | category | flops | bytes accessed | tf_op | source)
XLA Modules:
  0.0 142.5 jit_solution(922430710024760959)
XLA Ops:
  0.6 8.3 %shard_map.77 = f32[8,392,256]{2,1,0:T(8,128)} custom-call(s32[1]{0:T(128)} %bitcast.me_ref, s32[16,32]{1,0:T(8,128)} %bitcast.4, s32[1,32]{1,0:T(1,128)} %bitcast.6, s32[1,16]{1,0:T(1,128)} %starts_hbm.3, f32[96,1024]{1,0:T(8,128)} %vol_hbm.1, bf16[1,16,256,256]{3,2,1,0:T(8,128)(2,1)} %mats_hbm.3), custom_call_target="tpu_custom_call" | custom-call | flops 603979776 | bytes 6291456 | tf_op jit(solution)/shard_map/pallas_call | solution.py:141
  9.0 40.1 %all_to_all.10.in_ref = f32[8,392,256]{2,1,0:T(8,128)S(1)} all-to-all(f32[8,392,256]{2,1,0:T(8,128)} %shard_map.77), channel_id=1, replica_groups={{0,16,32,48,64,80,96,112},{128,144,160,176,192,208,224,240},{256,272,28..., dimensions={0} | all-to-all | bytes 6422528 | tf_op jit(solution)/shard_map/all_to_all | solution.py:35
  49.1 0.0 copy-start.6
  49.1 0.1 shard_map.78
  49.3 8.0 %collective-permute-start.2 = (f32[104,256]{1,0:T(8,128)S(1)}, f32[104,256]{1,0:T(8,128)S(1)}, u32[]{:S(2)}, u32[]{:S(2)}) collective-permute-start(f32[104,256]{1,0:T(8,128)S(1)} %get-tuple-element.8), channel_id=1, source_target_pairs={{0,128},{16,144},{32,160},{48,176},{64,192},{80,208},{96,224},{112... | collective-permute-start | bytes 319496 | tf_op jit(solution)/shard_map/ppermute | solution.py:47
  57.3 2.7 %collective-permute-start.3 = (f32[104,256]{1,0:T(8,128)S(1)}, f32[104,256]{1,0:T(8,128)S(1)}, u32[]{:S(2)}, u32[]{:S(2)}) collective-permute-start(f32[104,256]{1,0:T(8,128)S(1)} %get-tuple-element.9), channel_id=1, source_target_pairs={{0,384},{16,400},{32,416},{48,432},{64,448},{80,464},{96,480},{112... | collective-permute-start | bytes 319496 | tf_op jit(solution)/shard_map/ppermute | solution.py:47
  60.0 7.0 %collective-permute-start.4 = (f32[104,256]{1,0:T(8,128)S(1)}, f32[104,256]{1,0:T(8,128)S(1)}, u32[]{:S(2)}, u32[]{:S(2)}) collective-permute-start(f32[104,256]{1,0:T(8,128)S(1)} %get-tuple-element.10), channel_id=1, source_target_pairs={{0,256},{16,272},{32,288},{48,304},{64,320},{80,336},{96,352},{112... | collective-permute-start | bytes 319496 | tf_op jit(solution)/shard_map/ppermute | solution.py:47
  67.1 0.0 collective-permute-done.2
  67.1 0.0 collective-permute-done.3
  67.1 2.4 %collective-permute-done.4 = f32[104,256]{1,0:T(8,128)S(1)} collective-permute-done((f32[104,256]{1,0:T(8,128)S(1)}, f32[104,256]{1,0:T(8,128)S(1)}, u32[]{:S(2)}, u32[]{:S(2)}) %collective-permute-start.4) | collective-permute-done | bytes 106528 | tf_op jit(solution)/shard_map/ppermute | solution.py:47
  69.5 0.0 copy-done.6
  69.5 0.0 copy-start.1
  69.5 4.8 %collective-permute-start.5 = (f32[96,256]{1,0:T(8,128)S(1)}, f32[96,256]{1,0:T(8,128)S(1)}, u32[]{:S(2)}, u32[]{:S(2)}) collective-permute-start(f32[96,256]{1,0:T(8,128)S(1)} %fusion.2.refs_0_), channel_id=1, source_target_pairs={{0,128},{16,144},{32,160},{48,176},{64,192},{80,208},{96,224},{112... | collective-permute-start | bytes 294920 | tf_op jit(solution)/shard_map/ppermute | solution.py:47
  74.4 4.2 %collective-permute-start.6 = (f32[96,256]{1,0:T(8,128)S(1)}, f32[96,256]{1,0:T(8,128)S(1)}, u32[]{:S(2)}, u32[]{:S(2)}) collective-permute-start(f32[96,256]{1,0:T(8,128)S(1)} %fusion.2.refs_0_), channel_id=1, source_target_pairs={{0,256},{16,272},{32,288},{48,304},{64,320},{80,336},{96,352},{112... | collective-permute-start | bytes 294920 | tf_op jit(solution)/shard_map/ppermute | solution.py:47
  78.6 5.5 %collective-permute-start.7 = (f32[96,256]{1,0:T(8,128)S(1)}, f32[96,256]{1,0:T(8,128)S(1)}, u32[]{:S(2)}, u32[]{:S(2)}) collective-permute-start(f32[96,256]{1,0:T(8,128)S(1)} %fusion.2.refs_0_), channel_id=1, source_target_pairs={{0,384},{16,400},{32,416},{48,432},{64,448},{80,464},{96,480},{112... | collective-permute-start | bytes 294920 | tf_op jit(solution)/shard_map/ppermute | solution.py:47
  84.0 0.0 collective-permute-done.5.refs_1_
  84.1 1.3 collective-permute-done.6.refs_2_
  85.4 2.3 %collective-permute-done.7.refs_3_ = f32[96,256]{1,0:T(8,128)S(1)} collective-permute-done((f32[96,256]{1,0:T(8,128)S(1)}, f32[96,256]{1,0:T(8,128)S(1)}, u32[]{:S(2)}, u32[]{:S(2)}) %collective-permute-start.7) | collective-permute-done | bytes 98336 | tf_op jit(solution)/shard_map/ppermute | solution.py:47
  87.7 2.4 %shard_map.79 = (f32[8,4,96,256]{3,2,1,0:T(8,128)}, f32[8,128]{1,0:T(8,128)}) custom-call(f32[96,256]{1,0:T(8,128)S(1)} %fusion.2.refs_0_, f32[96,256]{1,0:T(8,128)S(1)} %collective-permute-done.5.refs_1_, f32[96,256]{1,0:T(8,128)S(1)} %collective-permute-done.6.refs_2_, f32[96,256]{1,0:T(8,128)S(1)} %collective-permute-done.7.refs_3_), custom_call_target="tpu_custom_call" | custom-call | tf_op jit(solution)/shard_map/pallas_call | solution.py:197
  90.1 0.0 copy-start.5
  90.1 0.0 copy-start
  90.1 0.0 copy-start.2
  90.1 0.0 copy-start.3
  90.1 0.0 copy-start.4
  90.1 0.0 copy-done.1
  90.1 4.6 %all-to-all-start.1 = ((f32[8,4,96,256]{3,2,1,0:T(8,128)}), f32[8,4,96,256]{3,2,1,0:T(8,128)}, u32[]{:S(2)}, u32[]{:S(2)}) async-start(f32[8,4,96,256]{3,2,1,0:T(8,128)} %get-tuple-element.11), calls=%async_computation.1 | async-start | bytes 6291456 | tf_op jit(solution)/shard_map/all_to_all | solution.py:35
  94.7 0.0 copy-done.5
  94.8 6.7 %collective-permute-start = (f32[1,1024]{1,0:T(1,128)S(1)}, f32[1,1024]{1,0:T(1,128)S(1)}, u32[]{:S(2)}, u32[]{:S(2)}) collective-permute-start(f32[1,1024]{1,0:T(1,128)S(1)} %get-tuple-element.12), channel_id=1, source_target_pairs={{1,0},{2,1},{3,2},{4,3},{5,4},{6,5},{7,6},{8,7},{9,8},{10,9},{11,1... | collective-permute-start | bytes 12296 | tf_op jit(solution)/shard_map/ppermute | solution.py:303
  101.5 3.9 %collective-permute-start.1 = (f32[1,1024]{1,0:T(1,128)S(1)}, f32[1,1024]{1,0:T(1,128)S(1)}, u32[]{:S(2)}, u32[]{:S(2)}) collective-permute-start(f32[1,1024]{1,0:T(1,128)S(1)} %get-tuple-element.13), channel_id=1, source_target_pairs={{0,1},{1,2},{2,3},{3,4},{4,5},{5,6},{6,7},{7,8},{8,9},{9,10},{10,1... | collective-permute-start | bytes 12296 | tf_op jit(solution)/shard_map/ppermute | solution.py:301
  105.4 0.0 collective-permute-done
  105.4 0.7 collective-permute-done.1
  106.2 0.1 rsqrt_multiply_fusion
  106.3 0.1 fusion.1.base_hbm
  106.4 25.1 %all-to-all-done.1.got_hbm = f32[8,4,96,256]{3,2,1,0:T(8,128)} async-done(((f32[8,4,96,256]{3,2,1,0:T(8,128)}), f32[8,4,96,256]{3,2,1,0:T(8,128)}, u32[]{:S(2)}, u32[]{:S(2)}) %all-to-all-start.1) | async-done | bytes 3145760 | tf_op jit(solution)/shard_map/all_to_all | solution.py:35
  131.4 0.0 copy-done
  131.4 0.0 copy-done.2
  131.4 0.0 copy-done.3
  131.5 0.0 copy-done.4
  131.5 11.0 %shard_map.80 = f32[96,1024]{1,0:T(8,128)} custom-call(s32[1]{0:T(128)} %bitcast.me_ref, s32[16,32]{1,0:T(8,128)S(1)} %bitcast.5, s32[1,32]{1,0:T(1,128)S(1)} %bitcast.7, s32[1,16]{1,0:T(1,128)S(1)} %copy-done.4, f32[96,1024]{1,0:T(8,128)S(1)} %fusion.1.base_hbm, bf16[1,16,256,256]{3,2,1,0:T(8,128)(2,1)S(1)} %copy-done, f32[8,4,96,256]{3,2,1,0:T(8,128)} %all-to-all-done.1.got_hbm), custom_call_target="tpu_custom_call" | custom-call | flops 603979776 | bytes 6291456 | tf_op jit(solution)/shard_map/pallas_call | solution.py:270
  (4 shorter events, 0.1 us)
Async XLA Ops:
  49.1 20.4 %copy-start.6 = (f32[96,256]{1,0:T(8,128)S(1)}, f32[96,256]{1,0:T(8,128)}, u32[]{:S(2)}) copy-start(f32[96,256]{1,0:T(8,128)} %param.7) | copy-start | bytes 294916
  49.3 17.8 %collective-permute-start.2 = (f32[104,256]{1,0:T(8,128)S(1)}, f32[104,256]{1,0:T(8,128)S(1)}, u32[]{:S(2)}, u32[]{:S(2)}) collective-permute-start(f32[104,256]{1,0:T(8,128)S(1)} %get-tuple-element.8), channel_id=1, source_target_pairs={{0,128},{16,144},{32,160},{48,176},{64,192},{80,208},{96,224},{112... | collective-permute-start | bytes 319496 | tf_op jit(solution)/shard_map/ppermute | solution.py:47
  57.3 9.8 %collective-permute-start.3 = (f32[104,256]{1,0:T(8,128)S(1)}, f32[104,256]{1,0:T(8,128)S(1)}, u32[]{:S(2)}, u32[]{:S(2)}) collective-permute-start(f32[104,256]{1,0:T(8,128)S(1)} %get-tuple-element.9), channel_id=1, source_target_pairs={{0,384},{16,400},{32,416},{48,432},{64,448},{80,464},{96,480},{112... | collective-permute-start | bytes 319496 | tf_op jit(solution)/shard_map/ppermute | solution.py:47
  60.0 9.5 %collective-permute-start.4 = (f32[104,256]{1,0:T(8,128)S(1)}, f32[104,256]{1,0:T(8,128)S(1)}, u32[]{:S(2)}, u32[]{:S(2)}) collective-permute-start(f32[104,256]{1,0:T(8,128)S(1)} %get-tuple-element.10), channel_id=1, source_target_pairs={{0,256},{16,272},{32,288},{48,304},{64,320},{80,336},{96,352},{112... | collective-permute-start | bytes 319496 | tf_op jit(solution)/shard_map/ppermute | solution.py:47
  69.5 20.6 %copy-start.1 = (f32[96,256]{1,0:T(8,128)}, f32[96,256]{1,0:T(8,128)S(1)}, u32[]{:S(2)}) copy-start(f32[96,256]{1,0:T(8,128)S(1)} %fusion.2.refs_0_) | copy-start | bytes 294916
  69.5 14.5 %collective-permute-start.5 = (f32[96,256]{1,0:T(8,128)S(1)}, f32[96,256]{1,0:T(8,128)S(1)}, u32[]{:S(2)}, u32[]{:S(2)}) collective-permute-start(f32[96,256]{1,0:T(8,128)S(1)} %fusion.2.refs_0_), channel_id=1, source_target_pairs={{0,128},{16,144},{32,160},{48,176},{64,192},{80,208},{96,224},{112... | collective-permute-start | bytes 294920 | tf_op jit(solution)/shard_map/ppermute | solution.py:47
  74.4 11.0 %collective-permute-start.6 = (f32[96,256]{1,0:T(8,128)S(1)}, f32[96,256]{1,0:T(8,128)S(1)}, u32[]{:S(2)}, u32[]{:S(2)}) collective-permute-start(f32[96,256]{1,0:T(8,128)S(1)} %fusion.2.refs_0_), channel_id=1, source_target_pairs={{0,256},{16,272},{32,288},{48,304},{64,320},{80,336},{96,352},{112... | collective-permute-start | bytes 294920 | tf_op jit(solution)/shard_map/ppermute | solution.py:47
  78.6 9.1 %collective-permute-start.7 = (f32[96,256]{1,0:T(8,128)S(1)}, f32[96,256]{1,0:T(8,128)S(1)}, u32[]{:S(2)}, u32[]{:S(2)}) collective-permute-start(f32[96,256]{1,0:T(8,128)S(1)} %fusion.2.refs_0_), channel_id=1, source_target_pairs={{0,384},{16,400},{32,416},{48,432},{64,448},{80,464},{96,480},{112... | collective-permute-start | bytes 294920 | tf_op jit(solution)/shard_map/ppermute | solution.py:47
  90.1 4.7 %copy-start.5 = (f32[96,1024]{1,0:T(8,128)S(1)}, f32[96,1024]{1,0:T(8,128)}, u32[]{:S(2)}) copy-start(f32[96,1024]{1,0:T(8,128)} %vol_hbm.1) | copy-start | bytes 1179652
  90.1 41.4 %copy-start = (bf16[1,16,256,256]{3,2,1,0:T(8,128)(2,1)S(1)}, bf16[1,16,256,256]{3,2,1,0:T(8,128)(2,1)}, u32[]{:S(2)}) copy-start(bf16[1,16,256,256]{3,2,1,0:T(8,128)(2,1)} %mats_hbm.3) | copy-start | bytes 6291460
  90.1 41.3 %copy-start.2 = (s32[32,16]{0,1:T(8,128)S(1)}, s32[32,16]{0,1:T(8,128)}, u32[]{:S(2)}) copy-start(s32[32,16]{0,1:T(8,128)} %param.10) | copy-start | bytes 6148
  90.1 41.3 %copy-start.3 = (s32[32]{0:T(128)S(1)}, s32[32]{0:T(128)}, u32[]{:S(2)}) copy-start(s32[32]{0:T(128)} %param.11) | copy-start | bytes 388
  90.1 41.3 %copy-start.4 = (s32[1,16]{1,0:T(1,128)S(1)}, s32[1,16]{1,0:T(1,128)}, u32[]{:S(2)}) copy-start(s32[1,16]{1,0:T(1,128)} %starts_hbm.3) | copy-start | bytes 196
  90.1 41.3 %all-to-all-start.1 = ((f32[8,4,96,256]{3,2,1,0:T(8,128)}), f32[8,4,96,256]{3,2,1,0:T(8,128)}, u32[]{:S(2)}, u32[]{:S(2)}) async-start(f32[8,4,96,256]{3,2,1,0:T(8,128)} %get-tuple-element.11), calls=%async_computation.1 | async-start | bytes 6291456 | tf_op jit(solution)/shard_map/all_to_all | solution.py:35
  94.8 10.7 %collective-permute-start = (f32[1,1024]{1,0:T(1,128)S(1)}, f32[1,1024]{1,0:T(1,128)S(1)}, u32[]{:S(2)}, u32[]{:S(2)}) collective-permute-start(f32[1,1024]{1,0:T(1,128)S(1)} %get-tuple-element.12), channel_id=1, source_target_pairs={{1,0},{2,1},{3,2},{4,3},{5,4},{6,5},{7,6},{8,7},{9,8},{10,9},{11,1... | collective-permute-start | bytes 12296 | tf_op jit(solution)/shard_map/ppermute | solution.py:303
  101.5 4.7 %collective-permute-start.1 = (f32[1,1024]{1,0:T(1,128)S(1)}, f32[1,1024]{1,0:T(1,128)S(1)}, u32[]{:S(2)}, u32[]{:S(2)}) collective-permute-start(f32[1,1024]{1,0:T(1,128)S(1)} %get-tuple-element.13), channel_id=1, source_target_pairs={{0,1},{1,2},{2,3},{3,4},{4,5},{5,6},{6,7},{7,8},{8,9},{9,10},{10,1... | collective-permute-start | bytes 12296 | tf_op jit(solution)/shard_map/ppermute | solution.py:301

commit v4 on v1

v4 whole, which is shorter than its diff:
```python
import functools

import jax
import jax.numpy as jnp
from jax import lax
from jax.experimental import pallas as pl
from jax.experimental.pallas import tpu as pltpu
from jax.sharding import PartitionSpec as P

relax = 1.0
tv_weight = 0.2
smooth_sq = 0.01

NX, NY = 4, 8
PAIRS = NY // 2
NEAR_SIZE = 2 * NX
W = 256
LANES = 128
VMEM_LIMIT = 32 * 1024 * 1024


def device_of(pair, odd, x):
    return (2 * pair + odd) * NX + x


NEAR = [[device_of(p, q, x) for q in range(2) for x in range(NX)] for p in range(PAIRS)]
FAR = [[device_of(p, q, x) for p in range(PAIRS)] for q in range(2) for x in range(NX)]


def exchange(value, groups):
    return lax.all_to_all(
        value, "xy", split_axis=0, concat_axis=0, axis_index_groups=groups, tiled=True
    )


def split3(value):
    high = value.astype(jnp.bfloat16)
    rest = value - high.astype(jnp.float32)
    mid = rest.astype(jnp.bfloat16)
    low = (rest - mid.astype(jnp.float32)).astype(jnp.bfloat16)
    return [high, mid, low]


def with_ones(value):
    ones = jnp.ones((16, value.shape[1]), jnp.bfloat16)
    return jnp.concatenate(split3(value) + [ones], axis=0)


def near_far(owner):
    y, x = owner // NX, owner % NX
    return (y % 2) * NX + x, y // 2


def join3(product, rows):
    return product[2 * rows : 3 * rows] + product[rows : 2 * rows] + product[:rows]


def fetch_all(pairs, sems):
    copies = [pltpu.make_async_copy(src, dst, sems.at[i]) for i, (src, dst) in enumerate(pairs)]
    for copy in copies:
        copy.start()
    return copies


def pinned(value, space):
    return pltpu.with_memory_space_constraint(value, space)


ANY = pl.BlockSpec(memory_space=pl.ANY)
SMEM = pl.BlockSpec(memory_space=pltpu.SMEM)
VMEM = pl.BlockSpec(memory_space=pltpu.VMEM)
PARAMS = pltpu.CompilerParams(vmem_limit_bytes=VMEM_LIMIT)


def small_scratch(lists, owners, starts):
    return [pltpu.SMEM(a.shape, jnp.int32) for a in (lists, owners, starts)]


def project_kernel(
    me_ref, lists_hbm, owners_hbm, starts_hbm, vol_hbm, mats_hbm, out_ref, mats_ref,
    lists, owners, starts, wide, sems,
):
    rows, cols = vol_hbm.shape
    count = mats_ref.shape[0]
    copies = fetch_all(
        [
            (lists_hbm, lists),
            (owners_hbm, owners),
            (starts_hbm, starts),
            (vol_hbm, wide.at[:, pl.ds(0, cols)]),
            (mats_hbm.at[0], mats_ref),
        ],
        sems,
    )
    wide[:, cols:] = jnp.zeros((rows, LANES), jnp.float32)
    out_ref[...] = jnp.zeros(out_ref.shape, jnp.float32)
    for copy in copies:
        copy.wait()
    me = me_ref[0]
    for k in range(count):
        start = starts[0, k]
        near, far = near_far(owners[0, lists[k, me]])
        base = pl.multiple_of((start // LANES) * LANES, LANES)
        window = wide[:, pl.ds(base, W + LANES)]
        window = pltpu.roll(window, (W + LANES) - start % LANES, 1)[:, :W]
        product = jnp.dot(with_ones(window), mats_ref[k], preferred_element_type=jnp.float32)
        out_ref[near, pl.ds(pl.multiple_of(far * rows, 8), rows), :] = join3(product, rows)
        out_ref[near, pl.ds(PAIRS * rows + far, 1), :] = product[3 * rows : 3 * rows + 1]


def project(me, lists, owners, starts, volume, mats):
    rows, cols = volume.shape
    operands = [pinned(a, pltpu.HBM) for a in (lists, owners, starts, volume, mats)]
    return pl.pallas_call(
        project_kernel,
        out_shape=[
            pltpu.VMEM((NEAR_SIZE, PAIRS * rows + 8, W), jnp.float32),
            pltpu.VMEM(mats.shape[1:], jnp.bfloat16),
        ],
        in_specs=[SMEM] + [ANY] * 5,
        out_specs=[VMEM, VMEM],
        scratch_shapes=small_scratch(lists, owners, starts)
        + [pltpu.VMEM((rows, cols + LANES), jnp.float32), pltpu.SemaphoreType.DMA((5,))],
        compiler_params=PARAMS,
    )(me, *operands)


def gather_kernel(rows, in_ref, vol_hbm, out_ref, first_ref, last_ref, ends, sems):
    height = vol_hbm.shape[0]
    copies = fetch_all(
        [
            (vol_hbm.at[pl.ds(0, 8)], ends.at[0]),
            (vol_hbm.at[pl.ds(height - 8, 8)], ends.at[1]),
        ],
        sems,
    )
    total = in_ref[0]
    for i in range(1, NEAR_SIZE):
        total = total + in_ref[i]
    for far in range(PAIRS):
        out_ref[far, :rows] = total[far * rows : (far + 1) * rows]
        out_ref[far, rows:] = jnp.broadcast_to(
            total[PAIRS * rows + far : PAIRS * rows + far + 1], (8, W)
        )
    for copy in copies:
        copy.wait()
    first_ref[...] = ends[0, :1]
    last_ref[...] = ends[1, 7:]


def gather_near(arrived, volume):
    rows, cols = volume.shape
    face = jax.ShapeDtypeStruct((1, cols), jnp.float32)
    return pl.pallas_call(
        functools.partial(gather_kernel, rows),
        out_shape=[jax.ShapeDtypeStruct((PAIRS, rows + 8, W), jnp.float32), face, face],
        in_specs=[VMEM, ANY],
        out_specs=[VMEM] * 3,
        scratch_shapes=[pltpu.VMEM((2, 8, cols), jnp.float32), pltpu.SemaphoreType.DMA((2,))],
        compiler_params=PARAMS,
    )(pinned(arrived, pltpu.VMEM), pinned(volume, pltpu.HBM))


def spread_kernel(column_ref, after_ref, out_ref):
    for i in range(NEAR_SIZE):
        out_ref[i] = column_ref[...]


def spread_near(column, after):
    return pl.pallas_call(
        spread_kernel,
        out_shape=pltpu.VMEM((NEAR_SIZE,) + column.shape, jnp.float32),
        in_specs=[VMEM, ANY],
        out_specs=VMEM,
        compiler_params=PARAMS,
    )(column, after)


def back_kernel(
    me_ref, lists_hbm, owners_hbm, starts_hbm, base_ref, mats_ref, got_ref, out_ref,
    lists, owners, starts, total, sems,
):
    rows, cols = base_ref.shape
    count = mats_ref.shape[0]
    copies = fetch_all([(lists_hbm, lists), (owners_hbm, owners), (starts_hbm, starts)], sems)
    total[...] = jnp.zeros(total.shape, jnp.float32)
    for copy in copies:
        copy.wait()
    me = me_ref[0]
    for k in range(count):
        start = starts[0, k]
        near, far = near_far(owners[0, lists[k, me]])
        base = pl.multiple_of((start // LANES) * LANES, LANES)
        product = lax.dot_general(
            with_ones(got_ref[near, far]),
            mats_ref[k],
            (((1,), (1,)), ((), ())),
            preferred_element_type=jnp.float32,
        )
        value = jnp.concatenate([join3(product, rows), product[3 * rows : 3 * rows + 8]], axis=0)
        value = jnp.concatenate([value, jnp.zeros((rows + 8, LANES), jnp.float32)], axis=1)
        total[:, pl.ds(base, W + LANES)] += pltpu.roll(value, start % LANES, 1)
    column = jnp.maximum(total[rows : rows + 1, :cols], 1.0)
    out_ref[...] = base_ref[...] + relax * (total[:rows, :cols] / column)


def back_project(me, lists, owners, starts, base, mats, got):
    rows, cols = base.shape
    operands = [pinned(a, pltpu.HBM) for a in (lists, owners, starts)]
    operands += [pinned(a, pltpu.VMEM) for a in (base, mats, got)]
    return pl.pallas_call(
        back_kernel,
        out_shape=jax.ShapeDtypeStruct((rows, cols), jnp.float32),
        in_specs=[SMEM] + [ANY] * 3 + [VMEM] * 3,
        out_specs=VMEM,
        scratch_shapes=small_scratch(lists, owners, starts)
        + [pltpu.VMEM((rows + 8, cols + LANES), jnp.float32), pltpu.SemaphoreType.DMA((3,))],
        compiler_params=PARAMS,
    )(me, *operands)


def with_faces(volume, first, last):
    count = lax.axis_size("gz")
    up = [(i, i + 1) for i in range(count - 1)]
    down = [(i + 1, i) for i in range(count - 1)]
    return jnp.concatenate(
        [lax.ppermute(last, "gz", up), volume, lax.ppermute(first, "gz", down)], axis=0
    )


def total_variation(padded):
    diffs = padded[1:] - padded[:-1]
    slopes = diffs / jnp.sqrt(diffs * diffs + smooth_sq)
    return slopes[:-1] - slopes[1:]


def per_device(volume, sinogram, ray_mats, offsets, ray_lists, owner_map):
    rows = volume.shape[0]
    me = lax.axis_index("xy").astype(jnp.int32).reshape(1)
    plan = (me, ray_lists.T, owner_map.reshape(1, -1), offsets)
    outgoing, mats = project(*plan, volume, ray_mats)
    outgoing, first, last = gather_near(exchange(outgoing, NEAR), volume)
    arrived = jnp.sum(exchange(outgoing, FAR), axis=0)
    base = volume - tv_weight * total_variation(with_faces(volume, first, last))
    weighted = (sinogram - arrived[:rows]) / arrived[rows : rows + 1]
    column = exchange(jnp.broadcast_to(weighted[None], (PAIRS, rows, W)), FAR)
    got = exchange(spread_near(column, base), NEAR)
    new_volume = back_project(*plan, base, mats, got)
    return (new_volume, weighted)


def solution(mesh):
    in_specs = (P("gz", "xy"), P("gz", "xy"), P("xy", None, None, None), P("xy", None), P(), P())
    out_specs = (P("gz", "xy"), P("gz", "xy"))
    return jax.shard_map(
        per_device, mesh=mesh, in_specs=in_specs, out_specs=out_specs, check_vma=False
    )
```

time: 142 us -> 126 us (0.89)
  the two profiles are of different devices: /device:TPU:1 before, /device:TPU:208 now
where the time goes in v4:
time: 126 us
  blocking collectives  103 us (82%)
  starting transfers between devices  9.11 us (7%)
  Pallas kernels  6.95 us (6%)
  waiting for transfers between devices  5 us (4%)
    all_to_all x3, blocking collectives, exchange(): lax.all_to_all(value, 'xy', split_axis=0, concat_axis=0, axis_index_group...  103 us
    all_to_all x1, starting transfers between devices, exchange(): lax.all_to_all(value, 'xy', split_axis=0, concat_axis=0, axis_index_group...  4.79 us
    pallas_call x1, Pallas kernels, project(): pl.pallas_call(project_kernel, out_shape=[pltpu.VMEM((NEAR_SIZE, PAIRS *...  3.05 us
    pallas_call x1, Pallas kernels, back_project(): pl.pallas_call(back_kernel, out_shape=jax.ShapeDtypeStruct((rows, cols),...  2.85 us
  transfers between devices with their start and end apart: 3, of which 2 were waited for; matrix products, arithmetic and copies ran while one was open for 0% of the time, Pallas kernels for 0%

profile of v4, /device:TPU:208, one launch (start us, length us, event | category | flops | bytes accessed | tf_op | source)
XLA Modules:
  0.0 126.0 jit_solution(865727147572221172)
XLA Ops:
  0.6 3.0 %shard_map.77 = (f32[8,392,256]{2,1,0:T(8,128)S(1)}, bf16[16,256,256]{2,1,0:T(8,128)(2,1)S(1)}) custom-call(s32[1]{0:T(128)} %bitcast.me_ref, s32[16,32]{1,0:T(8,128)} %bitcast.4, s32[1,32]{1,0:T(1,128)} %bitcast.7, s32[1,16]{1,0:T(1,128)} %starts_hbm.3, f32[96,1024]{1,0:T(8,128)} %vol_hbm.3, bf16[1,16,256,256]{3,2,1,0:T(8,128)(2,1)} %mats_hbm.1), custom_call_target="tpu_custom_call" | custom-call | tf_op jit(solution)/shard_map/pallas_call | solution.py:114
  3.7 44.6 %all_to_all.20.in_ref = f32[8,392,256]{2,1,0:T(8,128)S(1)} all-to-all(f32[8,392,256]{2,1,0:T(8,128)S(1)} %get-tuple-element.7), channel_id=1, replica_groups={{0,16,32,48,64,80,96,112},{128,144,160,176,192,208,224,240},{256,272,28..., dimensions={0} | all-to-all | bytes 6422528 | tf_op jit(solution)/shard_map/all_to_all | solution.py:31
  48.3 0.0 copy-start.2
  48.3 0.0 copy-start
  48.3 0.9 shard_map.78
  49.1 17.7 %all_to_all.21 = f32[4,104,256]{2,1,0:T(8,128)S(1)} all-to-all(f32[4,104,256]{2,1,0:T(8,128)S(1)} %get-tuple-element.11), channel_id=1, replica_groups={{0,128,256,384},{16,144,272,400},{32,160,288,416},{48,176,304,432},{64,..., dimensions={0} | all-to-all | bytes 851968 | tf_op jit(solution)/shard_map/all_to_all | solution.py:31
  66.9 0.0 copy-done.2
  66.9 0.0 copy-start.1
  66.9 0.8 broadcast_in_dim.2
  67.7 4.8 %all-to-all-start.2 = ((f32[4,96,256]{2,1,0:T(8,128)}), f32[4,96,256]{2,1,0:T(8,128)S(1)}, u32[]{:S(2)}, u32[]{:S(2)}) async-start(f32[4,96,256]{2,1,0:T(8,128)} %broadcast_in_dim.2), calls=%async_computation.2 | async-start | bytes 786432 | tf_op jit(solution)/shard_map/all_to_all | solution.py:31
  72.5 1.9 %collective-permute-start = (f32[1,1024]{1,0:T(1,128)S(1)}, f32[1,1024]{1,0:T(1,128)S(1)}, u32[]{:S(2)}, u32[]{:S(2)}) collective-permute-start(f32[1,1024]{1,0:T(1,128)S(1)} %get-tuple-element.8), channel_id=1, source_target_pairs={{1,0},{2,1},{3,2},{4,3},{5,4},{6,5},{7,6},{8,7},{9,8},{10,9},{11,1... | collective-permute-start | bytes 12296 | tf_op jit(solution)/shard_map/ppermute | solution.py:227
  74.4 2.4 %collective-permute-start.1 = (f32[1,1024]{1,0:T(1,128)S(1)}, f32[1,1024]{1,0:T(1,128)S(1)}, u32[]{:S(2)}, u32[]{:S(2)}) collective-permute-start(f32[1,1024]{1,0:T(1,128)S(1)} %get-tuple-element.9), channel_id=1, source_target_pairs={{0,1},{1,2},{2,3},{3,4},{4,5},{5,6},{6,7},{7,8},{8,9},{9,10},{10,1... | collective-permute-start | bytes 12296 | tf_op jit(solution)/shard_map/ppermute | solution.py:227
  76.8 0.0 collective-permute-done
  76.8 2.5 %collective-permute-done.1 = f32[1,1024]{1,0:T(1,128)S(1)} collective-permute-done((f32[1,1024]{1,0:T(1,128)S(1)}, f32[1,1024]{1,0:T(1,128)S(1)}, u32[]{:S(2)}, u32[]{:S(2)}) %collective-permute-start.1) | collective-permute-done | bytes 4128 | tf_op jit(solution)/shard_map/ppermute | solution.py:227
  79.3 0.0 copy-done
  79.3 0.1 rsqrt_multiply_fusion
  79.5 0.1 fusion.1.after_ref.base_ref
  79.5 2.5 %all-to-all-done.2.column_ref = f32[4,96,256]{2,1,0:T(8,128)S(1)} async-done(((f32[4,96,256]{2,1,0:T(8,128)}), f32[4,96,256]{2,1,0:T(8,128)S(1)}, u32[]{:S(2)}, u32[]{:S(2)}) %all-to-all-start.2) | async-done | bytes 393248 | tf_op jit(solution)/shard_map/all_to_all | solution.py:31
  82.0 0.2 shard_map.79
  82.2 0.0 copy-done.1
  82.3 40.9 %all_to_all.22.got_ref = f32[8,4,96,256]{3,2,1,0:T(8,128)S(1)} all-to-all(f32[8,4,96,256]{3,2,1,0:T(8,128)S(1)} %shard_map.79), channel_id=1, replica_groups={{0,16,32,48,64,80,96,112},{128,144,160,176,192,208,224,240},{256,272,28..., dimensions={0} | all-to-all | bytes 6291456 | tf_op jit(solution)/shard_map/all_to_all | solution.py:31
  123.2 2.9 %shard_map.80 = f32[96,1024]{1,0:T(8,128)} custom-call(s32[1]{0:T(128)} %bitcast.me_ref, s32[16,32]{1,0:T(8,128)} %bitcast.5, s32[1,32]{1,0:T(1,128)} %bitcast.8, s32[1,16]{1,0:T(1,128)} %starts_hbm.3, f32[96,1024]{1,0:T(8,128)S(1)} %fusion.1.after_ref.base_ref, bf16[16,256,256]{2,1,0:T(8,128)(2,1)S(1)} %get-tuple-element.10.mats_ref, ...), custom_call_target="tpu_custom_call" | custom-call | tf_op jit(solution)/shard_map/pallas_call | solution.py:211
  (3 shorter events, 0.1 us)
Async XLA Ops:
  48.3 18.6 %copy-start.2 = (f32[96,256]{1,0:T(8,128)S(1)}, f32[96,256]{1,0:T(8,128)}, u32[]{:S(2)}) copy-start(f32[96,256]{1,0:T(8,128)} %param.7) | copy-start | bytes 294916
  48.3 31.1 %copy-start = (f32[96,1024]{1,0:T(8,128)S(1)}, f32[96,1024]{1,0:T(8,128)}, u32[]{:S(2)}) copy-start(f32[96,1024]{1,0:T(8,128)} %vol_hbm.3) | copy-start | bytes 1179652
  66.9 15.3 %copy-start.1 = (f32[96,256]{1,0:T(8,128)}, f32[96,256]{1,0:T(8,128)S(1)}, u32[]{:S(2)}) copy-start(f32[96,256]{1,0:T(8,128)S(1)} %fusion.2) | copy-start | bytes 294916
  67.7 14.3 %all-to-all-start.2 = ((f32[4,96,256]{2,1,0:T(8,128)}), f32[4,96,256]{2,1,0:T(8,128)S(1)}, u32[]{:S(2)}, u32[]{:S(2)}) async-start(f32[4,96,256]{2,1,0:T(8,128)} %broadcast_in_dim.2), calls=%async_computation.2 | async-start | bytes 786432 | tf_op jit(solution)/shard_map/all_to_all | solution.py:31
  72.5 4.3 %collective-permute-start = (f32[1,1024]{1,0:T(1,128)S(1)}, f32[1,1024]{1,0:T(1,128)S(1)}, u32[]{:S(2)}, u32[]{:S(2)}) collective-permute-start(f32[1,1024]{1,0:T(1,128)S(1)} %get-tuple-element.8), channel_id=1, source_target_pairs={{1,0},{2,1},{3,2},{4,3},{5,4},{6,5},{7,6},{8,7},{9,8},{10,9},{11,1... | collective-permute-start | bytes 12296 | tf_op jit(solution)/shard_map/ppermute | solution.py:227
  74.4 4.9 %collective-permute-start.1 = (f32[1,1024]{1,0:T(1,128)S(1)}, f32[1,1024]{1,0:T(1,128)S(1)}, u32[]{:S(2)}, u32[]{:S(2)}) collective-permute-start(f32[1,1024]{1,0:T(1,128)S(1)} %get-tuple-element.9), channel_id=1, source_target_pairs={{0,1},{1,2},{2,3},{3,4},{4,5},{5,6},{6,7},{7,8},{8,9},{9,10},{10,1... | collective-permute-start | bytes 12296 | tf_op jit(solution)/shard_map/ppermute | solution.py:227

commit v5 on v4

v5 whole, which is shorter than its diff:
```python
import functools

import jax
import jax.numpy as jnp
from jax import lax
from jax.experimental import pallas as pl
from jax.experimental.pallas import tpu as pltpu
from jax.sharding import PartitionSpec as P

relax = 1.0
tv_weight = 0.2
smooth_sq = 0.01

NX, NY = 4, 8
BX, BY = NX // 2, NY // 2
QUAD, SLOTS = 4, BX * BY
ROWS_A = 48
ROWS_B = 24
MATS_AT_ONCE = 4
W = 256
LANES = 128
VMEM_LIMIT = 32 * 1024 * 1024


def device_of(y, x):
    return (y % NY) * NX + x % NX


PARITIES = [(qy, qx) for qy in range(2) for qx in range(2)]
BLOCKS = [(by, bx) for by in range(BY) for bx in range(BX)]
NEAR = [[device_of(2 * by + qy, 2 * bx + qx) for qy, qx in PARITIES] for by, bx in BLOCKS]
FAR = [[device_of(2 * by + qy, 2 * bx + qx) for by, bx in BLOCKS] for qy, qx in PARITIES]
ODD_X = [(device_of(y, x), device_of(y, x + 2 * (x % 2) - 1)) for y in range(NY) for x in range(NX)]
ODD_Y = [(device_of(y, x), device_of(y + 2 * (y % 2) - 1, x)) for y in range(NY) for x in range(NX)]


def swap_x(value):
    return lax.ppermute(value, "xy", ODD_X)


def swap_y(value):
    return lax.ppermute(value, "xy", ODD_Y)


def exchange(value, groups):
    return lax.all_to_all(
        value, "xy", split_axis=0, concat_axis=0, axis_index_groups=groups, tiled=True
    )


def split3(value):
    high = value.astype(jnp.bfloat16)
    rest = value - high.astype(jnp.float32)
    mid = rest.astype(jnp.bfloat16)
    low = (rest - mid.astype(jnp.float32)).astype(jnp.bfloat16)
    return [high, mid, low]


def with_ones(value):
    ones = jnp.ones((16, value.shape[1]), jnp.bfloat16)
    return jnp.concatenate(split3(value) + [ones], axis=0)


def place(owner, me):
    y, x = owner // NX, owner % NX
    my_y, my_x = me // NX, me % NX
    quad = (y % 2) * 2 + x % 2
    slot = (y // 2) * BX + x // 2
    return quad, slot, (x + my_x) % 2, (y + my_y) % 2


def join3(product, rows):
    return product[2 * rows : 3 * rows] + product[rows : 2 * rows] + product[:rows]


def fetch_all(pairs, sems):
    copies = [pltpu.make_async_copy(src, dst, sems.at[i]) for i, (src, dst) in enumerate(pairs)]
    for copy in copies:
        copy.start()
    return copies


def pinned(value, space):
    return pltpu.with_memory_space_constraint(value, space)


ANY = pl.BlockSpec(memory_space=pl.ANY)
SMEM = pl.BlockSpec(memory_space=pltpu.SMEM)
VMEM = pl.BlockSpec(memory_space=pltpu.VMEM)
PARAMS = pltpu.CompilerParams(vmem_limit_bytes=VMEM_LIMIT)


def small_scratch(lists, owners, starts):
    return [pltpu.SMEM(a.shape, jnp.int32) for a in (lists, owners, starts)]


def slot_rows(slot, rows):
    return pl.ds(pl.multiple_of(slot * rows, 8), rows)


def fetch_mats(mats_hbm, mats, sems):
    return fetch_all(
        [
            (mats_hbm.at[0, pl.ds(k, MATS_AT_ONCE)], mats.at[pl.ds(k, MATS_AT_ONCE)])
            for k in range(0, mats.shape[0], MATS_AT_ONCE)
        ],
        sems,
    )


def wait_mats(copies, k):
    if k % MATS_AT_ONCE == 0:
        copies[k // MATS_AT_ONCE].wait()


def mats_scratch(mats, others):
    count = mats.shape[1]
    return [
        pltpu.VMEM(mats.shape[1:], jnp.bfloat16),
        pltpu.SemaphoreType.DMA((others,)),
        pltpu.SemaphoreType.DMA((count // MATS_AT_ONCE,)),
    ]


def project_kernel(
    me_ref, lists_hbm, owners_hbm, starts_hbm, vol_hbm, mats_hbm,
    a_ref, keep1_ref, send1_ref, keep2_ref, send2_ref,
    lists, owners, starts, wide, part1, part2, mats, sems, mat_sems,
):
    rows, cols = vol_hbm.shape
    count = mats.shape[0]
    copies = fetch_all(
        [
            (lists_hbm, lists),
            (owners_hbm, owners),
            (starts_hbm, starts),
            (vol_hbm, wide.at[:, pl.ds(0, cols)]),
        ],
        sems,
    )
    mat_copies = fetch_mats(mats_hbm, mats, mat_sems)
    wide[:, cols:] = jnp.zeros((rows, LANES), jnp.float32)
    for ref in (a_ref, part1, part2):
        ref[...] = jnp.zeros(ref.shape, jnp.float32)
    for copy in copies:
        copy.wait()
    me = me_ref[0]
    for k in range(count):
        start = starts[0, k]
        quad, slot, other_x, other_y = place(owners[0, lists[k, me]], me)
        base = pl.multiple_of((start // LANES) * LANES, LANES)
        window = wide[:, pl.ds(base, W + LANES)]
        window = pltpu.roll(window, (W + LANES) - start % LANES, 1)[:, :W]
        wait_mats(mat_copies, k)
        product = jnp.dot(with_ones(window), mats[k], preferred_element_type=jnp.float32)
        value = join3(product, rows)
        a_ref[quad, slot_rows(slot, ROWS_A), :] = value[:ROWS_A]
        a_ref[quad, pl.ds(SLOTS * ROWS_A + slot, 1), :] = product[3 * rows : 3 * rows + 1]
        b_rows = slot_rows(slot, ROWS_B)
        part1[other_x, other_y, b_rows, :] = value[ROWS_A : ROWS_A + ROWS_B]
        part2[other_y, other_x, b_rows, :] = value[ROWS_A + ROWS_B :]
    keep1_ref[...] = part1[0]
    send1_ref[...] = part1[1]
    keep2_ref[...] = part2[0]
    send2_ref[...] = part2[1]


def project(me, lists, owners, starts, volume, mats):
    rows, cols = volume.shape
    operands = [pinned(a, pltpu.HBM) for a in (lists, owners, starts, volume, mats)]
    half = pltpu.VMEM((2, SLOTS * ROWS_B, W), jnp.float32)
    return pl.pallas_call(
        project_kernel,
        out_shape=[jax.ShapeDtypeStruct((QUAD, SLOTS * ROWS_A + SLOTS, W), jnp.float32)]
        + [half] * 4,
        in_specs=[SMEM] + [ANY] * 5,
        out_specs=[VMEM] * 5,
        scratch_shapes=small_scratch(lists, owners, starts)
        + [pltpu.VMEM((rows, cols + LANES), jnp.float32)]
        + [pltpu.VMEM((2, 2, SLOTS * ROWS_B, W), jnp.float32)] * 2
        + mats_scratch(mats, 4),
        compiler_params=PARAMS,
    )(me, *operands)


def turn_kernel(keep1, came1, keep2, came2, own1, send1, own2, send2):
    own1[...] = keep1[0] + came1[0]
    send1[...] = keep1[1] + came1[1]
    own2[...] = keep2[0] + came2[0]
    send2[...] = keep2[1] + came2[1]


def turn(keep1, came1, keep2, came2):
    return pl.pallas_call(
        turn_kernel,
        out_shape=[pltpu.VMEM((SLOTS * ROWS_B, W), jnp.float32)] * 4,
        in_specs=[VMEM] * 4,
        out_specs=[VMEM] * 4,
        compiler_params=PARAMS,
    )(*(pinned(a, pltpu.VMEM) for a in (keep1, came1, keep2, came2)))


def gather_kernel(a_ref, own1, came1, own2, came2, vol_hbm, out_ref, first_ref, last_ref, ends, sems):
    height = vol_hbm.shape[0]
    copies = fetch_all(
        [
            (vol_hbm.at[pl.ds(0, 8)], ends.at[0]),
            (vol_hbm.at[pl.ds(height - 8, 8)], ends.at[1]),
        ],
        sems,
    )
    total = a_ref[0]
    for i in range(1, QUAD):
        total = total + a_ref[i]
    total1 = own1[...] + came1[...]
    total2 = own2[...] + came2[...]
    for slot in range(SLOTS):
        out_ref[slot, :ROWS_A] = total[slot * ROWS_A : (slot + 1) * ROWS_A]
        b_rows = slice(slot * ROWS_B, (slot + 1) * ROWS_B)
        out_ref[slot, ROWS_A : ROWS_A + ROWS_B] = total1[b_rows]
        out_ref[slot, ROWS_A + ROWS_B : ROWS_A + 2 * ROWS_B] = total2[b_rows]
        at = SLOTS * ROWS_A + slot
        out_ref[slot, ROWS_A + 2 * ROWS_B :] = jnp.broadcast_to(total[at : at + 1], (8, W))
    for copy in copies:
        copy.wait()
    first_ref[...] = ends[0, :1]
    last_ref[...] = ends[1, 7:]


def gather_near(arrived, own1, came1, own2, came2, volume):
    rows, cols = volume.shape
    face = jax.ShapeDtypeStruct((1, cols), jnp.float32)
    return pl.pallas_call(
        gather_kernel,
        out_shape=[pltpu.VMEM((SLOTS, rows + 8, W), jnp.float32), face, face],
        in_specs=[VMEM] * 5 + [ANY],
        out_specs=[VMEM] * 3,
        scratch_shapes=[pltpu.VMEM((2, 8, cols), jnp.float32), pltpu.SemaphoreType.DMA((2,))],
        compiler_params=PARAMS,
    )(arrived, own1, came1, own2, came2, pinned(volume, pltpu.HBM))


def spread_kernel(column_ref, after_ref, a_ref, one_ref, two_ref):
    for slot in range(SLOTS):
        for i in range(QUAD):
            a_ref[i, slot * ROWS_A : (slot + 1) * ROWS_A] = column_ref[slot, :ROWS_A]
        b_rows = slice(slot * ROWS_B, (slot + 1) * ROWS_B)
        one_ref[b_rows] = column_ref[slot, ROWS_A : ROWS_A + ROWS_B]
        two_ref[b_rows] = column_ref[slot, ROWS_A + ROWS_B :]


def spread_near(column, after):
    part = pltpu.VMEM((SLOTS * ROWS_B, W), jnp.float32)
    return pl.pallas_call(
        spread_kernel,
        out_shape=[jax.ShapeDtypeStruct((QUAD, SLOTS * ROWS_A, W), jnp.float32), part, part],
        in_specs=[VMEM, ANY],
        out_specs=[VMEM] * 3,
        compiler_params=PARAMS,
    )(column, after)


def stack_kernel(own1, came1, own2, came2, pair1, pair2):
    pair1[0] = own1[...]
    pair1[1] = came1[...]
    pair2[0] = own2[...]
    pair2[1] = came2[...]


def stack_pairs(own1, came1, own2, came2):
    return pl.pallas_call(
        stack_kernel,
        out_shape=[pltpu.VMEM((2, SLOTS * ROWS_B, W), jnp.float32)] * 2,
        in_specs=[VMEM] * 4,
        out_specs=[VMEM] * 2,
        compiler_params=PARAMS,
    )(*(pinned(a, pltpu.VMEM) for a in (own1, came1, own2, came2)))


def back_kernel(
    me_ref, lists_hbm, owners_hbm, starts_hbm, mats_hbm,
    base_ref, a_ref, own1, came1, own2, came2, out_ref,
    lists, owners, starts, total, part1, part2, mats, sems, mat_sems,
):
    rows, cols = base_ref.shape
    count = mats.shape[0]
    copies = fetch_all([(lists_hbm, lists), (owners_hbm, owners), (starts_hbm, starts)], sems)
    mat_copies = fetch_mats(mats_hbm, mats, mat_sems)
    total[...] = jnp.zeros(total.shape, jnp.float32)
    part1[0] = own1[...]
    part1[1] = came1[...]
    part2[0] = own2[...]
    part2[1] = came2[...]
    for copy in copies:
        copy.wait()
    me = me_ref[0]
    for k in range(count):
        start = starts[0, k]
        quad, slot, other_x, other_y = place(owners[0, lists[k, me]], me)
        base = pl.multiple_of((start // LANES) * LANES, LANES)
        b_rows = slot_rows(slot, ROWS_B)
        needed = jnp.concatenate(
            [
                a_ref[quad, slot_rows(slot, ROWS_A), :],
                part1[other_x, other_y, b_rows, :],
                part2[other_y, other_x, b_rows, :],
            ],
            axis=0,
        )
        wait_mats(mat_copies, k)
        product = lax.dot_general(
            with_ones(needed),
            mats[k],
            (((1,), (1,)), ((), ())),
            preferred_element_type=jnp.float32,
        )
        value = jnp.concatenate([join3(product, rows), product[3 * rows : 3 * rows + 8]], axis=0)
        value = jnp.concatenate([value, jnp.zeros((rows + 8, LANES), jnp.float32)], axis=1)
        total[:, pl.ds(base, W + LANES)] += pltpu.roll(value, start % LANES, 1)
    column = jnp.maximum(total[rows : rows + 1, :cols], 1.0)
    out_ref[...] = base_ref[...] + relax * (total[:rows, :cols] / column)


def back_project(me, lists, owners, starts, base, mats, *parts):
    rows, cols = base.shape
    operands = [pinned(a, pltpu.HBM) for a in (lists, owners, starts, mats)]
    operands += [pinned(a, pltpu.VMEM) for a in (base,) + parts]
    return pl.pallas_call(
        back_kernel,
        out_shape=jax.ShapeDtypeStruct((rows, cols), jnp.float32),
        in_specs=[SMEM] + [ANY] * 4 + [VMEM] * 6,
        out_specs=VMEM,
        scratch_shapes=small_scratch(lists, owners, starts)
        + [pltpu.VMEM((rows + 8, cols + LANES), jnp.float32)]
        + [pltpu.VMEM((2, 2, SLOTS * ROWS_B, W), jnp.float32)] * 2
        + mats_scratch(mats, 3),
        compiler_params=PARAMS,
    )(me, *operands)


def with_faces(volume, first, last):
    count = lax.axis_size("gz")
    up = [(i, i + 1) for i in range(count - 1)]
    down = [(i + 1, i) for i in range(count - 1)]
    return jnp.concatenate(
        [lax.ppermute(last, "gz", up), volume, lax.ppermute(first, "gz", down)], axis=0
    )


def total_variation(padded):
    diffs = padded[1:] - padded[:-1]
    slopes = diffs / jnp.sqrt(diffs * diffs + smooth_sq)
    return slopes[:-1] - slopes[1:]


def per_device(volume, sinogram, ray_mats, offsets, ray_lists, owner_map):
    rows = volume.shape[0]
    me = lax.axis_index("xy").astype(jnp.int32).reshape(1)
    plan = (me, ray_lists.T, owner_map.reshape(1, -1), offsets)
    a, keep1, send1, keep2, send2 = project(*plan, volume, ray_mats)
    own1, send1, own2, send2 = turn(keep1, swap_x(send1), keep2, swap_y(send2))
    a = exchange(a, NEAR)
    outgoing, first, last = gather_near(a, own1, swap_y(send1), own2, swap_x(send2), volume)
    arrived = jnp.sum(exchange(outgoing, FAR), axis=0)
    base = volume - tv_weight * total_variation(with_faces(volume, first, last))
    weighted = (sinogram - arrived[:rows]) / arrived[rows : rows + 1]
    column = exchange(jnp.broadcast_to(weighted[None], (SLOTS, rows, W)), FAR)
    a, own1, own2 = spread_near(column, base)
    pair1, pair2 = stack_pairs(own1, swap_y(own1), own2, swap_x(own2))
    got = (exchange(a, NEAR), pair1, swap_x(pair1), pair2, swap_y(pair2))
    new_volume = back_project(*plan, base, ray_mats, *got)
    return (new_volume, weighted)


def solution(mesh):
    in_specs = (P("gz", "xy"), P("gz", "xy"), P("xy", None, None, None), P("xy", None), P(), P())
    out_specs = (P("gz", "xy"), P("gz", "xy"))
    return jax.shard_map(
        per_device, mesh=mesh, in_specs=in_specs, out_specs=out_specs, check_vma=False
    )
```

time: 126 us -> 133 us (1.056)
  the two profiles are of different devices: /device:TPU:208 before, /device:TPU:1 now
where the time goes in v5:
time: 133 us; the launch traced here: 131 us
  starting transfers between devices  57.5 us (43%)
  waiting for transfers between devices  33.1 us (25%)
  blocking collectives  27.5 us (21%)
  Pallas kernels  10.4 us (8%)
    all_to_all x1, blocking collectives, exchange(): lax.all_to_all(value, 'xy', split_axis=0, concat_axis=0, axis_index_group...  27.5 us
    ppermute x4, starting transfers between devices, swap_y(): return lax.ppermute(value, 'xy', ODD_Y)  20.4 us
    ppermute x4, starting transfers between devices, swap_x(): return lax.ppermute(value, 'xy', ODD_X)  17.9 us
    ppermute x4, waiting for transfers between devices, swap_y(): return lax.ppermute(value, 'xy', ODD_Y)  13.5 us
    all_to_all x3, starting transfers between devices, exchange(): lax.all_to_all(value, 'xy', split_axis=0, concat_axis=0, axis_index_group...  12.3 us
    ppermute x4, waiting for transfers between devices, swap_x(): return lax.ppermute(value, 'xy', ODD_X)  11.7 us
    all_to_all x3, waiting for transfers between devices, exchange(): lax.all_to_all(value, 'xy', split_axis=0, concat_axis=0, axis_index_group...  7.19 us
    pallas_call x1, Pallas kernels, project(): pl.pallas_call(project_kernel, out_shape=[jax.ShapeDtypeStruct((QUAD, SLO...  4.27 us
  transfers between devices with their start and end apart: 13, of which 8 were waited for; matrix products, arithmetic and copies ran while one was open for 0% of the time, Pallas kernels for 0%

profile of v5, /device:TPU:1, one launch (start us, length us, event | category | flops | bytes accessed | tf_op | source)
XLA Modules:
  0.0 130.6 jit_solution(6256774625919886798)
XLA Ops:
  0.6 4.3 %shard_map.77 = (f32[4,392,256]{2,1,0:T(8,128)}, f32[2,192,256]{2,1,0:T(8,128)S(1)}, f32[2,192,256]{2,1,0:T(8,128)S(1)}, f32[2,192,256]{2,1,0:T(8,128)S(1)}, f32[2,192,256]{2,1,0:T(8,128)S(1)}) custom-call(s32[1]{0:T(128)} %bitcast.me_ref, s32[16,32]{1,0:T(8,128)} %bitcast.4, s32[1,32]{1,0:T(1,128)} %bitcast.7, s32[1,16]{1,0:T(1,128)} %starts_hbm.3, ...), custom_call_target="tpu_custom_call" | custom-call | tf_op jit(solution)/shard_map/pallas_call | solution.py:172
  4.9 4.3 %all-to-all-start = ((f32[4,392,256]{2,1,0:T(8,128)}), f32[4,392,256]{2,1,0:T(8,128)S(1)}, u32[]{:S(2)}, u32[]{:S(2)}) async-start(f32[4,392,256]{2,1,0:T(8,128)} %get-tuple-element.19), calls=%async_computation | async-start | bytes 3211264 | tf_op jit(solution)/shard_map/all_to_all | solution.py:46
  9.2 5.0 %collective-permute-start = (f32[2,192,256]{2,1,0:T(8,128)S(1)}, f32[2,192,256]{2,1,0:T(8,128)S(1)}, u32[]{:S(2)}, u32[]{:S(2)}) collective-permute-start(f32[2,192,256]{2,1,0:T(8,128)S(1)} %get-tuple-element.21), channel_id=1, source_target_pairs={{0,48},{16,32},{32,16},{48,0},{64,112},{80,96},{96,80},{112,64},{1... | collective-permute-start | bytes 1179656 | tf_op jit(solution)/shard_map/ppermute | solution.py:38
  14.2 5.9 %collective-permute-start.1 = (f32[2,192,256]{2,1,0:T(8,128)S(1)}, f32[2,192,256]{2,1,0:T(8,128)S(1)}, u32[]{:S(2)}, u32[]{:S(2)}) collective-permute-start(f32[2,192,256]{2,1,0:T(8,128)S(1)} %get-tuple-element.23), channel_id=1, source_target_pairs={{0,448},{16,464},{32,480},{48,496},{64,128},{80,144},{96,160},{112... | collective-permute-start | bytes 1179656 | tf_op jit(solution)/shard_map/ppermute | solution.py:42
  20.1 0.0 collective-permute-done.came1
  20.1 7.3 %collective-permute-done.1.came2 = f32[2,192,256]{2,1,0:T(8,128)S(1)} collective-permute-done((f32[2,192,256]{2,1,0:T(8,128)S(1)}, f32[2,192,256]{2,1,0:T(8,128)S(1)}, u32[]{:S(2)}, u32[]{:S(2)}) %collective-permute-start.1) | collective-permute-done | bytes 393248 | tf_op jit(solution)/shard_map/ppermute | solution.py:42
  27.5 0.1 shard_map.78
  27.6 5.1 %collective-permute-start.2 = (f32[192,256]{1,0:T(8,128)S(1)}, f32[192,256]{1,0:T(8,128)S(1)}, u32[]{:S(2)}, u32[]{:S(2)}) collective-permute-start(f32[192,256]{1,0:T(8,128)S(1)} %get-tuple-element.25), channel_id=1, source_target_pairs={{0,448},{16,464},{32,480},{48,496},{64,128},{80,144},{96,160},{112... | collective-permute-start | bytes 589832 | tf_op jit(solution)/shard_map/ppermute | solution.py:42
  32.7 1.9 %collective-permute-start.3 = (f32[192,256]{1,0:T(8,128)S(1)}, f32[192,256]{1,0:T(8,128)S(1)}, u32[]{:S(2)}, u32[]{:S(2)}) collective-permute-start(f32[192,256]{1,0:T(8,128)S(1)} %get-tuple-element.27), channel_id=1, source_target_pairs={{0,48},{16,32},{32,16},{48,0},{64,112},{80,96},{96,80},{112,64},{1... | collective-permute-start | bytes 589832 | tf_op jit(solution)/shard_map/ppermute | solution.py:38
  34.6 1.1 collective-permute-done.2.came1
  35.7 4.6 %collective-permute-done.3.came2 = f32[192,256]{1,0:T(8,128)S(1)} collective-permute-done((f32[192,256]{1,0:T(8,128)S(1)}, f32[192,256]{1,0:T(8,128)S(1)}, u32[]{:S(2)}, u32[]{:S(2)}) %collective-permute-start.3) | collective-permute-done | bytes 196640 | tf_op jit(solution)/shard_map/ppermute | solution.py:38
  40.3 0.0 all-to-all-done.a_ref
  40.3 0.8 shard_map.79
  41.1 0.0 copy-start.2
  41.1 27.5 %all_to_all.20 = f32[8,104,256]{2,1,0:T(8,128)S(1)} all-to-all(f32[8,104,256]{2,1,0:T(8,128)S(1)} %get-tuple-element.30), channel_id=1, replica_groups={{0,32,128,160,256,288,384,416},{16,48,144,176,272,304,400,432},{64,96,1..., dimensions={0} | all-to-all | bytes 1703936 | tf_op jit(solution)/shard_map/all_to_all | solution.py:46
  68.6 0.1 reduce_sum.9
  68.7 0.0 copy-start
  68.7 0.0 copy-done.2
  68.7 0.0 copy-start.1
  68.7 0.9 broadcast_in_dim.2
  69.7 4.4 %all-to-all-start.2 = ((f32[8,96,256]{2,1,0:T(8,128)}), f32[8,96,256]{2,1,0:T(8,128)S(1)}, u32[]{:S(2)}, u32[]{:S(2)}) async-start(f32[8,96,256]{2,1,0:T(8,128)} %broadcast_in_dim.2), calls=%async_computation.2 | async-start | bytes 1572864 | tf_op jit(solution)/shard_map/all_to_all | solution.py:46
  74.1 3.0 %collective-permute-start.4 = (f32[1,1024]{1,0:T(1,128)S(1)}, f32[1,1024]{1,0:T(1,128)S(1)}, u32[]{:S(2)}, u32[]{:S(2)}) collective-permute-start(f32[1,1024]{1,0:T(1,128)S(1)} %get-tuple-element.28), channel_id=1, source_target_pairs={{1,0},{2,1},{3,2},{4,3},{5,4},{6,5},{7,6},{8,7},{9,8},{10,9},{11,1... | collective-permute-start | bytes 12296 | tf_op jit(solution)/shard_map/ppermute | solution.py:346
  77.1 3.9 %collective-permute-start.5 = (f32[1,1024]{1,0:T(1,128)S(1)}, f32[1,1024]{1,0:T(1,128)S(1)}, u32[]{:S(2)}, u32[]{:S(2)}) collective-permute-start(f32[1,1024]{1,0:T(1,128)S(1)} %get-tuple-element.29), channel_id=1, source_target_pairs={{0,1},{1,2},{2,3},{3,4},{4,5},{5,6},{6,7},{7,8},{8,9},{9,10},{10,1... | collective-permute-start | bytes 12296 | tf_op jit(solution)/shard_map/ppermute | solution.py:346
  81.0 0.0 collective-permute-done.4
  81.0 0.7 collective-permute-done.5
  81.7 0.0 copy-done
  81.7 0.1 rsqrt_multiply_fusion
  81.8 0.0 copy-done.1
  81.9 0.1 fusion.1.after_ref.base_ref
  81.9 7.2 %all-to-all-done.2.column_ref = f32[8,96,256]{2,1,0:T(8,128)S(1)} async-done(((f32[8,96,256]{2,1,0:T(8,128)}), f32[8,96,256]{2,1,0:T(8,128)S(1)}, u32[]{:S(2)}, u32[]{:S(2)}) %all-to-all-start.2) | async-done | bytes 786464 | tf_op jit(solution)/shard_map/all_to_all | solution.py:46
  89.1 1.3 shard_map.80
  90.4 3.6 %all-to-all-start.3 = ((f32[4,384,256]{2,1,0:T(8,128)}), f32[4,384,256]{2,1,0:T(8,128)S(1)}, u32[]{:S(2)}, u32[]{:S(2)}) async-start(f32[4,384,256]{2,1,0:T(8,128)} %get-tuple-element.31), calls=%async_computation.3 | async-start | bytes 3145728 | tf_op jit(solution)/shard_map/all_to_all | solution.py:46
  94.0 7.2 %collective-permute-start.6 = (f32[192,256]{1,0:T(8,128)S(1)}, f32[192,256]{1,0:T(8,128)S(1)}, u32[]{:S(2)}, u32[]{:S(2)}) collective-permute-start(f32[192,256]{1,0:T(8,128)S(1)} %get-tuple-element.32.own1), channel_id=1, source_target_pairs={{0,448},{16,464},{32,480},{48,496},{64,128},{80,144},{96,160},{112... | collective-permute-start | bytes 589832 | tf_op jit(solution)/shard_map/ppermute | solution.py:42
  101.2 6.0 %collective-permute-start.7 = (f32[192,256]{1,0:T(8,128)S(1)}, f32[192,256]{1,0:T(8,128)S(1)}, u32[]{:S(2)}, u32[]{:S(2)}) collective-permute-start(f32[192,256]{1,0:T(8,128)S(1)} %get-tuple-element.33.own2), channel_id=1, source_target_pairs={{0,48},{16,32},{32,16},{48,0},{64,112},{80,96},{96,80},{112,64},{1... | collective-permute-start | bytes 589832 | tf_op jit(solution)/shard_map/ppermute | solution.py:38
  107.2 0.0 collective-permute-done.6.came1
  107.2 3.2 %collective-permute-done.7.came2 = f32[192,256]{1,0:T(8,128)S(1)} collective-permute-done((f32[192,256]{1,0:T(8,128)S(1)}, f32[192,256]{1,0:T(8,128)S(1)}, u32[]{:S(2)}, u32[]{:S(2)}) %collective-permute-start.7) | collective-permute-done | bytes 196640 | tf_op jit(solution)/shard_map/ppermute | solution.py:38
  110.4 0.1 shard_map.81
  110.4 5.0 %collective-permute-start.8 = (f32[2,192,256]{2,1,0:T(8,128)S(1)}, f32[2,192,256]{2,1,0:T(8,128)S(1)}, u32[]{:S(2)}, u32[]{:S(2)}) collective-permute-start(f32[2,192,256]{2,1,0:T(8,128)S(1)} %get-tuple-element.34.own1), channel_id=1, source_target_pairs={{0,48},{16,32},{32,16},{48,0},{64,112},{80,96},{96,80},{112,64},{1... | collective-permute-start | bytes 1179656 | tf_op jit(solution)/shard_map/ppermute | solution.py:38
  115.5 2.2 %collective-permute-start.9 = (f32[2,192,256]{2,1,0:T(8,128)S(1)}, f32[2,192,256]{2,1,0:T(8,128)S(1)}, u32[]{:S(2)}, u32[]{:S(2)}) collective-permute-start(f32[2,192,256]{2,1,0:T(8,128)S(1)} %get-tuple-element.35.own2), channel_id=1, source_target_pairs={{0,448},{16,464},{32,480},{48,496},{64,128},{80,144},{96,160},{112... | collective-permute-start | bytes 1179656 | tf_op jit(solution)/shard_map/ppermute | solution.py:42
  117.7 4.0 %collective-permute-done.8.came1 = f32[2,192,256]{2,1,0:T(8,128)S(1)} collective-permute-done((f32[2,192,256]{2,1,0:T(8,128)S(1)}, f32[2,192,256]{2,1,0:T(8,128)S(1)}, u32[]{:S(2)}, u32[]{:S(2)}) %collective-permute-start.8) | collective-permute-done | bytes 393248 | tf_op jit(solution)/shard_map/ppermute | solution.py:38
  121.7 5.0 %collective-permute-done.9.came2 = f32[2,192,256]{2,1,0:T(8,128)S(1)} collective-permute-done((f32[2,192,256]{2,1,0:T(8,128)S(1)}, f32[2,192,256]{2,1,0:T(8,128)S(1)}, u32[]{:S(2)}, u32[]{:S(2)}) %collective-permute-start.9) | collective-permute-done | bytes 393248 | tf_op jit(solution)/shard_map/ppermute | solution.py:42
  126.7 0.0 all-to-all-done.3.a_ref
  126.7 3.9 %shard_map.82 = f32[96,1024]{1,0:T(8,128)} custom-call(s32[1]{0:T(128)} %bitcast.me_ref, s32[16,32]{1,0:T(8,128)} %bitcast.5, s32[1,32]{1,0:T(1,128)} %bitcast.8, s32[1,16]{1,0:T(1,128)} %starts_hbm.3, bf16[1,16,256,256]{3,2,1,0:T(8,128)(2,1)} %mats_hbm.3, f32[96,1024]{1,0:T(8,128)S(1)} %fusion.1.after_ref.base_ref, ...), custom_call_target="tpu_custom_call" | custom-call | tf_op jit(solution)/shard_map/pallas_call | solution.py:328
  (2 shorter events, 0.0 us)
Async XLA Ops:
  4.9 35.4 %all-to-all-start = ((f32[4,392,256]{2,1,0:T(8,128)}), f32[4,392,256]{2,1,0:T(8,128)S(1)}, u32[]{:S(2)}, u32[]{:S(2)}) async-start(f32[4,392,256]{2,1,0:T(8,128)} %get-tuple-element.19), calls=%async_computation | async-start | bytes 3211264 | tf_op jit(solution)/shard_map/all_to_all | solution.py:46
  9.2 10.9 %collective-permute-start = (f32[2,192,256]{2,1,0:T(8,128)S(1)}, f32[2,192,256]{2,1,0:T(8,128)S(1)}, u32[]{:S(2)}, u32[]{:S(2)}) collective-permute-start(f32[2,192,256]{2,1,0:T(8,128)S(1)} %get-tuple-element.21), channel_id=1, source_target_pairs={{0,48},{16,32},{32,16},{48,0},{64,112},{80,96},{96,80},{112,64},{1... | collective-permute-start | bytes 1179656 | tf_op jit(solution)/shard_map/ppermute | solution.py:38
  14.2 13.3 %collective-permute-start.1 = (f32[2,192,256]{2,1,0:T(8,128)S(1)}, f32[2,192,256]{2,1,0:T(8,128)S(1)}, u32[]{:S(2)}, u32[]{:S(2)}) collective-permute-start(f32[2,192,256]{2,1,0:T(8,128)S(1)} %get-tuple-element.23), channel_id=1, source_target_pairs={{0,448},{16,464},{32,480},{48,496},{64,128},{80,144},{96,160},{112... | collective-permute-start | bytes 1179656 | tf_op jit(solution)/shard_map/ppermute | solution.py:42
  27.6 8.2 %collective-permute-start.2 = (f32[192,256]{1,0:T(8,128)S(1)}, f32[192,256]{1,0:T(8,128)S(1)}, u32[]{:S(2)}, u32[]{:S(2)}) collective-permute-start(f32[192,256]{1,0:T(8,128)S(1)} %get-tuple-element.25), channel_id=1, source_target_pairs={{0,448},{16,464},{32,480},{48,496},{64,128},{80,144},{96,160},{112... | collective-permute-start | bytes 589832 | tf_op jit(solution)/shard_map/ppermute | solution.py:42
  32.7 7.6 %collective-permute-start.3 = (f32[192,256]{1,0:T(8,128)S(1)}, f32[192,256]{1,0:T(8,128)S(1)}, u32[]{:S(2)}, u32[]{:S(2)}) collective-permute-start(f32[192,256]{1,0:T(8,128)S(1)} %get-tuple-element.27), channel_id=1, source_target_pairs={{0,48},{16,32},{32,16},{48,0},{64,112},{80,96},{96,80},{112,64},{1... | collective-permute-start | bytes 589832 | tf_op jit(solution)/shard_map/ppermute | solution.py:38
  41.1 27.6 %copy-start.2 = (f32[96,256]{1,0:T(8,128)S(1)}, f32[96,256]{1,0:T(8,128)}, u32[]{:S(2)}) copy-start(f32[96,256]{1,0:T(8,128)} %param.7) | copy-start | bytes 294916
  68.7 13.1 %copy-start = (f32[96,1024]{1,0:T(8,128)S(1)}, f32[96,1024]{1,0:T(8,128)}, u32[]{:S(2)}) copy-start(f32[96,1024]{1,0:T(8,128)} %vol_hbm.3) | copy-start | bytes 1179652
  68.7 13.1 %copy-start.1 = (f32[96,256]{1,0:T(8,128)}, f32[96,256]{1,0:T(8,128)S(1)}, u32[]{:S(2)}) copy-start(f32[96,256]{1,0:T(8,128)S(1)} %fusion.2) | copy-start | bytes 294916
  69.7 19.4 %all-to-all-start.2 = ((f32[8,96,256]{2,1,0:T(8,128)}), f32[8,96,256]{2,1,0:T(8,128)S(1)}, u32[]{:S(2)}, u32[]{:S(2)}) async-start(f32[8,96,256]{2,1,0:T(8,128)} %broadcast_in_dim.2), calls=%async_computation.2 | async-start | bytes 1572864 | tf_op jit(solution)/shard_map/all_to_all | solution.py:46
  74.1 6.9 %collective-permute-start.4 = (f32[1,1024]{1,0:T(1,128)S(1)}, f32[1,1024]{1,0:T(1,128)S(1)}, u32[]{:S(2)}, u32[]{:S(2)}) collective-permute-start(f32[1,1024]{1,0:T(1,128)S(1)} %get-tuple-element.28), channel_id=1, source_target_pairs={{1,0},{2,1},{3,2},{4,3},{5,4},{6,5},{7,6},{8,7},{9,8},{10,9},{11,1... | collective-permute-start | bytes 12296 | tf_op jit(solution)/shard_map/ppermute | solution.py:346
  77.1 4.6 %collective-permute-start.5 = (f32[1,1024]{1,0:T(1,128)S(1)}, f32[1,1024]{1,0:T(1,128)S(1)}, u32[]{:S(2)}, u32[]{:S(2)}) collective-permute-start(f32[1,1024]{1,0:T(1,128)S(1)} %get-tuple-element.29), channel_id=1, source_target_pairs={{0,1},{1,2},{2,3},{3,4},{4,5},{5,6},{6,7},{7,8},{8,9},{9,10},{10,1... | collective-permute-start | bytes 12296 | tf_op jit(solution)/shard_map/ppermute | solution.py:346
  90.4 36.3 %all-to-all-start.3 = ((f32[4,384,256]{2,1,0:T(8,128)}), f32[4,384,256]{2,1,0:T(8,128)S(1)}, u32[]{:S(2)}, u32[]{:S(2)}) async-start(f32[4,384,256]{2,1,0:T(8,128)} %get-tuple-element.31), calls=%async_computation.3 | async-start | bytes 3145728 | tf_op jit(solution)/shard_map/all_to_all | solution.py:46
  94.0 13.2 %collective-permute-start.6 = (f32[192,256]{1,0:T(8,128)S(1)}, f32[192,256]{1,0:T(8,128)S(1)}, u32[]{:S(2)}, u32[]{:S(2)}) collective-permute-start(f32[192,256]{1,0:T(8,128)S(1)} %get-tuple-element.32.own1), channel_id=1, source_target_pairs={{0,448},{16,464},{32,480},{48,496},{64,128},{80,144},{96,160},{112... | collective-permute-start | bytes 589832 | tf_op jit(solution)/shard_map/ppermute | solution.py:42
  101.2 9.2 %collective-permute-start.7 = (f32[192,256]{1,0:T(8,128)S(1)}, f32[192,256]{1,0:T(8,128)S(1)}, u32[]{:S(2)}, u32[]{:S(2)}) collective-permute-start(f32[192,256]{1,0:T(8,128)S(1)} %get-tuple-element.33.own2), channel_id=1, source_target_pairs={{0,48},{16,32},{32,16},{48,0},{64,112},{80,96},{96,80},{112,64},{1... | collective-permute-start | bytes 589832 | tf_op jit(solution)/shard_map/ppermute | solution.py:38
  110.4 11.2 %collective-permute-start.8 = (f32[2,192,256]{2,1,0:T(8,128)S(1)}, f32[2,192,256]{2,1,0:T(8,128)S(1)}, u32[]{:S(2)}, u32[]{:S(2)}) collective-permute-start(f32[2,192,256]{2,1,0:T(8,128)S(1)} %get-tuple-element.34.own1), channel_id=1, source_target_pairs={{0,48},{16,32},{32,16},{48,0},{64,112},{80,96},{96,80},{112,64},{1... | collective-permute-start | bytes 1179656 | tf_op jit(solution)/shard_map/ppermute | solution.py:38
  115.5 11.2 %collective-permute-start.9 = (f32[2,192,256]{2,1,0:T(8,128)S(1)}, f32[2,192,256]{2,1,0:T(8,128)S(1)}, u32[]{:S(2)}, u32[]{:S(2)}) collective-permute-start(f32[2,192,256]{2,1,0:T(8,128)S(1)} %get-tuple-element.35.own2), channel_id=1, source_target_pairs={{0,448},{16,464},{32,480},{48,496},{64,128},{80,144},{96,160},{112... | collective-permute-start | bytes 1179656 | tf_op jit(solution)/shard_map/ppermute | solution.py:42

commit v6 on v5

--- a/solution.py
+++ b/solution.py
@@ -14,8 +14,8 @@
 NX, NY = 4, 8
 BX, BY = NX // 2, NY // 2
 QUAD, SLOTS = 4, BX * BY
-ROWS_A = 48
-ROWS_B = 24
+ROWS_A = 64
+ROWS_B = 32
 MATS_AT_ONCE = 4
 W = 256
 LANES = 128
@@ -124,8 +124,7 @@
 
 def project_kernel(
     me_ref, lists_hbm, owners_hbm, starts_hbm, vol_hbm, mats_hbm,
-    a_ref, keep1_ref, send1_ref, keep2_ref, send2_ref,
-    lists, owners, starts, wide, part1, part2, mats, sems, mat_sems,
+    a_ref, keep_ref, send_ref, lists, owners, starts, wide, part, mats, sems, mat_sems,
 ):
     rows, cols = vol_hbm.shape
     count = mats.shape[0]
@@ -140,7 +139,7 @@
     )
     mat_copies = fetch_mats(mats_hbm, mats, mat_sems)
     wide[:, cols:] = jnp.zeros((rows, LANES), jnp.float32)
-    for ref in (a_ref, part1, part2):
+    for ref in (a_ref, part):
         ref[...] = jnp.zeros(ref.shape, jnp.float32)
     for copy in copies:
         copy.wait()
@@ -156,13 +155,9 @@
         value = join3(product, rows)
         a_ref[quad, slot_rows(slot, ROWS_A), :] = value[:ROWS_A]
         a_ref[quad, pl.ds(SLOTS * ROWS_A + slot, 1), :] = product[3 * rows : 3 * rows + 1]
-        b_rows = slot_rows(slot, ROWS_B)
-        part1[other_x, other_y, b_rows, :] = value[ROWS_A : ROWS_A + ROWS_B]
-        part2[other_y, other_x, b_rows, :] = value[ROWS_A + ROWS_B :]
-    keep1_ref[...] = part1[0]
-    send1_ref[...] = part1[1]
-    keep2_ref[...] = part2[0]
-    send2_ref[...] = part2[1]
+        part[other_x, other_y, slot_rows(slot, ROWS_B), :] = value[ROWS_A:]
+    keep_ref[...] = part[0]
+    send_ref[...] = part[1]
 
 
 def project(me, lists, owners, starts, volume, mats):
@@ -172,35 +167,33 @@
     return pl.pallas_call(
         project_kernel,
         out_shape=[jax.ShapeDtypeStruct((QUAD, SLOTS * ROWS_A + SLOTS, W), jnp.float32)]
-        + [half] * 4,
+        + [half] * 2,
         in_specs=[SMEM] + [ANY] * 5,
-        out_specs=[VMEM] * 5,
+        out_specs=[VMEM] * 3,
         scratch_shapes=small_scratch(lists, owners, starts)
         + [pltpu.VMEM((rows, cols + LANES), jnp.float32)]
-        + [pltpu.VMEM((2, 2, SLOTS * ROWS_B, W), jnp.float32)] * 2
+        + [pltpu.VMEM((2, 2, SLOTS * ROWS_B, W), jnp.float32)]
         + mats_scratch(mats, 4),
         compiler_params=PARAMS,
     )(me, *operands)
 
 
-def turn_kernel(keep1, came1, keep2, came2, own1, send1, own2, send2):
-    own1[...] = keep1[0] + came1[0]
-    send1[...] = keep1[1] + came1[1]
-    own2[...] = keep2[0] + came2[0]
-    send2[...] = keep2[1] + came2[1]
-
-
-def turn(keep1, came1, keep2, came2):
+def turn_kernel(keep, came, own, send):
+    own[...] = keep[0] + came[0]
+    send[...] = keep[1] + came[1]
+
+
+def turn(keep, came):
     return pl.pallas_call(
         turn_kernel,
-        out_shape=[pltpu.VMEM((SLOTS * ROWS_B, W), jnp.float32)] * 4,
-        in_specs=[VMEM] * 4,
-        out_specs=[VMEM] * 4,
-        compiler_params=PARAMS,
-    )(*(pinned(a, pltpu.VMEM) for a in (keep1, came1, keep2, came2)))
-
-
-def gather_kernel(a_ref, own1, came1, own2, came2, vol_hbm, out_ref, first_ref, last_ref, ends, sems):
+        out_shape=[pltpu.VMEM((SLOTS * ROWS_B, W), jnp.float32)] * 2,
+        in_specs=[VMEM] * 2,
+        out_specs=[VMEM] * 2,
+        compiler_params=PARAMS,
+    )(pinned(keep, pltpu.VMEM), pinned(came, pltpu.VMEM))
+
+
+def gather_kernel(a_ref, own, came, vol_hbm, out_ref, first_ref, last_ref, ends, sems):
     height = vol_hbm.shape[0]
     copies = fetch_all(
         [
@@ -212,85 +205,76 @@
     total = a_ref[0]
     for i in range(1, QUAD):
         total = total + a_ref[i]
-    total1 = own1[...] + came1[...]
-    total2 = own2[...] + came2[...]
+    total_b = own[...] + came[...]
     for slot in range(SLOTS):
         out_ref[slot, :ROWS_A] = total[slot * ROWS_A : (slot + 1) * ROWS_A]
-        b_rows = slice(slot * ROWS_B, (slot + 1) * ROWS_B)
-        out_ref[slot, ROWS_A : ROWS_A + ROWS_B] = total1[b_rows]
-        out_ref[slot, ROWS_A + ROWS_B : ROWS_A + 2 * ROWS_B] = total2[b_rows]
+        rows = ROWS_A + ROWS_B
+        out_ref[slot, ROWS_A:rows] = total_b[slot * ROWS_B : (slot + 1) * ROWS_B]
         at = SLOTS * ROWS_A + slot
-        out_ref[slot, ROWS_A + 2 * ROWS_B :] = jnp.broadcast_to(total[at : at + 1], (8, W))
+        out_ref[slot, rows:] = jnp.broadcast_to(total[at : at + 1], (8, W))
     for copy in copies:
         copy.wait()
     first_ref[...] = ends[0, :1]
     last_ref[...] = ends[1, 7:]
 
 
-def gather_near(arrived, own1, came1, own2, came2, volume):
+def gather_near(arrived, own, came, volume):
     rows, cols = volume.shape
     face = jax.ShapeDtypeStruct((1, cols), jnp.float32)
     return pl.pallas_call(
         gather_kernel,
         out_shape=[pltpu.VMEM((SLOTS, rows + 8, W), jnp.float32), face, face],
-        in_specs=[VMEM] * 5 + [ANY],
+        in_specs=[VMEM] * 3 + [ANY],
         out_specs=[VMEM] * 3,
         scratch_shapes=[pltpu.VMEM((2, 8, cols), jnp.float32), pltpu.SemaphoreType.DMA((2,))],
         compiler_params=PARAMS,
-    )(arrived, own1, came1, own2, came2, pinned(volume, pltpu.HBM))
-
-
-def spread_kernel(column_ref, after_ref, a_ref, one_ref, two_ref):
+    )(arrived, own, came, pinned(volume, pltpu.HBM))
+
+
+def spread_kernel(column_ref, after_ref, a_ref, b_ref):
     for slot in range(SLOTS):
         for i in range(QUAD):
             a_ref[i, slot * ROWS_A : (slot + 1) * ROWS_A] = column_ref[slot, :ROWS_A]
-        b_rows = slice(slot * ROWS_B, (slot + 1) * ROWS_B)
-        one_ref[b_rows] = column_ref[slot, ROWS_A : ROWS_A + ROWS_B]
-        two_ref[b_rows] = column_ref[slot, ROWS_A + ROWS_B :]
+        b_ref[slot * ROWS_B : (slot + 1) * ROWS_B] = column_ref[slot, ROWS_A:]
 
 
 def spread_near(column, after):
     part = pltpu.VMEM((SLOTS * ROWS_B, W), jnp.float32)
     return pl.pallas_call(
         spread_kernel,
-        out_shape=[jax.ShapeDtypeStruct((QUAD, SLOTS * ROWS_A, W), jnp.float32), part, part],
+        out_shape=[jax.ShapeDtypeStruct((QUAD, SLOTS * ROWS_A, W), jnp.float32), part],
         in_specs=[VMEM, ANY],
-        out_specs=[VMEM] * 3,
+        out_specs=[VMEM] * 2,
         compiler_params=PARAMS,
     )(column, after)
 
 
-def stack_kernel(own1, came1, own2, came2, pair1, pair2):
-    pair1[0] = own1[...]
-    pair1[1] = came1[...]
-    pair2[0] = own2[...]
-    pair2[1] = came2[...]
-
-
-def stack_pairs(own1, came1, own2, came2):
+def stack_kernel(own, came, pair):
+    pair[0] = own[...]
+    pair[1] = came[...]
+
+
+def stack_pair(own, came):
     return pl.pallas_call(
         stack_kernel,
-        out_shape=[pltpu.VMEM((2, SLOTS * ROWS_B, W), jnp.float32)] * 2,
-        in_specs=[VMEM] * 4,
-        out_specs=[VMEM] * 2,
-        compiler_params=PARAMS,
-    )(*(pinned(a, pltpu.VMEM) for a in (own1, came1, own2, came2)))
+        out_shape=pltpu.VMEM((2, SLOTS * ROWS_B, W), jnp.float32),
+        in_specs=[VMEM] * 2,
+        out_specs=VMEM,
+        compiler_params=PARAMS,
+    )(pinned(own, pltpu.VMEM), pinned(came, pltpu.VMEM))
 
 
 def back_kernel(
     me_ref, lists_hbm, owners_hbm, starts_hbm, mats_hbm,
-    base_ref, a_ref, own1, came1, own2, came2, out_ref,
-    lists, owners, starts, total, part1, part2, mats, sems, mat_sems,
+    base_ref, a_ref, own, came, out_ref, lists, owners, starts, total, part, mats, sems, mat_sems,
 ):
     rows, cols = base_ref.shape
     count = mats.shape[0]
     copies = fetch_all([(lists_hbm, lists), (owners_hbm, owners), (starts_hbm, starts)], sems)
     mat_copies = fetch_mats(mats_hbm, mats, mat_sems)
     total[...] = jnp.zeros(total.shape, jnp.float32)
-    part1[0] = own1[...]
-    part1[1] = came1[...]
-    part2[0] = own2[...]
-    part2[1] = came2[...]
+    part[0] = own[...]
+    part[1] = came[...]
     for copy in copies:
         copy.wait()
     me = me_ref[0]
@@ -298,12 +282,10 @@
         start = starts[0, k]
         quad, slot, other_x, other_y = place(owners[0, lists[k, me]], me)
         base = pl.multiple_of((start // LANES) * LANES, LANES)
-        b_rows = slot_rows(slot, ROWS_B)
         needed = jnp.concatenate(
             [
                 a_ref[quad, slot_rows(slot, ROWS_A), :],
-                part1[other_x, other_y, b_rows, :],
-                part2[other_y, other_x, b_rows, :],
+                part[other_x, other_y, slot_rows(slot, ROWS_B), :],
             ],
             axis=0,
         )
@@ -328,11 +310,11 @@
     return pl.pallas_call(
         back_kernel,
         out_shape=jax.ShapeDtypeStruct((rows, cols), jnp.float32),
-        in_specs=[SMEM] + [ANY] * 4 + [VMEM] * 6,
+        in_specs=[SMEM] + [ANY] * 4 + [VMEM] * 4,
         out_specs=VMEM,
         scratch_shapes=small_scratch(lists, owners, starts)
         + [pltpu.VMEM((rows + 8, cols + LANES), jnp.float32)]
-        + [pltpu.VMEM((2, 2, SLOTS * ROWS_B, W), jnp.float32)] * 2
+        + [pltpu.VMEM((2, 2, SLOTS * ROWS_B, W), jnp.float32)]
         + mats_scratch(mats, 3),
         compiler_params=PARAMS,
     )(me, *operands)
@@ -357,17 +339,16 @@
     rows = volume.shape[0]
     me = lax.axis_index("xy").astype(jnp.int32).reshape(1)
     plan = (me, ray_lists.T, owner_map.reshape(1, -1), offsets)
-    a, keep1, send1, keep2, send2 = project(*plan, volume, ray_mats)
-    own1, send1, own2, send2 = turn(keep1, swap_x(send1), keep2, swap_y(send2))
-    a = exchange(a, NEAR)
-    outgoing, first, last = gather_near(a, own1, swap_y(send1), own2, swap_x(send2), volume)
+    a, keep, send = project(*plan, volume, ray_mats)
+    own, send = turn(keep, swap_x(send))
+    outgoing, first, last = gather_near(exchange(a, NEAR), own, swap_y(send), volume)
     arrived = jnp.sum(exchange(outgoing, FAR), axis=0)
     base = volume - tv_weight * total_variation(with_faces(volume, first, last))
     weighted = (sinogram - arrived[:rows]) / arrived[rows : rows + 1]
     column = exchange(jnp.broadcast_to(weighted[None], (SLOTS, rows, W)), FAR)
-    a, own1, own2 = spread_near(column, base)
-    pair1, pair2 = stack_pairs(own1, swap_y(own1), own2, swap_x(own2))
-    got = (exchange(a, NEAR), pair1, swap_x(pair1), pair2, swap_y(pair2))
+    a, own = spread_near(column, base)
+    pair = stack_pair(own, swap_y(own))
+    got = (exchange(a, NEAR), pair, swap_x(pair))
     new_volume = back_project(*plan, base, ray_mats, *got)
     return (new_volume, weighted)
 

time: 133 us -> 131 us (0.985)
  local copies, waits for them, and re-layouts: 0.97 us -> 3.65 us
  Pallas kernels: 10.4 us -> 8.12 us
  blocking collectives: 27.5 us -> 25.7 us
    all_to_all x3, starting transfers between devices: 12.3 us -> 25.9 us  [exchange(): lax.all_to_all(value, 'xy', split_axis=0, concat_axis=0, axis_index_group...]
    ppermute x4 -> x2, starting transfers between devices: 17.9 us -> 6.93 us  [swap_x(): return lax.ppermute(value, 'xy', ODD_X)]
    ppermute x4 -> x2, waiting for transfers between devices: 11.7 us -> 21.3 us  [swap_x(): return lax.ppermute(value, 'xy', ODD_X)]
    ppermute x4 -> x2, starting transfers between devices: 20.4 us -> 12.9 us  [swap_y(): return lax.ppermute(value, 'xy', ODD_Y)]
    all_to_all x3, waiting for transfers between devices: 7.19 us -> 0.01 us  [exchange(): lax.all_to_all(value, 'xy', split_axis=0, concat_axis=0, axis_index_group...]
    ppermute x1, starting transfers between devices: 3.01 us -> 8.53 us  [with_faces(): lax.ppermute(first, 'gz', down)]
    ppermute x4 -> x2, waiting for transfers between devices: 13.5 us -> 10.6 us  [swap_y(): return lax.ppermute(value, 'xy', ODD_Y)]
    unnamed x6 -> x10, local copies, waits for them, and re-layouts: 0.02 us -> 2.68 us
  transfers between devices with their start and end apart: 13 -> 9, of which waited for: 8 -> 5; matrix products, arithmetic and copies ran while one was open for 0% -> 0% of each run, Pallas kernels for 0% -> 0%
where the time goes in v6:
time: 131 us; the launch traced here: 129 us
  starting transfers between devices  58.2 us (44%)
  waiting for transfers between devices  32.6 us (25%)
  blocking collectives  25.7 us (20%)
  Pallas kernels  8.12 us (6%)
  local copies, waits for them, and re-layouts  3.65 us (3%)
    all_to_all x3, starting transfers between devices, exchange(): lax.all_to_all(value, 'xy', split_axis=0, concat_axis=0, axis_index_group...  25.9 us
    all_to_all x1, blocking collectives, exchange(): lax.all_to_all(value, 'xy', split_axis=0, concat_axis=0, axis_index_group...  25.7 us
    ppermute x2, waiting for transfers between devices, swap_x(): return lax.ppermute(value, 'xy', ODD_X)  21.3 us
    ppermute x2, starting transfers between devices, swap_y(): return lax.ppermute(value, 'xy', ODD_Y)  12.9 us
    ppermute x2, waiting for transfers between devices, swap_y(): return lax.ppermute(value, 'xy', ODD_Y)  10.6 us
    ppermute x1, starting transfers between devices, with_faces(): lax.ppermute(first, 'gz', down)  8.53 us
    ppermute x2, starting transfers between devices, swap_x(): return lax.ppermute(value, 'xy', ODD_X)  6.93 us
    ppermute x1, starting transfers between devices, with_faces(): lax.ppermute(last, 'gz', up)  3.9 us
  transfers between devices with their start and end apart: 9, of which 5 were waited for; matrix products, arithmetic and copies ran while one was open for 0% of the time, Pallas kernels for 0%

profile of v6, /device:TPU:1, one launch (start us, length us, event | category | flops | bytes accessed | tf_op | source)
XLA Modules:
  0.0 129.3 jit_solution(16168428688506390673)
XLA Ops:
  0.6 3.2 %shard_map.77 = (f32[4,520,256]{2,1,0:T(8,128)S(1)}, f32[2,256,256]{2,1,0:T(8,128)S(1)}, f32[2,256,256]{2,1,0:T(8,128)S(1)}) custom-call(s32[1]{0:T(128)} %bitcast.me_ref, s32[16,32]{1,0:T(8,128)} %bitcast.4, s32[1,32]{1,0:T(1,128)} %bitcast.7, s32[1,16]{1,0:T(1,128)} %starts_hbm.3, f32[96,1024]{1,0:T(8,128)} %vol_hbm.3, bf16[1,16,256,256]{3,2,1,0:T(8,128)(2,1)} %mats_hbm.3), custom_call_target="tpu_custom_call" | custom-call | tf_op jit(solution)/shard_map/pallas_call | solution.py:167
  3.8 0.0 copy-start
  3.8 1.3 %copy-done = f32[4,520,256]{2,1,0:T(8,128)} copy-done((f32[4,520,256]{2,1,0:T(8,128)}, f32[4,520,256]{2,1,0:T(8,128)S(1)}, u32[]{:S(2)}) %copy-start) | copy-done | bytes 2129944
  5.1 4.3 %all-to-all-start = ((f32[4,520,256]{2,1,0:T(8,128)}), f32[4,520,256]{2,1,0:T(8,128)S(1)}, u32[]{:S(2)}, u32[]{:S(2)}) async-start(f32[4,520,256]{2,1,0:T(8,128)} %copy-done), calls=%async_computation | async-start | bytes 4259840 | tf_op jit(solution)/shard_map/all_to_all | solution.py:46
  9.5 5.0 %collective-permute-start = (f32[2,256,256]{2,1,0:T(8,128)S(1)}, f32[2,256,256]{2,1,0:T(8,128)S(1)}, u32[]{:S(2)}, u32[]{:S(2)}) collective-permute-start(f32[2,256,256]{2,1,0:T(8,128)S(1)} %get-tuple-element.14), channel_id=1, source_target_pairs={{0,48},{16,32},{32,16},{48,0},{64,112},{80,96},{96,80},{112,64},{1... | collective-permute-start | bytes 1572872 | tf_op jit(solution)/shard_map/ppermute | solution.py:38
  14.5 8.4 %collective-permute-done.came = f32[2,256,256]{2,1,0:T(8,128)S(1)} collective-permute-done((f32[2,256,256]{2,1,0:T(8,128)S(1)}, f32[2,256,256]{2,1,0:T(8,128)S(1)}, u32[]{:S(2)}, u32[]{:S(2)}) %collective-permute-start) | collective-permute-done | bytes 524320 | tf_op jit(solution)/shard_map/ppermute | solution.py:38
  22.9 0.1 shard_map.78
  22.9 8.6 %collective-permute-start.1 = (f32[256,256]{1,0:T(8,128)S(1)}, f32[256,256]{1,0:T(8,128)S(1)}, u32[]{:S(2)}, u32[]{:S(2)}) collective-permute-start(f32[256,256]{1,0:T(8,128)S(1)} %get-tuple-element.16), channel_id=1, source_target_pairs={{0,448},{16,464},{32,480},{48,496},{64,128},{80,144},{96,160},{112... | collective-permute-start | bytes 786440 | tf_op jit(solution)/shard_map/ppermute | solution.py:42
  31.5 4.8 %collective-permute-done.1.came = f32[256,256]{1,0:T(8,128)S(1)} collective-permute-done((f32[256,256]{1,0:T(8,128)S(1)}, f32[256,256]{1,0:T(8,128)S(1)}, u32[]{:S(2)}, u32[]{:S(2)}) %collective-permute-start.1) | collective-permute-done | bytes 262176 | tf_op jit(solution)/shard_map/ppermute | solution.py:42
  36.4 0.0 all-to-all-done.a_ref
  36.4 0.0 copy-start.4
  36.4 0.8 shard_map.79
  37.2 25.7 %all_to_all.20 = f32[8,104,256]{2,1,0:T(8,128)S(1)} all-to-all(f32[8,104,256]{2,1,0:T(8,128)S(1)} %get-tuple-element.19), channel_id=1, replica_groups={{0,32,128,160,256,288,384,416},{16,48,144,176,272,304,400,432},{64,96,1..., dimensions={0} | all-to-all | bytes 1703936 | tf_op jit(solution)/shard_map/all_to_all | solution.py:46
  62.9 0.0 copy-start.2
  62.9 0.1 reduce_sum.9
  63.0 0.0 copy-done.4
  63.0 0.0 copy-start.3
  63.0 1.0 broadcast_in_dim.2
  64.0 0.0 copy-done.3
  64.0 4.3 %all-to-all-start.2 = ((f32[8,96,256]{2,1,0:T(8,128)}), f32[8,96,256]{2,1,0:T(8,128)S(1)}, u32[]{:S(2)}, u32[]{:S(2)}) async-start(f32[8,96,256]{2,1,0:T(8,128)} %broadcast_in_dim.2), calls=%async_computation.2 | async-start | bytes 1572864 | tf_op jit(solution)/shard_map/all_to_all | solution.py:46
  68.3 8.5 %collective-permute-start.2 = (f32[1,1024]{1,0:T(1,128)S(1)}, f32[1,1024]{1,0:T(1,128)S(1)}, u32[]{:S(2)}, u32[]{:S(2)}) collective-permute-start(f32[1,1024]{1,0:T(1,128)S(1)} %get-tuple-element.17), channel_id=1, source_target_pairs={{1,0},{2,1},{3,2},{4,3},{5,4},{6,5},{7,6},{8,7},{9,8},{10,9},{11,1... | collective-permute-start | bytes 12296 | tf_op jit(solution)/shard_map/ppermute | solution.py:328
  76.8 3.9 %collective-permute-start.3 = (f32[1,1024]{1,0:T(1,128)S(1)}, f32[1,1024]{1,0:T(1,128)S(1)}, u32[]{:S(2)}, u32[]{:S(2)}) collective-permute-start(f32[1,1024]{1,0:T(1,128)S(1)} %get-tuple-element.18), channel_id=1, source_target_pairs={{0,1},{1,2},{2,3},{3,4},{4,5},{5,6},{6,7},{7,8},{8,9},{9,10},{10,1... | collective-permute-start | bytes 12296 | tf_op jit(solution)/shard_map/ppermute | solution.py:328
  80.7 0.0 collective-permute-done.2
  80.7 0.7 collective-permute-done.3
  81.5 0.0 copy-done.2
  81.5 0.1 rsqrt_multiply_fusion
  81.6 0.1 fusion.1.after_ref.base_ref
  81.7 0.0 all-to-all-done.2.column_ref
  81.7 0.2 shard_map.80
  81.8 0.0 copy-start.1
  81.8 1.3 %copy-done.1 = f32[4,512,256]{2,1,0:T(8,128)} copy-done((f32[4,512,256]{2,1,0:T(8,128)}, f32[4,512,256]{2,1,0:T(8,128)S(1)}, u32[]{:S(2)}) %copy-start.1) | copy-done | bytes 2097176
  83.2 17.3 %all-to-all-start.3 = ((f32[4,512,256]{2,1,0:T(8,128)}), f32[4,512,256]{2,1,0:T(8,128)S(1)}, u32[]{:S(2)}, u32[]{:S(2)}) async-start(f32[4,512,256]{2,1,0:T(8,128)} %copy-done.1), calls=%async_computation.3 | async-start | bytes 4194304 | tf_op jit(solution)/shard_map/all_to_all | solution.py:46
  100.5 4.3 %collective-permute-start.4 = (f32[256,256]{1,0:T(8,128)S(1)}, f32[256,256]{1,0:T(8,128)S(1)}, u32[]{:S(2)}, u32[]{:S(2)}) collective-permute-start(f32[256,256]{1,0:T(8,128)S(1)} %get-tuple-element.21.own), channel_id=1, source_target_pairs={{0,448},{16,464},{32,480},{48,496},{64,128},{80,144},{96,160},{112... | collective-permute-start | bytes 786440 | tf_op jit(solution)/shard_map/ppermute | solution.py:42
  104.8 5.8 %collective-permute-done.4.came = f32[256,256]{1,0:T(8,128)S(1)} collective-permute-done((f32[256,256]{1,0:T(8,128)S(1)}, f32[256,256]{1,0:T(8,128)S(1)}, u32[]{:S(2)}, u32[]{:S(2)}) %collective-permute-start.4) | collective-permute-done | bytes 262176 | tf_op jit(solution)/shard_map/ppermute | solution.py:42
  110.6 1.9 %collective-permute-start.5 = (f32[2,256,256]{2,1,0:T(8,128)S(1)}, f32[2,256,256]{2,1,0:T(8,128)S(1)}, u32[]{:S(2)}, u32[]{:S(2)}) collective-permute-start(f32[2,256,256]{2,1,0:T(8,128)S(1)} %shard_map.81.own), channel_id=1, source_target_pairs={{0,48},{16,32},{32,16},{48,0},{64,112},{80,96},{96,80},{112,64},{1... | collective-permute-start | bytes 1572872 | tf_op jit(solution)/shard_map/ppermute | solution.py:38
  112.5 12.9 %collective-permute-done.5.came = f32[2,256,256]{2,1,0:T(8,128)S(1)} collective-permute-done((f32[2,256,256]{2,1,0:T(8,128)S(1)}, f32[2,256,256]{2,1,0:T(8,128)S(1)}, u32[]{:S(2)}, u32[]{:S(2)}) %collective-permute-start.5) | collective-permute-done | bytes 524320 | tf_op jit(solution)/shard_map/ppermute | solution.py:38
  125.4 0.0 all-to-all-done.3.a_ref
  125.4 3.9 %shard_map.82 = f32[96,1024]{1,0:T(8,128)} custom-call(s32[1]{0:T(128)} %bitcast.me_ref, s32[16,32]{1,0:T(8,128)} %bitcast.5, s32[1,32]{1,0:T(1,128)} %bitcast.8, s32[1,16]{1,0:T(1,128)} %starts_hbm.3, bf16[1,16,256,256]{3,2,1,0:T(8,128)(2,1)} %mats_hbm.3, f32[96,1024]{1,0:T(8,128)S(1)} %fusion.1.after_ref.base_ref, ...), custom_call_target="tpu_custom_call" | custom-call | tf_op jit(solution)/shard_map/pallas_call | solution.py:310
  (3 shorter events, 0.1 us)
Async XLA Ops:
  3.8 1.3 %copy-start = (f32[4,520,256]{2,1,0:T(8,128)}, f32[4,520,256]{2,1,0:T(8,128)S(1)}, u32[]{:S(2)}) copy-start(f32[4,520,256]{2,1,0:T(8,128)S(1)} %get-tuple-element.12) | copy-start | bytes 6389764
  5.1 31.2 %all-to-all-start = ((f32[4,520,256]{2,1,0:T(8,128)}), f32[4,520,256]{2,1,0:T(8,128)S(1)}, u32[]{:S(2)}, u32[]{:S(2)}) async-start(f32[4,520,256]{2,1,0:T(8,128)} %copy-done), calls=%async_computation | async-start | bytes 4259840 | tf_op jit(solution)/shard_map/all_to_all | solution.py:46
  9.5 13.4 %collective-permute-start = (f32[2,256,256]{2,1,0:T(8,128)S(1)}, f32[2,256,256]{2,1,0:T(8,128)S(1)}, u32[]{:S(2)}, u32[]{:S(2)}) collective-permute-start(f32[2,256,256]{2,1,0:T(8,128)S(1)} %get-tuple-element.14), channel_id=1, source_target_pairs={{0,48},{16,32},{32,16},{48,0},{64,112},{80,96},{96,80},{112,64},{1... | collective-permute-start | bytes 1572872 | tf_op jit(solution)/shard_map/ppermute | solution.py:38
  22.9 13.4 %collective-permute-start.1 = (f32[256,256]{1,0:T(8,128)S(1)}, f32[256,256]{1,0:T(8,128)S(1)}, u32[]{:S(2)}, u32[]{:S(2)}) collective-permute-start(f32[256,256]{1,0:T(8,128)S(1)} %get-tuple-element.16), channel_id=1, source_target_pairs={{0,448},{16,464},{32,480},{48,496},{64,128},{80,144},{96,160},{112... | collective-permute-start | bytes 786440 | tf_op jit(solution)/shard_map/ppermute | solution.py:42
  36.4 26.6 %copy-start.4 = (f32[96,256]{1,0:T(8,128)S(1)}, f32[96,256]{1,0:T(8,128)}, u32[]{:S(2)}) copy-start(f32[96,256]{1,0:T(8,128)} %param.7) | copy-start | bytes 294916
  62.9 18.6 %copy-start.2 = (f32[96,1024]{1,0:T(8,128)S(1)}, f32[96,1024]{1,0:T(8,128)}, u32[]{:S(2)}) copy-start(f32[96,1024]{1,0:T(8,128)} %vol_hbm.3) | copy-start | bytes 1179652
  63.0 1.0 copy-start.3
  64.0 17.7 %all-to-all-start.2 = ((f32[8,96,256]{2,1,0:T(8,128)}), f32[8,96,256]{2,1,0:T(8,128)S(1)}, u32[]{:S(2)}, u32[]{:S(2)}) async-start(f32[8,96,256]{2,1,0:T(8,128)} %broadcast_in_dim.2), calls=%async_computation.2 | async-start | bytes 1572864 | tf_op jit(solution)/shard_map/all_to_all | solution.py:46
  68.3 12.4 %collective-permute-start.2 = (f32[1,1024]{1,0:T(1,128)S(1)}, f32[1,1024]{1,0:T(1,128)S(1)}, u32[]{:S(2)}, u32[]{:S(2)}) collective-permute-start(f32[1,1024]{1,0:T(1,128)S(1)} %get-tuple-element.17), channel_id=1, source_target_pairs={{1,0},{2,1},{3,2},{4,3},{5,4},{6,5},{7,6},{8,7},{9,8},{10,9},{11,1... | collective-permute-start | bytes 12296 | tf_op jit(solution)/shard_map/ppermute | solution.py:328
  76.8 4.6 %collective-permute-start.3 = (f32[1,1024]{1,0:T(1,128)S(1)}, f32[1,1024]{1,0:T(1,128)S(1)}, u32[]{:S(2)}, u32[]{:S(2)}) collective-permute-start(f32[1,1024]{1,0:T(1,128)S(1)} %get-tuple-element.18), channel_id=1, source_target_pairs={{0,1},{1,2},{2,3},{3,4},{4,5},{5,6},{6,7},{7,8},{8,9},{9,10},{10,1... | collective-permute-start | bytes 12296 | tf_op jit(solution)/shard_map/ppermute | solution.py:328
  81.8 1.3 %copy-start.1 = (f32[4,512,256]{2,1,0:T(8,128)}, f32[4,512,256]{2,1,0:T(8,128)S(1)}, u32[]{:S(2)}) copy-start(f32[4,512,256]{2,1,0:T(8,128)S(1)} %get-tuple-element.20) | copy-start | bytes 6291460
  83.2 42.2 %all-to-all-start.3 = ((f32[4,512,256]{2,1,0:T(8,128)}), f32[4,512,256]{2,1,0:T(8,128)S(1)}, u32[]{:S(2)}, u32[]{:S(2)}) async-start(f32[4,512,256]{2,1,0:T(8,128)} %copy-done.1), calls=%async_computation.3 | async-start | bytes 4194304 | tf_op jit(solution)/shard_map/all_to_all | solution.py:46
  100.5 10.1 %collective-permute-start.4 = (f32[256,256]{1,0:T(8,128)S(1)}, f32[256,256]{1,0:T(8,128)S(1)}, u32[]{:S(2)}, u32[]{:S(2)}) collective-permute-start(f32[256,256]{1,0:T(8,128)S(1)} %get-tuple-element.21.own), channel_id=1, source_target_pairs={{0,448},{16,464},{32,480},{48,496},{64,128},{80,144},{96,160},{112... | collective-permute-start | bytes 786440 | tf_op jit(solution)/shard_map/ppermute | solution.py:42
  110.6 14.8 %collective-permute-start.5 = (f32[2,256,256]{2,1,0:T(8,128)S(1)}, f32[2,256,256]{2,1,0:T(8,128)S(1)}, u32[]{:S(2)}, u32[]{:S(2)}) collective-permute-start(f32[2,256,256]{2,1,0:T(8,128)S(1)} %shard_map.81.own), channel_id=1, source_target_pairs={{0,48},{16,32},{32,16},{48,0},{64,112},{80,96},{96,80},{112,64},{1... | collective-permute-start | bytes 1572872 | tf_op jit(solution)/shard_map/ppermute | solution.py:38

commit v7 on v6

--- a/solution.py
+++ b/solution.py
@@ -14,8 +14,8 @@
 NX, NY = 4, 8
 BX, BY = NX // 2, NY // 2
 QUAD, SLOTS = 4, BX * BY
-ROWS_A = 64
-ROWS_B = 32
+ROWS_A = 48
+ROWS_B = 48
 MATS_AT_ONCE = 4
 W = 256
 LANES = 128
@@ -30,16 +30,23 @@
 BLOCKS = [(by, bx) for by in range(BY) for bx in range(BX)]
 NEAR = [[device_of(2 * by + qy, 2 * bx + qx) for qy, qx in PARITIES] for by, bx in BLOCKS]
 FAR = [[device_of(2 * by + qy, 2 * bx + qx) for by, bx in BLOCKS] for qy, qx in PARITIES]
-ODD_X = [(device_of(y, x), device_of(y, x + 2 * (x % 2) - 1)) for y in range(NY) for x in range(NX)]
-ODD_Y = [(device_of(y, x), device_of(y + 2 * (y % 2) - 1, x)) for y in range(NY) for x in range(NX)]
-
-
-def swap_x(value):
-    return lax.ppermute(value, "xy", ODD_X)
-
-
-def swap_y(value):
-    return lax.ppermute(value, "xy", ODD_Y)
+
+
+def odd_pair(y, x, along_y):
+    if along_y:
+        return device_of(y + 2 * (y % 2) - 1, x)
+    return device_of(y, x + 2 * (x % 2) - 1)
+
+
+def swap(value, turn):
+    slabs = lax.axis_size("gz")
+    moves = [
+        (device_of(y, x) * slabs + z, odd_pair(y, x, (z + turn) % 2) * slabs + z)
+        for y in range(NY)
+        for x in range(NX)
+        for z in range(slabs)
+    ]
+    return lax.ppermute(value, ("xy", "gz"), moves)
 
 
 def exchange(value, groups):
@@ -63,10 +70,11 @@
 
 def place(owner, me):
     y, x = owner // NX, owner % NX
-    my_y, my_x = me // NX, me % NX
+    my_y, my_x, core = me[0] // NX, me[0] % NX, me[1]
+    other_x, other_y = (x + my_x) % 2, (y + my_y) % 2
     quad = (y % 2) * 2 + x % 2
     slot = (y // 2) * BX + x // 2
-    return quad, slot, (x + my_x) % 2, (y + my_y) % 2
+    return quad, slot, other_x + core * (other_y - other_x), other_y + core * (other_x - other_y)
 
 
 def join3(product, rows):
@@ -143,10 +151,10 @@
         ref[...] = jnp.zeros(ref.shape, jnp.float32)
     for copy in copies:
         copy.wait()
-    me = me_ref[0]
+    me = me_ref[0], me_ref[1]
     for k in range(count):
         start = starts[0, k]
-        quad, slot, other_x, other_y = place(owners[0, lists[k, me]], me)
+        quad, slot, across0, across1 = place(owners[0, lists[k, me[0]]], me)
         base = pl.multiple_of((start // LANES) * LANES, LANES)
         window = wide[:, pl.ds(base, W + LANES)]
         window = pltpu.roll(window, (W + LANES) - start % LANES, 1)[:, :W]
@@ -155,7 +163,7 @@
         value = join3(product, rows)
         a_ref[quad, slot_rows(slot, ROWS_A), :] = value[:ROWS_A]
         a_ref[quad, pl.ds(SLOTS * ROWS_A + slot, 1), :] = product[3 * rows : 3 * rows + 1]
-        part[other_x, other_y, slot_rows(slot, ROWS_B), :] = value[ROWS_A:]
+        part[across0, across1, slot_rows(slot, ROWS_B), :] = value[ROWS_A:]
     keep_ref[...] = part[0]
     send_ref[...] = part[1]
 
@@ -277,15 +285,15 @@
     part[1] = came[...]
     for copy in copies:
         copy.wait()
-    me = me_ref[0]
+    me = me_ref[0], me_ref[1]
     for k in range(count):
         start = starts[0, k]
-        quad, slot, other_x, other_y = place(owners[0, lists[k, me]], me)
+        quad, slot, across0, across1 = place(owners[0, lists[k, me[0]]], me)
         base = pl.multiple_of((start // LANES) * LANES, LANES)
         needed = jnp.concatenate(
             [
                 a_ref[quad, slot_rows(slot, ROWS_A), :],
-                part[other_x, other_y, slot_rows(slot, ROWS_B), :],
+                part[across0, across1, slot_rows(slot, ROWS_B), :],
             ],
             axis=0,
         )
@@ -337,18 +345,18 @@
 
 def per_device(volume, sinogram, ray_mats, offsets, ray_lists, owner_map):
     rows = volume.shape[0]
-    me = lax.axis_index("xy").astype(jnp.int32).reshape(1)
+    me = jnp.stack([lax.axis_index("xy"), lax.axis_index("gz") % 2]).astype(jnp.int32)
     plan = (me, ray_lists.T, owner_map.reshape(1, -1), offsets)
     a, keep, send = project(*plan, volume, ray_mats)
-    own, send = turn(keep, swap_x(send))
-    outgoing, first, last = gather_near(exchange(a, NEAR), own, swap_y(send), volume)
+    own, send = turn(keep, swap(send, 0))
+    outgoing, first, last = gather_near(exchange(a, NEAR), own, swap(send, 1), volume)
     arrived = jnp.sum(exchange(outgoing, FAR), axis=0)
     base = volume - tv_weight * total_variation(with_faces(volume, first, last))
     weighted = (sinogram - arrived[:rows]) / arrived[rows : rows + 1]
     column = exchange(jnp.broadcast_to(weighted[None], (SLOTS, rows, W)), FAR)
     a, own = spread_near(column, base)
-    pair = stack_pair(own, swap_y(own))
-    got = (exchange(a, NEAR), pair, swap_x(pair))
+    pair = stack_pair(own, swap(own, 1))
+    got = (exchange(a, NEAR), pair, swap(pair, 0))
     new_volume = back_project(*plan, base, ray_mats, *got)
     return (new_volume, weighted)
 

time: 131 us -> 131 us (level)
  the two profiles are of different devices: /device:TPU:1 before, /device:TPU:136 now
where the time goes in v7:
time: 131 us; the launch traced here: 130 us
  waiting for transfers between devices  56.7 us (43%)
  blocking collectives  30.2 us (23%)
  starting transfers between devices  29.8 us (23%)
  Pallas kernels  11.6 us (9%)
    ppermute x4, waiting for transfers between devices, swap(): return lax.ppermute(value, ('xy', 'gz'), moves)  39.1 us
    all_to_all x1, blocking collectives, exchange(): lax.all_to_all(value, 'xy', split_axis=0, concat_axis=0, axis_index_group...  30.2 us
    all_to_all x3, waiting for transfers between devices, exchange(): lax.all_to_all(value, 'xy', split_axis=0, concat_axis=0, axis_index_group...  15.1 us
    all_to_all x3, starting transfers between devices, exchange(): lax.all_to_all(value, 'xy', split_axis=0, concat_axis=0, axis_index_group...  13.8 us
    ppermute x4, starting transfers between devices, swap(): return lax.ppermute(value, ('xy', 'gz'), moves)  11.7 us
    pallas_call x1, Pallas kernels, project(): pl.pallas_call(project_kernel, out_shape=[jax.ShapeDtypeStruct((QUAD, SLO...  4.86 us
    pallas_call x1, Pallas kernels, back_project(): pl.pallas_call(back_kernel, out_shape=jax.ShapeDtypeStruct((rows, cols),...  4.5 us
  transfers between devices with their start and end apart: 9, of which 6 were waited for; matrix products, arithmetic and copies ran while one was open for 0% of the time, Pallas kernels for 0%

profile of v7, /device:TPU:136, one launch (start us, length us, event | category | flops | bytes accessed | tf_op | source)
XLA Modules:
  0.0 130.5 jit_solution(5556708312926311470)
XLA Ops:
  0.6 0.1 pad_add_fusion.me_ref
  0.7 4.9 %shard_map.77 = (f32[4,392,256]{2,1,0:T(8,128)}, f32[2,384,256]{2,1,0:T(8,128)S(1)}, f32[2,384,256]{2,1,0:T(8,128)S(1)}) custom-call(s32[2]{0:T(128)S(1)} %pad_add_fusion.me_ref, s32[16,32]{1,0:T(8,128)} %bitcast.5, s32[1,32]{1,0:T(1,128)} %bitcast.8, s32[1,16]{1,0:T(1,128)} %starts_hbm.3, f32[96,1024]{1,0:T(8,128)} %vol_hbm.3, ...), custom_call_target="tpu_custom_call" | custom-call | tf_op jit(solution)/shard_map/pallas_call | solution.py:175
  5.6 4.2 %all-to-all-start = ((f32[4,392,256]{2,1,0:T(8,128)}), f32[4,392,256]{2,1,0:T(8,128)S(1)}, u32[]{:S(2)}, u32[]{:S(2)}) async-start(f32[4,392,256]{2,1,0:T(8,128)} %get-tuple-element.12), calls=%async_computation | async-start | bytes 3211264 | tf_op jit(solution)/shard_map/all_to_all | solution.py:53
  9.8 4.7 %collective-permute-start = (f32[2,384,256]{2,1,0:T(8,128)S(1)}, f32[2,384,256]{2,1,0:T(8,128)S(1)}, u32[]{:S(2)}, u32[]{:S(2)}) collective-permute-start(f32[2,384,256]{2,1,0:T(8,128)S(1)} %get-tuple-element.14), channel_id=1, source_target_pairs={{0,48},{1,449},{2,50},{3,451},{4,52},{5,453},{6,54},{7,455},{8,56}... | collective-permute-start | bytes 2359304 | tf_op jit(solution)/shard_map/ppermute | solution.py:49
  14.5 10.4 %collective-permute-done.came = f32[2,384,256]{2,1,0:T(8,128)S(1)} collective-permute-done((f32[2,384,256]{2,1,0:T(8,128)S(1)}, f32[2,384,256]{2,1,0:T(8,128)S(1)}, u32[]{:S(2)}, u32[]{:S(2)}) %collective-permute-start) | collective-permute-done | bytes 786464 | tf_op jit(solution)/shard_map/ppermute | solution.py:49
  24.9 0.1 shard_map.78
  25.0 3.2 %collective-permute-start.1 = (f32[384,256]{1,0:T(8,128)S(1)}, f32[384,256]{1,0:T(8,128)S(1)}, u32[]{:S(2)}, u32[]{:S(2)}) collective-permute-start(f32[384,256]{1,0:T(8,128)S(1)} %get-tuple-element.16), channel_id=1, source_target_pairs={{0,448},{1,49},{2,450},{3,51},{4,452},{5,53},{6,454},{7,55},{8,456... | collective-permute-start | bytes 1179656 | tf_op jit(solution)/shard_map/ppermute | solution.py:49
  28.1 6.5 %collective-permute-done.1.came = f32[384,256]{1,0:T(8,128)S(1)} collective-permute-done((f32[384,256]{1,0:T(8,128)S(1)}, f32[384,256]{1,0:T(8,128)S(1)}, u32[]{:S(2)}, u32[]{:S(2)}) %collective-permute-start.1) | collective-permute-done | bytes 393248 | tf_op jit(solution)/shard_map/ppermute | solution.py:49
  34.7 0.0 all-to-all-done.a_ref
  34.7 0.8 shard_map.79
  35.5 0.0 copy-start.2
  35.5 30.2 %all_to_all.20 = f32[8,104,256]{2,1,0:T(8,128)S(1)} all-to-all(f32[8,104,256]{2,1,0:T(8,128)S(1)} %get-tuple-element.19), channel_id=1, replica_groups={{0,32,128,160,256,288,384,416},{16,48,144,176,272,304,400,432},{64,96,1..., dimensions={0} | all-to-all | bytes 1703936 | tf_op jit(solution)/shard_map/all_to_all | solution.py:53
  65.7 0.1 reduce_sum.9
  65.7 0.0 copy-start
  65.7 0.0 copy-done.2
  65.8 0.0 copy-start.1
  65.8 1.0 broadcast_in_dim.2
  66.8 4.3 %all-to-all-start.2 = ((f32[8,96,256]{2,1,0:T(8,128)}), f32[8,96,256]{2,1,0:T(8,128)S(1)}, u32[]{:S(2)}, u32[]{:S(2)}) async-start(f32[8,96,256]{2,1,0:T(8,128)} %broadcast_in_dim.2), calls=%async_computation.2 | async-start | bytes 1572864 | tf_op jit(solution)/shard_map/all_to_all | solution.py:53
  71.1 1.9 %collective-permute-start.2 = (f32[1,1024]{1,0:T(1,128)S(1)}, f32[1,1024]{1,0:T(1,128)S(1)}, u32[]{:S(2)}, u32[]{:S(2)}) collective-permute-start(f32[1,1024]{1,0:T(1,128)S(1)} %get-tuple-element.17), channel_id=1, source_target_pairs={{1,0},{2,1},{3,2},{4,3},{5,4},{6,5},{7,6},{8,7},{9,8},{10,9},{11,1... | collective-permute-start | bytes 12296 | tf_op jit(solution)/shard_map/ppermute | solution.py:336
  73.0 2.4 %collective-permute-start.3 = (f32[1,1024]{1,0:T(1,128)S(1)}, f32[1,1024]{1,0:T(1,128)S(1)}, u32[]{:S(2)}, u32[]{:S(2)}) collective-permute-start(f32[1,1024]{1,0:T(1,128)S(1)} %get-tuple-element.18), channel_id=1, source_target_pairs={{0,1},{1,2},{2,3},{3,4},{4,5},{5,6},{6,7},{7,8},{8,9},{9,10},{10,1... | collective-permute-start | bytes 12296 | tf_op jit(solution)/shard_map/ppermute | solution.py:336
  75.4 0.0 collective-permute-done.2
  75.4 2.5 %collective-permute-done.3 = f32[1,1024]{1,0:T(1,128)S(1)} collective-permute-done((f32[1,1024]{1,0:T(1,128)S(1)}, f32[1,1024]{1,0:T(1,128)S(1)}, u32[]{:S(2)}, u32[]{:S(2)}) %collective-permute-start.3) | collective-permute-done | bytes 4128 | tf_op jit(solution)/shard_map/ppermute | solution.py:336
  77.9 0.0 copy-done
  77.9 0.1 rsqrt_multiply_fusion
  78.0 0.0 copy-done.1
  78.1 0.1 fusion.1.after_ref.base_ref
  78.1 15.1 %all-to-all-done.2.column_ref = f32[8,96,256]{2,1,0:T(8,128)S(1)} async-done(((f32[8,96,256]{2,1,0:T(8,128)}), f32[8,96,256]{2,1,0:T(8,128)S(1)}, u32[]{:S(2)}, u32[]{:S(2)}) %all-to-all-start.2) | async-done | bytes 786464 | tf_op jit(solution)/shard_map/all_to_all | solution.py:53
  93.2 1.3 shard_map.80
  94.5 5.3 %all-to-all-start.3 = ((f32[4,384,256]{2,1,0:T(8,128)}), f32[4,384,256]{2,1,0:T(8,128)S(1)}, u32[]{:S(2)}, u32[]{:S(2)}) async-start(f32[4,384,256]{2,1,0:T(8,128)} %get-tuple-element.20), calls=%async_computation.3 | async-start | bytes 3145728 | tf_op jit(solution)/shard_map/all_to_all | solution.py:53
  99.8 1.9 %collective-permute-start.4 = (f32[384,256]{1,0:T(8,128)S(1)}, f32[384,256]{1,0:T(8,128)S(1)}, u32[]{:S(2)}, u32[]{:S(2)}) collective-permute-start(f32[384,256]{1,0:T(8,128)S(1)} %get-tuple-element.21.own), channel_id=1, source_target_pairs={{0,448},{1,49},{2,450},{3,51},{4,452},{5,53},{6,454},{7,55},{8,456... | collective-permute-start | bytes 1179656 | tf_op jit(solution)/shard_map/ppermute | solution.py:49
  101.7 9.1 %collective-permute-done.4.came = f32[384,256]{1,0:T(8,128)S(1)} collective-permute-done((f32[384,256]{1,0:T(8,128)S(1)}, f32[384,256]{1,0:T(8,128)S(1)}, u32[]{:S(2)}, u32[]{:S(2)}) %collective-permute-start.4) | collective-permute-done | bytes 393248 | tf_op jit(solution)/shard_map/ppermute | solution.py:49
  110.8 0.1 shard_map.81.own
  110.9 1.9 %collective-permute-start.5 = (f32[2,384,256]{2,1,0:T(8,128)S(1)}, f32[2,384,256]{2,1,0:T(8,128)S(1)}, u32[]{:S(2)}, u32[]{:S(2)}) collective-permute-start(f32[2,384,256]{2,1,0:T(8,128)S(1)} %shard_map.81.own), channel_id=1, source_target_pairs={{0,48},{1,449},{2,50},{3,451},{4,52},{5,453},{6,54},{7,455},{8,56}... | collective-permute-start | bytes 2359304 | tf_op jit(solution)/shard_map/ppermute | solution.py:49
  112.8 13.2 %collective-permute-done.5.came = f32[2,384,256]{2,1,0:T(8,128)S(1)} collective-permute-done((f32[2,384,256]{2,1,0:T(8,128)S(1)}, f32[2,384,256]{2,1,0:T(8,128)S(1)}, u32[]{:S(2)}, u32[]{:S(2)}) %collective-permute-start.5) | collective-permute-done | bytes 786464 | tf_op jit(solution)/shard_map/ppermute | solution.py:49
  126.0 0.0 all-to-all-done.3.a_ref
  126.0 4.5 %shard_map.82 = f32[96,1024]{1,0:T(8,128)} custom-call(s32[2]{0:T(128)S(1)} %pad_add_fusion.me_ref, s32[16,32]{1,0:T(8,128)} %bitcast.6, s32[1,32]{1,0:T(1,128)} %bitcast.9, s32[1,16]{1,0:T(1,128)} %starts_hbm.3, bf16[1,16,256,256]{3,2,1,0:T(8,128)(2,1)} %mats_hbm.3, f32[96,1024]{1,0:T(8,128)S(1)} %fusion.1.after_ref.base_ref, ...), custom_call_target="tpu_custom_call" | custom-call | tf_op jit(solution)/shard_map/pallas_call | solution.py:318
  (2 shorter events, 0.0 us)
Async XLA Ops:
  5.6 29.1 %all-to-all-start = ((f32[4,392,256]{2,1,0:T(8,128)}), f32[4,392,256]{2,1,0:T(8,128)S(1)}, u32[]{:S(2)}, u32[]{:S(2)}) async-start(f32[4,392,256]{2,1,0:T(8,128)} %get-tuple-element.12), calls=%async_computation | async-start | bytes 3211264 | tf_op jit(solution)/shard_map/all_to_all | solution.py:53
  9.8 15.1 %collective-permute-start = (f32[2,384,256]{2,1,0:T(8,128)S(1)}, f32[2,384,256]{2,1,0:T(8,128)S(1)}, u32[]{:S(2)}, u32[]{:S(2)}) collective-permute-start(f32[2,384,256]{2,1,0:T(8,128)S(1)} %get-tuple-element.14), channel_id=1, source_target_pairs={{0,48},{1,449},{2,50},{3,451},{4,52},{5,453},{6,54},{7,455},{8,56}... | collective-permute-start | bytes 2359304 | tf_op jit(solution)/shard_map/ppermute | solution.py:49
  25.0 9.7 %collective-permute-start.1 = (f32[384,256]{1,0:T(8,128)S(1)}, f32[384,256]{1,0:T(8,128)S(1)}, u32[]{:S(2)}, u32[]{:S(2)}) collective-permute-start(f32[384,256]{1,0:T(8,128)S(1)} %get-tuple-element.16), channel_id=1, source_target_pairs={{0,448},{1,49},{2,450},{3,51},{4,452},{5,53},{6,454},{7,55},{8,456... | collective-permute-start | bytes 1179656 | tf_op jit(solution)/shard_map/ppermute | solution.py:49
  35.5 30.3 %copy-start.2 = (f32[96,256]{1,0:T(8,128)S(1)}, f32[96,256]{1,0:T(8,128)}, u32[]{:S(2)}) copy-start(f32[96,256]{1,0:T(8,128)} %param.7) | copy-start | bytes 294916
  65.7 12.2 %copy-start = (f32[96,1024]{1,0:T(8,128)S(1)}, f32[96,1024]{1,0:T(8,128)}, u32[]{:S(2)}) copy-start(f32[96,1024]{1,0:T(8,128)} %vol_hbm.3) | copy-start | bytes 1179652
  65.8 12.3 %copy-start.1 = (f32[96,256]{1,0:T(8,128)}, f32[96,256]{1,0:T(8,128)S(1)}, u32[]{:S(2)}) copy-start(f32[96,256]{1,0:T(8,128)S(1)} %fusion.2) | copy-start | bytes 294916
  66.8 26.5 %all-to-all-start.2 = ((f32[8,96,256]{2,1,0:T(8,128)}), f32[8,96,256]{2,1,0:T(8,128)S(1)}, u32[]{:S(2)}, u32[]{:S(2)}) async-start(f32[8,96,256]{2,1,0:T(8,128)} %broadcast_in_dim.2), calls=%async_computation.2 | async-start | bytes 1572864 | tf_op jit(solution)/shard_map/all_to_all | solution.py:53
  71.1 4.3 %collective-permute-start.2 = (f32[1,1024]{1,0:T(1,128)S(1)}, f32[1,1024]{1,0:T(1,128)S(1)}, u32[]{:S(2)}, u32[]{:S(2)}) collective-permute-start(f32[1,1024]{1,0:T(1,128)S(1)} %get-tuple-element.17), channel_id=1, source_target_pairs={{1,0},{2,1},{3,2},{4,3},{5,4},{6,5},{7,6},{8,7},{9,8},{10,9},{11,1... | collective-permute-start | bytes 12296 | tf_op jit(solution)/shard_map/ppermute | solution.py:336
  73.0 4.9 %collective-permute-start.3 = (f32[1,1024]{1,0:T(1,128)S(1)}, f32[1,1024]{1,0:T(1,128)S(1)}, u32[]{:S(2)}, u32[]{:S(2)}) collective-permute-start(f32[1,1024]{1,0:T(1,128)S(1)} %get-tuple-element.18), channel_id=1, source_target_pairs={{0,1},{1,2},{2,3},{3,4},{4,5},{5,6},{6,7},{7,8},{8,9},{9,10},{10,1... | collective-permute-start | bytes 12296 | tf_op jit(solution)/shard_map/ppermute | solution.py:336
  94.5 31.4 %all-to-all-start.3 = ((f32[4,384,256]{2,1,0:T(8,128)}), f32[4,384,256]{2,1,0:T(8,128)S(1)}, u32[]{:S(2)}, u32[]{:S(2)}) async-start(f32[4,384,256]{2,1,0:T(8,128)} %get-tuple-element.20), calls=%async_computation.3 | async-start | bytes 3145728 | tf_op jit(solution)/shard_map/all_to_all | solution.py:53
  99.8 11.0 %collective-permute-start.4 = (f32[384,256]{1,0:T(8,128)S(1)}, f32[384,256]{1,0:T(8,128)S(1)}, u32[]{:S(2)}, u32[]{:S(2)}) collective-permute-start(f32[384,256]{1,0:T(8,128)S(1)} %get-tuple-element.21.own), channel_id=1, source_target_pairs={{0,448},{1,49},{2,450},{3,51},{4,452},{5,53},{6,454},{7,55},{8,456... | collective-permute-start | bytes 1179656 | tf_op jit(solution)/shard_map/ppermute | solution.py:49
  110.9 15.1 %collective-permute-start.5 = (f32[2,384,256]{2,1,0:T(8,128)S(1)}, f32[2,384,256]{2,1,0:T(8,128)S(1)}, u32[]{:S(2)}, u32[]{:S(2)}) collective-permute-start(f32[2,384,256]{2,1,0:T(8,128)S(1)} %shard_map.81.own), channel_id=1, source_target_pairs={{0,48},{1,449},{2,50},{3,451},{4,52},{5,453},{6,54},{7,455},{8,56}... | collective-permute-start | bytes 2359304 | tf_op jit(solution)/shard_map/ppermute | solution.py:49

commit v8 on v4

--- a/solution.py
+++ b/solution.py
@@ -12,24 +12,37 @@
 smooth_sq = 0.01
 
 NX, NY = 4, 8
-PAIRS = NY // 2
-NEAR_SIZE = 2 * NX
+BX, BY = NX // 2, NY // 2
+QUAD, SLOTS = 4, BX * BY
 W = 256
 LANES = 128
 VMEM_LIMIT = 32 * 1024 * 1024
 
 
-def device_of(pair, odd, x):
-    return (2 * pair + odd) * NX + x
-
-
-NEAR = [[device_of(p, q, x) for q in range(2) for x in range(NX)] for p in range(PAIRS)]
-FAR = [[device_of(p, q, x) for p in range(PAIRS)] for q in range(2) for x in range(NX)]
-
-
-def exchange(value, groups):
+def device_of(y, x):
+    return (y % NY) * NX + x % NX
+
+
+PLACES = [(qy, qx) for qy in range(2) for qx in range(2)]
+BLOCKS = [(by, bx) for by in range(BY) for bx in range(BX)]
+
+
+def exchange(value, near):
+    slabs = lax.axis_size("gz")
+
+    def member(slab, block, place):
+        core = slab % 2
+        y, x = 2 * block[0] + place[0] + core, 2 * block[1] + place[1] + core
+        return device_of(y, x) * slabs + slab
+
+    groups = []
+    for slab in range(slabs):
+        if near:
+            groups += [[member(slab, block, place) for place in PLACES] for block in BLOCKS]
+        else:
+            groups += [[member(slab, block, place) for block in BLOCKS] for place in PLACES]
     return lax.all_to_all(
-        value, "xy", split_axis=0, concat_axis=0, axis_index_groups=groups, tiled=True
+        value, ("xy", "gz"), split_axis=0, concat_axis=0, axis_index_groups=groups, tiled=True
     )
 
 
@@ -46,9 +59,9 @@
     return jnp.concatenate(split3(value) + [ones], axis=0)
 
 
-def near_far(owner):
-    y, x = owner // NX, owner % NX
-    return (y % 2) * NX + x, y // 2
+def near_far(owner, core):
+    y, x = (owner // NX + NY - core) % NY, (owner % NX + NX - core) % NX
+    return (y % 2) * 2 + x % 2, (y // 2) * BX + x // 2
 
 
 def join3(product, rows):
@@ -96,16 +109,16 @@
     out_ref[...] = jnp.zeros(out_ref.shape, jnp.float32)
     for copy in copies:
         copy.wait()
-    me = me_ref[0]
+    me, core = me_ref[0], me_ref[1]
     for k in range(count):
         start = starts[0, k]
-        near, far = near_far(owners[0, lists[k, me]])
+        near, far = near_far(owners[0, lists[k, me]], core)
         base = pl.multiple_of((start // LANES) * LANES, LANES)
         window = wide[:, pl.ds(base, W + LANES)]
         window = pltpu.roll(window, (W + LANES) - start % LANES, 1)[:, :W]
         product = jnp.dot(with_ones(window), mats_ref[k], preferred_element_type=jnp.float32)
         out_ref[near, pl.ds(pl.multiple_of(far * rows, 8), rows), :] = join3(product, rows)
-        out_ref[near, pl.ds(PAIRS * rows + far, 1), :] = product[3 * rows : 3 * rows + 1]
+        out_ref[near, pl.ds(SLOTS * rows + far, 1), :] = product[3 * rows : 3 * rows + 1]
 
 
 def project(me, lists, owners, starts, volume, mats):
@@ -114,7 +127,7 @@
     return pl.pallas_call(
         project_kernel,
         out_shape=[
-            pltpu.VMEM((NEAR_SIZE, PAIRS * rows + 8, W), jnp.float32),
+            pltpu.VMEM((QUAD, SLOTS * rows + 8, W), jnp.float32),
             pltpu.VMEM(mats.shape[1:], jnp.bfloat16),
         ],
         in_specs=[SMEM] + [ANY] * 5,
@@ -135,12 +148,12 @@
         sems,
     )
     total = in_ref[0]
-    for i in range(1, NEAR_SIZE):
+    for i in range(1, QUAD):
         total = total + in_ref[i]
-    for far in range(PAIRS):
+    for far in range(SLOTS):
         out_ref[far, :rows] = total[far * rows : (far + 1) * rows]
         out_ref[far, rows:] = jnp.broadcast_to(
-            total[PAIRS * rows + far : PAIRS * rows + far + 1], (8, W)
+            total[SLOTS * rows + far : SLOTS * rows + far + 1], (8, W)
         )
     for copy in copies:
         copy.wait()
@@ -153,7 +166,7 @@
     face = jax.ShapeDtypeStruct((1, cols), jnp.float32)
     return pl.pallas_call(
         functools.partial(gather_kernel, rows),
-        out_shape=[jax.ShapeDtypeStruct((PAIRS, rows + 8, W), jnp.float32), face, face],
+        out_shape=[jax.ShapeDtypeStruct((SLOTS, rows + 8, W), jnp.float32), face, face],
         in_specs=[VMEM, ANY],
         out_specs=[VMEM] * 3,
         scratch_shapes=[pltpu.VMEM((2, 8, cols), jnp.float32), pltpu.SemaphoreType.DMA((2,))],
@@ -162,14 +175,14 @@
 
 
 def spread_kernel(column_ref, after_ref, out_ref):
-    for i in range(NEAR_SIZE):
+    for i in range(QUAD):
         out_ref[i] = column_ref[...]
 
 
 def spread_near(column, after):
     return pl.pallas_call(
         spread_kernel,
-        out_shape=pltpu.VMEM((NEAR_SIZE,) + column.shape, jnp.float32),
+        out_shape=pltpu.VMEM((QUAD,) + column.shape, jnp.float32),
         in_specs=[VMEM, ANY],
         out_specs=VMEM,
         compiler_params=PARAMS,
@@ -186,10 +199,10 @@
     total[...] = jnp.zeros(total.shape, jnp.float32)
     for copy in copies:
         copy.wait()
-    me = me_ref[0]
+    me, core = me_ref[0], me_ref[1]
     for k in range(count):
         start = starts[0, k]
-        near, far = near_far(owners[0, lists[k, me]])
+        near, far = near_far(owners[0, lists[k, me]], core)
         base = pl.multiple_of((start // LANES) * LANES, LANES)
         product = lax.dot_general(
             with_ones(got_ref[near, far]),
@@ -236,15 +249,15 @@
 
 def per_device(volume, sinogram, ray_mats, offsets, ray_lists, owner_map):
     rows = volume.shape[0]
-    me = lax.axis_index("xy").astype(jnp.int32).reshape(1)
+    me = jnp.stack([lax.axis_index("xy"), lax.axis_index("gz") % 2]).astype(jnp.int32)
     plan = (me, ray_lists.T, owner_map.reshape(1, -1), offsets)
     outgoing, mats = project(*plan, volume, ray_mats)
-    outgoing, first, last = gather_near(exchange(outgoing, NEAR), volume)
-    arrived = jnp.sum(exchange(outgoing, FAR), axis=0)
+    outgoing, first, last = gather_near(exchange(outgoing, True), volume)
+    arrived = jnp.sum(exchange(outgoing, False), axis=0)
     base = volume - tv_weight * total_variation(with_faces(volume, first, last))
     weighted = (sinogram - arrived[:rows]) / arrived[rows : rows + 1]
-    column = exchange(jnp.broadcast_to(weighted[None], (PAIRS, rows, W)), FAR)
-    got = exchange(spread_near(column, base), NEAR)
+    column = exchange(jnp.broadcast_to(weighted[None], (SLOTS, rows, W)), False)
+    got = exchange(spread_near(column, base), True)
     new_volume = back_project(*plan, base, mats, got)
     return (new_volume, weighted)
 

time: 126 us -> 120 us (0.952)
  the two profiles are of different devices: /device:TPU:208 before, /device:TPU:1 now
where the time goes in v8:
time: 120 us
  blocking collectives  81.2 us (68%)
  starting transfers between devices  13.5 us (11%)
  waiting for transfers between devices  12.9 us (11%)
  Pallas kernels  7.99 us (7%)
  other arithmetic  2.22 us (2%)
    all_to_all x3, blocking collectives, exchange(): lax.all_to_all(value, ('xy', 'gz'), split_axis=0, concat_axis=0, axis_ind...  81.2 us
    all_to_all x1, waiting for transfers between devices, exchange(): lax.all_to_all(value, ('xy', 'gz'), split_axis=0, concat_axis=0, axis_ind...  12.1 us
    all_to_all x1, starting transfers between devices, exchange(): lax.all_to_all(value, ('xy', 'gz'), split_axis=0, concat_axis=0, axis_ind...  7.68 us
    ppermute x1, starting transfers between devices, with_faces(): lax.ppermute(last, 'gz', up)  3.91 us
    pallas_call x1, Pallas kernels, project(): pl.pallas_call(project_kernel, out_shape=[pltpu.VMEM((QUAD, SLOTS * rows...  3.59 us
    pallas_call x1, Pallas kernels, back_project(): pl.pallas_call(back_kernel, out_shape=jax.ShapeDtypeStruct((rows, cols),...  3.41 us
  transfers between devices with their start and end apart: 3, of which 2 were waited for; matrix products, arithmetic and copies ran while one was open for 1% of the time, Pallas kernels for 0%

profile of v8, /device:TPU:1, one launch (start us, length us, event | category | flops | bytes accessed | tf_op | source)
XLA Modules:
  0.0 119.5 jit_solution(17603786143834356131)
XLA Ops:
  0.6 0.1 pad_add_fusion.me_ref
  0.7 3.6 %shard_map.77 = (f32[4,776,256]{2,1,0:T(8,128)S(1)}, bf16[16,256,256]{2,1,0:T(8,128)(2,1)S(1)}) custom-call(s32[2]{0:T(128)S(1)} %pad_add_fusion.me_ref, s32[16,32]{1,0:T(8,128)} %bitcast.5, s32[1,32]{1,0:T(1,128)} %bitcast.8, s32[1,16]{1,0:T(1,128)} %starts_hbm.3, f32[96,1024]{1,0:T(8,128)} %vol_hbm.3, bf16[1,16,256,256]{3,2,1,0:T(8,128)(2,1)} %mats_hbm.1), custom_call_target="tpu_custom_call" | custom-call | tf_op jit(solution)/shard_map/pallas_call | solution.py:127
  4.3 27.3 %all_to_all.20.in_ref = f32[4,776,256]{2,1,0:T(8,128)S(1)} all-to-all(f32[4,776,256]{2,1,0:T(8,128)S(1)} %get-tuple-element.7), channel_id=1, replica_groups={{0,16,64,80},{32,48,96,112},{128,144,192,208},{160,176,224,240},{256,27..., dimensions={0} | all-to-all | bytes 6356992 | tf_op jit(solution)/shard_map/all_to_all | solution.py:44
  31.6 0.8 shard_map.78
  32.4 0.0 copy-start
  32.5 29.1 %all_to_all.21 = f32[8,104,256]{2,1,0:T(8,128)S(1)} all-to-all(f32[8,104,256]{2,1,0:T(8,128)S(1)} %get-tuple-element.11), channel_id=1, replica_groups={{0,32,128,160,256,288,384,416},{16,48,144,176,272,304,400,432},{64,96,1..., dimensions={0} | all-to-all | bytes 1703936 | tf_op jit(solution)/shard_map/all_to_all | solution.py:44
  61.6 0.1 reduce_sum.9
  61.7 0.9 fusion.2
  62.6 0.0 copy-start.1
  62.6 1.0 broadcast_in_dim.2
  63.6 0.0 copy-done.1
  63.6 7.7 %all-to-all-start.2 = ((f32[8,96,256]{2,1,0:T(8,128)}), f32[8,96,256]{2,1,0:T(8,128)S(1)}, u32[]{:S(2)}, u32[]{:S(2)}) async-start(f32[8,96,256]{2,1,0:T(8,128)} %broadcast_in_dim.2), calls=%async_computation.2 | async-start | bytes 1572864 | tf_op jit(solution)/shard_map/all_to_all | solution.py:44
  71.2 1.9 %collective-permute-start = (f32[1,1024]{1,0:T(1,128)S(1)}, f32[1,1024]{1,0:T(1,128)S(1)}, u32[]{:S(2)}, u32[]{:S(2)}) collective-permute-start(f32[1,1024]{1,0:T(1,128)S(1)} %get-tuple-element.8), channel_id=1, source_target_pairs={{1,0},{2,1},{3,2},{4,3},{5,4},{6,5},{7,6},{8,7},{9,8},{10,9},{11,1... | collective-permute-start | bytes 12296 | tf_op jit(solution)/shard_map/ppermute | solution.py:240
  73.2 3.9 %collective-permute-start.1 = (f32[1,1024]{1,0:T(1,128)S(1)}, f32[1,1024]{1,0:T(1,128)S(1)}, u32[]{:S(2)}, u32[]{:S(2)}) collective-permute-start(f32[1,1024]{1,0:T(1,128)S(1)} %get-tuple-element.9), channel_id=1, source_target_pairs={{0,1},{1,2},{2,3},{3,4},{4,5},{5,6},{6,7},{7,8},{8,9},{9,10},{10,1... | collective-permute-start | bytes 12296 | tf_op jit(solution)/shard_map/ppermute | solution.py:240
  77.1 0.0 collective-permute-done
  77.1 0.7 collective-permute-done.1
  77.8 0.0 copy-done
  77.8 0.1 rsqrt_multiply_fusion
  77.9 1.1 fusion.1.after_ref.base_ref
  79.0 12.1 %all-to-all-done.2.column_ref = f32[8,96,256]{2,1,0:T(8,128)S(1)} async-done(((f32[8,96,256]{2,1,0:T(8,128)}), f32[8,96,256]{2,1,0:T(8,128)S(1)}, u32[]{:S(2)}, u32[]{:S(2)}) %all-to-all-start.2) | async-done | bytes 786464 | tf_op jit(solution)/shard_map/all_to_all | solution.py:44
  91.1 0.2 shard_map.79
  91.3 24.8 %all_to_all.22.got_ref = f32[4,8,96,256]{3,2,1,0:T(8,128)S(1)} all-to-all(f32[4,8,96,256]{3,2,1,0:T(8,128)S(1)} %shard_map.79), channel_id=1, replica_groups={{0,16,64,80},{32,48,96,112},{128,144,192,208},{160,176,224,240},{256,27..., dimensions={0} | all-to-all | bytes 6291456 | tf_op jit(solution)/shard_map/all_to_all | solution.py:44
  116.1 3.4 %shard_map.80 = f32[96,1024]{1,0:T(8,128)} custom-call(s32[2]{0:T(128)S(1)} %pad_add_fusion.me_ref, s32[16,32]{1,0:T(8,128)} %bitcast.6, s32[1,32]{1,0:T(1,128)} %bitcast.9, s32[1,16]{1,0:T(1,128)} %starts_hbm.3, f32[96,1024]{1,0:T(8,128)S(1)} %fusion.1.after_ref.base_ref, bf16[16,256,256]{2,1,0:T(8,128)(2,1)S(1)} %get-tuple-element.10.mats_ref, ...), custom_call_target="tpu_custom_call" | custom-call | tf_op jit(solution)/shard_map/pallas_call | solution.py:224
  (1 shorter events, 0.0 us)
Async XLA Ops:
  32.4 45.4 %copy-start = (f32[96,1024]{1,0:T(8,128)S(1)}, f32[96,1024]{1,0:T(8,128)}, u32[]{:S(2)}) copy-start(f32[96,1024]{1,0:T(8,128)} %vol_hbm.3) | copy-start | bytes 1179652
  62.6 1.0 copy-start.1
  63.6 27.6 %all-to-all-start.2 = ((f32[8,96,256]{2,1,0:T(8,128)}), f32[8,96,256]{2,1,0:T(8,128)S(1)}, u32[]{:S(2)}, u32[]{:S(2)}) async-start(f32[8,96,256]{2,1,0:T(8,128)} %broadcast_in_dim.2), calls=%async_computation.2 | async-start | bytes 1572864 | tf_op jit(solution)/shard_map/all_to_all | solution.py:44
  71.2 5.9 %collective-permute-start = (f32[1,1024]{1,0:T(1,128)S(1)}, f32[1,1024]{1,0:T(1,128)S(1)}, u32[]{:S(2)}, u32[]{:S(2)}) collective-permute-start(f32[1,1024]{1,0:T(1,128)S(1)} %get-tuple-element.8), channel_id=1, source_target_pairs={{1,0},{2,1},{3,2},{4,3},{5,4},{6,5},{7,6},{8,7},{9,8},{10,9},{11,1... | collective-permute-start | bytes 12296 | tf_op jit(solution)/shard_map/ppermute | solution.py:240
  73.2 4.6 %collective-permute-start.1 = (f32[1,1024]{1,0:T(1,128)S(1)}, f32[1,1024]{1,0:T(1,128)S(1)}, u32[]{:S(2)}, u32[]{:S(2)}) collective-permute-start(f32[1,1024]{1,0:T(1,128)S(1)} %get-tuple-element.9), channel_id=1, source_target_pairs={{0,1},{1,2},{2,3},{3,4},{4,5},{5,6},{6,7},{7,8},{8,9},{9,10},{10,1... | collective-permute-start | bytes 12296 | tf_op jit(solution)/shard_map/ppermute | solution.py:240

commit v9 on v8

--- a/solution.py
+++ b/solution.py
@@ -13,7 +13,7 @@
 
 NX, NY = 4, 8
 BX, BY = NX // 2, NY // 2
-QUAD, SLOTS = 4, BX * BY
+QUAD, SLOTS, FAR = 4, 8, 2
 W = 256
 LANES = 128
 VMEM_LIMIT = 32 * 1024 * 1024
@@ -27,23 +27,25 @@
 BLOCKS = [(by, bx) for by in range(BY) for bx in range(BX)]
 
 
-def exchange(value, near):
+def exchange(value, level):
     slabs = lax.axis_size("gz")
 
     def member(slab, block, place):
-        core = slab % 2
-        y, x = 2 * block[0] + place[0] + core, 2 * block[1] + place[1] + core
+        shift = slab % 2 + level - 1
+        y, x = 2 * block[0] + place[0] + shift, 2 * block[1] + place[1] + shift
         return device_of(y, x) * slabs + slab
 
-    groups = []
-    for slab in range(slabs):
-        if near:
-            groups += [[member(slab, block, place) for place in PLACES] for block in BLOCKS]
-        else:
-            groups += [[member(slab, block, place) for block in BLOCKS] for place in PLACES]
+    groups = [
+        [member(slab, block, place) for place in PLACES] for slab in range(slabs) for block in BLOCKS
+    ]
     return lax.all_to_all(
         value, ("xy", "gz"), split_axis=0, concat_axis=0, axis_index_groups=groups, tiled=True
     )
+
+
+def swap_far(value):
+    moves = [(device_of(y, x), device_of(y + BY, x)) for y in range(NY) for x in range(NX)]
+    return lax.ppermute(value, "xy", moves)
 
 
 def split3(value):
@@ -59,9 +61,16 @@
     return jnp.concatenate(split3(value) + [ones], axis=0)
 
 
-def near_far(owner, core):
-    y, x = (owner // NX + NY - core) % NY, (owner % NX + NX - core) % NX
-    return (y % 2) * 2 + x % 2, (y // 2) * BX + x // 2
+def shifted(device, core):
+    return (device // NX + NY - core) % NY, (device % NX + NX - core) % NX
+
+
+def near_far(owner, me, core):
+    (y, x), (my_y, my_x) = shifted(owner, core), shifted(me, core)
+    near_y = ((y + 1) // 2 + my_y // 2) % 2
+    near_x = ((x + 1) // 2 + my_x // 2) % 2
+    place = (y + 1) % 2 * 2 + (x + 1) % 2
+    return near_y * 2 + near_x, place * FAR + y // BY
 
 
 def join3(product, rows):
@@ -90,8 +99,8 @@
 
 
 def project_kernel(
-    me_ref, lists_hbm, owners_hbm, starts_hbm, vol_hbm, mats_hbm, out_ref, mats_ref,
-    lists, owners, starts, wide, sems,
+    me_ref, lists_hbm, owners_hbm, starts_hbm, vol_hbm, mats_hbm,
+    out_ref, mats_ref, first_ref, last_ref, lists, owners, starts, wide, sems,
 ):
     rows, cols = vol_hbm.shape
     count = mats_ref.shape[0]
@@ -109,10 +118,12 @@
     out_ref[...] = jnp.zeros(out_ref.shape, jnp.float32)
     for copy in copies:
         copy.wait()
+    first_ref[...] = wide[:1, :cols]
+    last_ref[...] = wide[rows - 1 :, :cols]
     me, core = me_ref[0], me_ref[1]
     for k in range(count):
         start = starts[0, k]
-        near, far = near_far(owners[0, lists[k, me]], core)
+        near, far = near_far(owners[0, lists[k, me]], me, core)
         base = pl.multiple_of((start // LANES) * LANES, LANES)
         window = wide[:, pl.ds(base, W + LANES)]
         window = pltpu.roll(window, (W + LANES) - start % LANES, 1)[:, :W]
@@ -129,59 +140,92 @@
         out_shape=[
             pltpu.VMEM((QUAD, SLOTS * rows + 8, W), jnp.float32),
             pltpu.VMEM(mats.shape[1:], jnp.bfloat16),
+            pltpu.VMEM((1, cols), jnp.float32),
+            pltpu.VMEM((1, cols), jnp.float32),
         ],
         in_specs=[SMEM] + [ANY] * 5,
-        out_specs=[VMEM, VMEM],
+        out_specs=[VMEM] * 4,
         scratch_shapes=small_scratch(lists, owners, starts)
         + [pltpu.VMEM((rows, cols + LANES), jnp.float32), pltpu.SemaphoreType.DMA((5,))],
         compiler_params=PARAMS,
     )(me, *operands)
 
 
-def gather_kernel(rows, in_ref, vol_hbm, out_ref, first_ref, last_ref, ends, sems):
-    height = vol_hbm.shape[0]
-    copies = fetch_all(
-        [
-            (vol_hbm.at[pl.ds(0, 8)], ends.at[0]),
-            (vol_hbm.at[pl.ds(height - 8, 8)], ends.at[1]),
-        ],
-        sems,
-    )
-    total = in_ref[0]
-    for i in range(1, QUAD):
-        total = total + in_ref[i]
-    for far in range(SLOTS):
-        out_ref[far, :rows] = total[far * rows : (far + 1) * rows]
-        out_ref[far, rows:] = jnp.broadcast_to(
-            total[SLOTS * rows + far : SLOTS * rows + far + 1], (8, W)
-        )
-    for copy in copies:
-        copy.wait()
-    first_ref[...] = ends[0, :1]
-    last_ref[...] = ends[1, 7:]
-
-
-def gather_near(arrived, volume):
-    rows, cols = volume.shape
-    face = jax.ShapeDtypeStruct((1, cols), jnp.float32)
-    return pl.pallas_call(
-        functools.partial(gather_kernel, rows),
-        out_shape=[jax.ShapeDtypeStruct((SLOTS, rows + 8, W), jnp.float32), face, face],
-        in_specs=[VMEM, ANY],
+def sum_quad(ref):
+    return ref[0] + ref[1] + ref[2] + ref[3]
+
+
+def gather_near_kernel(rows, in_ref, first_in, last_in, out_ref, first_ref, last_ref):
+    total = sum_quad(in_ref)
+    for place in range(QUAD):
+        at = place * FAR
+        out_ref[place, : FAR * rows] = total[at * rows : (at + FAR) * rows]
+        sums = total[SLOTS * rows + at : SLOTS * rows + at + FAR]
+        out_ref[place, FAR * rows : FAR * rows + FAR] = sums
+        out_ref[place, FAR * rows + FAR :] = jnp.zeros((8 - FAR, W), jnp.float32)
+    first_ref[...] = first_in[...]
+    last_ref[...] = last_in[...]
+
+
+def gather_near(arrived, first, last):
+    rows = (arrived.shape[1] - 8) // SLOTS
+    face = jax.ShapeDtypeStruct(first.shape, jnp.float32)
+    return pl.pallas_call(
+        functools.partial(gather_near_kernel, rows),
+        out_shape=[pltpu.VMEM((QUAD, FAR * rows + 8, W), jnp.float32), face, face],
+        in_specs=[VMEM] * 3,
         out_specs=[VMEM] * 3,
-        scratch_shapes=[pltpu.VMEM((2, 8, cols), jnp.float32), pltpu.SemaphoreType.DMA((2,))],
-        compiler_params=PARAMS,
-    )(pinned(arrived, pltpu.VMEM), pinned(volume, pltpu.HBM))
-
-
-def spread_kernel(column_ref, after_ref, out_ref):
-    for i in range(QUAD):
-        out_ref[i] = column_ref[...]
+        compiler_params=PARAMS,
+    )(*(pinned(a, pltpu.VMEM) for a in (arrived, first, last)))
+
+
+def gather_far_kernel(rows, me_ref, in_ref, keep_ref, send_ref, total):
+    half = shifted(me_ref[0], me_ref[1])[0] // BY
+    total[...] = sum_quad(in_ref)
+    for ref, side in ((keep_ref, half), (send_ref, 1 - half)):
+        ref[:rows] = total[pl.ds(pl.multiple_of(side * rows, 8), rows), :]
+        ref[rows:] = jnp.broadcast_to(total[pl.ds(FAR * rows + side, 1), :], (8, W))
+
+
+def gather_far(me, arrived):
+    rows = (arrived.shape[1] - 8) // FAR
+    return pl.pallas_call(
+        functools.partial(gather_far_kernel, rows),
+        out_shape=[pltpu.VMEM((rows + 8, W), jnp.float32)] * 2,
+        in_specs=[SMEM, VMEM],
+        out_specs=[VMEM] * 2,
+        scratch_shapes=[pltpu.VMEM(arrived.shape[1:], jnp.float32)],
+        compiler_params=PARAMS,
+    )(me, pinned(arrived, pltpu.VMEM))
+
+
+def spread_far_kernel(me_ref, own_ref, came_ref, out_ref):
+    half = shifted(me_ref[0], me_ref[1])[0] // BY
+    rows = own_ref.shape[0]
+    for place in range(QUAD):
+        out_ref[place, pl.ds(pl.multiple_of(half * rows, 8), rows), :] = own_ref[...]
+        out_ref[place, pl.ds(pl.multiple_of((1 - half) * rows, 8), rows), :] = came_ref[...]
+
+
+def spread_far(me, own, came):
+    rows = own.shape[0]
+    return pl.pallas_call(
+        spread_far_kernel,
+        out_shape=jax.ShapeDtypeStruct((QUAD, FAR * rows, W), jnp.float32),
+        in_specs=[SMEM, VMEM, VMEM],
+        out_specs=VMEM,
+        compiler_params=PARAMS,
+    )(me, own, came)
+
+
+def spread_near_kernel(column_ref, after_ref, out_ref):
+    for place in range(QUAD):
+        out_ref[place] = column_ref[...]
 
 
 def spread_near(column, after):
     return pl.pallas_call(
-        spread_kernel,
+        spread_near_kernel,
         out_shape=pltpu.VMEM((QUAD,) + column.shape, jnp.float32),
         in_specs=[VMEM, ANY],
         out_specs=VMEM,
@@ -202,7 +246,7 @@
     me, core = me_ref[0], me_ref[1]
     for k in range(count):
         start = starts[0, k]
-        near, far = near_far(owners[0, lists[k, me]], core)
+        near, far = near_far(owners[0, lists[k, me]], me, core)
         base = pl.multiple_of((start // LANES) * LANES, LANES)
         product = lax.dot_general(
             with_ones(got_ref[near, far]),
@@ -249,15 +293,19 @@
 
 def per_device(volume, sinogram, ray_mats, offsets, ray_lists, owner_map):
     rows = volume.shape[0]
-    me = jnp.stack([lax.axis_index("xy"), lax.axis_index("gz") % 2]).astype(jnp.int32)
+    core = lax.axis_index("gz") % 2
+    device = lax.axis_index("xy")
+    me = jnp.stack([device, core]).astype(jnp.int32)
     plan = (me, ray_lists.T, owner_map.reshape(1, -1), offsets)
-    outgoing, mats = project(*plan, volume, ray_mats)
-    outgoing, first, last = gather_near(exchange(outgoing, True), volume)
-    arrived = jnp.sum(exchange(outgoing, False), axis=0)
+    outgoing, mats, first, last = project(*plan, volume, ray_mats)
+    outgoing, first, last = gather_near(exchange(outgoing, 1), first, last)
+    keep, send = gather_far(me, exchange(outgoing, 2))
+    total = keep + swap_far(send)
     base = volume - tv_weight * total_variation(with_faces(volume, first, last))
-    weighted = (sinogram - arrived[:rows]) / arrived[rows : rows + 1]
-    column = exchange(jnp.broadcast_to(weighted[None], (SLOTS, rows, W)), False)
-    got = exchange(spread_near(column, base), True)
+    weighted = (sinogram - total[:rows]) / total[rows : rows + 1]
+    column = exchange(spread_far(me, weighted, swap_far(weighted)), 2)
+    column = column.reshape(SLOTS, rows, W)
+    got = exchange(spread_near(column, base), 1)
     new_volume = back_project(*plan, base, mats, got)
     return (new_volume, weighted)
 

time: 120 us -> 115 us (0.958)
  blocking collectives: 81.2 us -> 61.8 us
  starting transfers between devices: 13.5 us -> 32.7 us
  waiting for transfers between devices: 12.9 us -> 8.07 us
  Pallas kernels: 7.99 us -> 9.68 us
    all_to_all x3, blocking collectives: 81.2 us -> 61.8 us  [exchange(): lax.all_to_all(value, ('xy', 'gz'), split_axis=0, concat_axis=0, axis_ind...]
    ppermute x1, starting transfers between devices: 1.93 us -> 15.6 us  [with_faces(): lax.ppermute(first, 'gz', down)]
    all_to_all x1, waiting for transfers between devices: 12.1 us -> 0.01 us  [exchange(): lax.all_to_all(value, ('xy', 'gz'), split_axis=0, concat_axis=0, axis_ind...]
    ppermute x0 -> x2, starting transfers between devices: none -> 11.7 us  [swap_far(): return lax.ppermute(value, 'xy', moves)]
    ppermute x0 -> x2, waiting for transfers between devices: none -> 6.94 us  [swap_far(): return lax.ppermute(value, 'xy', moves)]
    all_to_all x1, starting transfers between devices: 7.68 us -> 3.49 us  [exchange(): lax.all_to_all(value, ('xy', 'gz'), split_axis=0, concat_axis=0, axis_ind...]
    ppermute x1, starting transfers between devices: 3.91 us -> 1.92 us  [with_faces(): lax.ppermute(last, 'gz', up)]
    pallas_call x2 -> x4, Pallas kernels: 1 us -> 2.45 us  [the longest x1 1.5 us: spread_far(): pl.pallas_call(spread_far_kernel, out_shape=jax.ShapeDtypeStruct((QUAD, F...]
  transfers between devices with their start and end apart: 3 -> 5, of which waited for: 2 -> 3; matrix products, arithmetic and copies ran while one was open for 1% -> 1% of each run, Pallas kernels for 0% -> 0%
where the time goes in v9:
time: 115 us; the launch traced here: 114 us
  blocking collectives  61.8 us (54%)
  starting transfers between devices  32.7 us (28%)
  Pallas kernels  9.68 us (8%)
  waiting for transfers between devices  8.07 us (7%)
  other arithmetic  1.31 us (1%)
    all_to_all x3, blocking collectives, exchange(): lax.all_to_all(value, ('xy', 'gz'), split_axis=0, concat_axis=0, axis_ind...  61.8 us
    ppermute x1, starting transfers between devices, with_faces(): lax.ppermute(first, 'gz', down)  15.6 us
    ppermute x2, starting transfers between devices, swap_far(): return lax.ppermute(value, 'xy', moves)  11.7 us
    ppermute x2, waiting for transfers between devices, swap_far(): return lax.ppermute(value, 'xy', moves)  6.94 us
    pallas_call x1, Pallas kernels, project(): pl.pallas_call(project_kernel, out_shape=[pltpu.VMEM((QUAD, SLOTS * rows...  3.71 us
    pallas_call x1, Pallas kernels, back_project(): pl.pallas_call(back_kernel, out_shape=jax.ShapeDtypeStruct((rows, cols),...  3.52 us
    all_to_all x1, starting transfers between devices, exchange(): lax.all_to_all(value, ('xy', 'gz'), split_axis=0, concat_axis=0, axis_ind...  3.49 us
  transfers between devices with their start and end apart: 5, of which 3 were waited for; matrix products, arithmetic and copies ran while one was open for 1% of the time, Pallas kernels for 0%

profile of v9, /device:TPU:1, one launch (start us, length us, event | category | flops | bytes accessed | tf_op | source)
XLA Modules:
  0.0 114.3 jit_solution(16035432874384693393)
XLA Ops:
  0.6 0.1 pad_add_fusion.me_ref
  0.7 3.7 %shard_map.77 = (f32[4,776,256]{2,1,0:T(8,128)S(1)}, bf16[16,256,256]{2,1,0:T(8,128)(2,1)S(1)}, f32[1,1024]{1,0:T(1,128)S(1)}, f32[1,1024]{1,0:T(1,128)S(1)}) custom-call(s32[2]{0:T(128)S(1)} %pad_add_fusion.me_ref, s32[16,32]{1,0:T(8,128)} %bitcast.7, s32[1,32]{1,0:T(1,128)} %bitcast.10, s32[1,16]{1,0:T(1,128)} %starts_hbm.3, f32[96,1024]{1,0:T(8,128)} %vol_hbm.1, ...), custom_call_target="tpu_custom_call" | custom-call | tf_op jit(solution)/shard_map/pallas_call | solution.py:138
  4.4 27.3 %all_to_all.20.in_ref = f32[4,776,256]{2,1,0:T(8,128)S(1)} all-to-all(f32[4,776,256]{2,1,0:T(8,128)S(1)} %get-tuple-element.11), channel_id=1, replica_groups={{0,16,64,80},{32,48,96,112},{128,144,192,208},{160,176,224,240},{256,27..., dimensions={0} | all-to-all | bytes 6356992 | tf_op jit(solution)/shard_map/all_to_all | solution.py:41
  31.7 0.0 copy-start.2
  31.7 0.1 shard_map.78
  31.9 0.0 copy-start.1
  31.9 10.3 %all_to_all.21.in_ref = f32[4,200,256]{2,1,0:T(8,128)S(1)} all-to-all(f32[4,200,256]{2,1,0:T(8,128)S(1)} %get-tuple-element.17), channel_id=1, replica_groups={{80,96,144,160},{112,64,176,128},{208,224,272,288},{240,192,304,256},{3..., dimensions={0} | all-to-all | bytes 1638400 | tf_op jit(solution)/shard_map/all_to_all | solution.py:41
  42.2 0.6 shard_map.79
  42.8 5.8 %collective-permute-start.2 = (f32[104,256]{1,0:T(8,128)S(1)}, f32[104,256]{1,0:T(8,128)S(1)}, u32[]{:S(2)}, u32[]{:S(2)}) collective-permute-start(f32[104,256]{1,0:T(8,128)S(1)} %get-tuple-element.19), channel_id=1, source_target_pairs={{0,256},{16,272},{32,288},{48,304},{64,320},{80,336},{96,352},{112... | collective-permute-start | bytes 319496 | tf_op jit(solution)/shard_map/ppermute | solution.py:48
  48.7 3.5 %collective-permute-done.2 = f32[104,256]{1,0:T(8,128)S(1)} collective-permute-done((f32[104,256]{1,0:T(8,128)S(1)}, f32[104,256]{1,0:T(8,128)S(1)}, u32[]{:S(2)}, u32[]{:S(2)}) %collective-permute-start.2) | collective-permute-done | bytes 106528 | tf_op jit(solution)/shard_map/ppermute | solution.py:48
  52.2 0.0 copy-done.2
  52.3 0.0 copy-start
  52.3 5.9 %collective-permute-start.3 = (f32[96,256]{1,0:T(8,128)S(1)}, f32[96,256]{1,0:T(8,128)S(1)}, u32[]{:S(2)}, u32[]{:S(2)}) collective-permute-start(f32[96,256]{1,0:T(8,128)S(1)} %fusion.2.own_ref), channel_id=1, source_target_pairs={{0,256},{16,272},{32,288},{48,304},{64,320},{80,336},{96,352},{112... | collective-permute-start | bytes 294920 | tf_op jit(solution)/shard_map/ppermute | solution.py:48
  58.1 3.4 %collective-permute-done.3.came_ref = f32[96,256]{1,0:T(8,128)S(1)} collective-permute-done((f32[96,256]{1,0:T(8,128)S(1)}, f32[96,256]{1,0:T(8,128)S(1)}, u32[]{:S(2)}, u32[]{:S(2)}) %collective-permute-start.3) | collective-permute-done | bytes 98336 | tf_op jit(solution)/shard_map/ppermute | solution.py:48
  61.5 1.5 %shard_map.80 = f32[4,192,256]{2,1,0:T(8,128)} custom-call(s32[2]{0:T(128)S(1)} %pad_add_fusion.me_ref, f32[96,256]{1,0:T(8,128)S(1)} %fusion.2.own_ref, f32[96,256]{1,0:T(8,128)S(1)} %collective-permute-done.3.came_ref), custom_call_target="tpu_custom_call" | custom-call | tf_op jit(solution)/shard_map/pallas_call | solution.py:212
  63.0 3.5 %all-to-all-start.2 = ((f32[4,192,256]{2,1,0:T(8,128)}), f32[4,192,256]{2,1,0:T(8,128)S(1)}, u32[]{:S(2)}, u32[]{:S(2)}) async-start(f32[4,192,256]{2,1,0:T(8,128)} %shard_map.80), calls=%async_computation.2 | async-start | bytes 1572864 | tf_op jit(solution)/shard_map/all_to_all | solution.py:41
  66.5 15.6 %collective-permute-start = (f32[1,1024]{1,0:T(1,128)S(1)}, f32[1,1024]{1,0:T(1,128)S(1)}, u32[]{:S(2)}, u32[]{:S(2)}) collective-permute-start(f32[1,1024]{1,0:T(1,128)S(1)} %get-tuple-element.14), channel_id=1, source_target_pairs={{1,0},{2,1},{3,2},{4,3},{5,4},{6,5},{7,6},{8,7},{9,8},{10,9},{11,1... | collective-permute-start | bytes 12296 | tf_op jit(solution)/shard_map/ppermute | solution.py:284
  82.2 1.9 %collective-permute-start.1 = (f32[1,1024]{1,0:T(1,128)S(1)}, f32[1,1024]{1,0:T(1,128)S(1)}, u32[]{:S(2)}, u32[]{:S(2)}) collective-permute-start(f32[1,1024]{1,0:T(1,128)S(1)} %get-tuple-element.15), channel_id=1, source_target_pairs={{0,1},{1,2},{2,3},{3,4},{4,5},{5,6},{6,7},{7,8},{8,9},{9,10},{10,1... | collective-permute-start | bytes 12296 | tf_op jit(solution)/shard_map/ppermute | solution.py:284
  84.1 0.0 collective-permute-done
  84.1 1.1 collective-permute-done.1
  85.2 0.0 copy-done.1
  85.2 0.1 rsqrt_multiply_fusion
  85.3 1.1 fusion.1.after_ref.base_ref
  86.4 0.0 all-to-all-done.2
  86.4 0.2 shard_map.81
  86.7 0.0 copy-done
  86.7 24.1 %all_to_all.22.got_ref = f32[4,8,96,256]{3,2,1,0:T(8,128)S(1)} all-to-all(f32[4,8,96,256]{3,2,1,0:T(8,128)S(1)} %shard_map.81), channel_id=1, replica_groups={{0,16,64,80},{32,48,96,112},{128,144,192,208},{160,176,224,240},{256,27..., dimensions={0} | all-to-all | bytes 6291456 | tf_op jit(solution)/shard_map/all_to_all | solution.py:41
  110.8 3.5 %shard_map.82 = f32[96,1024]{1,0:T(8,128)} custom-call(s32[2]{0:T(128)S(1)} %pad_add_fusion.me_ref, s32[16,32]{1,0:T(8,128)} %bitcast.8, s32[1,32]{1,0:T(1,128)} %bitcast.11, s32[1,16]{1,0:T(1,128)} %starts_hbm.3, f32[96,1024]{1,0:T(8,128)S(1)} %fusion.1.after_ref.base_ref, bf16[16,256,256]{2,1,0:T(8,128)(2,1)S(1)} %get-tuple-element.16.mats_ref, ...), custom_call_target="tpu_custom_call" | custom-call | tf_op jit(solution)/shard_map/pallas_call | solution.py:268
  (3 shorter events, 0.0 us)
Async XLA Ops:
  31.7 20.5 %copy-start.2 = (f32[96,256]{1,0:T(8,128)S(1)}, f32[96,256]{1,0:T(8,128)}, u32[]{:S(2)}) copy-start(f32[96,256]{1,0:T(8,128)} %param.7) | copy-start | bytes 294916
  31.9 53.3 %copy-start.1 = (f32[96,1024]{1,0:T(8,128)S(1)}, f32[96,1024]{1,0:T(8,128)}, u32[]{:S(2)}) copy-start(f32[96,1024]{1,0:T(8,128)} %vol_hbm.1) | copy-start | bytes 1179652
  42.8 9.4 %collective-permute-start.2 = (f32[104,256]{1,0:T(8,128)S(1)}, f32[104,256]{1,0:T(8,128)S(1)}, u32[]{:S(2)}, u32[]{:S(2)}) collective-permute-start(f32[104,256]{1,0:T(8,128)S(1)} %get-tuple-element.19), channel_id=1, source_target_pairs={{0,256},{16,272},{32,288},{48,304},{64,320},{80,336},{96,352},{112... | collective-permute-start | bytes 319496 | tf_op jit(solution)/shard_map/ppermute | solution.py:48
  52.3 34.4 %copy-start = (f32[96,256]{1,0:T(8,128)}, f32[96,256]{1,0:T(8,128)S(1)}, u32[]{:S(2)}) copy-start(f32[96,256]{1,0:T(8,128)S(1)} %fusion.2.own_ref) | copy-start | bytes 294916
  52.3 9.3 %collective-permute-start.3 = (f32[96,256]{1,0:T(8,128)S(1)}, f32[96,256]{1,0:T(8,128)S(1)}, u32[]{:S(2)}, u32[]{:S(2)}) collective-permute-start(f32[96,256]{1,0:T(8,128)S(1)} %fusion.2.own_ref), channel_id=1, source_target_pairs={{0,256},{16,272},{32,288},{48,304},{64,320},{80,336},{96,352},{112... | collective-permute-start | bytes 294920 | tf_op jit(solution)/shard_map/ppermute | solution.py:48
  63.0 23.4 %all-to-all-start.2 = ((f32[4,192,256]{2,1,0:T(8,128)}), f32[4,192,256]{2,1,0:T(8,128)S(1)}, u32[]{:S(2)}, u32[]{:S(2)}) async-start(f32[4,192,256]{2,1,0:T(8,128)} %shard_map.80), calls=%async_computation.2 | async-start | bytes 1572864 | tf_op jit(solution)/shard_map/all_to_all | solution.py:41
  66.5 17.5 %collective-permute-start = (f32[1,1024]{1,0:T(1,128)S(1)}, f32[1,1024]{1,0:T(1,128)S(1)}, u32[]{:S(2)}, u32[]{:S(2)}) collective-permute-start(f32[1,1024]{1,0:T(1,128)S(1)} %get-tuple-element.14), channel_id=1, source_target_pairs={{1,0},{2,1},{3,2},{4,3},{5,4},{6,5},{7,6},{8,7},{9,8},{10,9},{11,1... | collective-permute-start | bytes 12296 | tf_op jit(solution)/shard_map/ppermute | solution.py:284
  82.2 3.1 %collective-permute-start.1 = (f32[1,1024]{1,0:T(1,128)S(1)}, f32[1,1024]{1,0:T(1,128)S(1)}, u32[]{:S(2)}, u32[]{:S(2)}) collective-permute-start(f32[1,1024]{1,0:T(1,128)S(1)} %get-tuple-element.15), channel_id=1, source_target_pairs={{0,1},{1,2},{2,3},{3,4},{4,5},{5,6},{6,7},{7,8},{8,9},{9,10},{10,1... | collective-permute-start | bytes 12296 | tf_op jit(solution)/shard_map/ppermute | solution.py:284

commit v10 on v9

v10 whole, which is shorter than its diff:
```python
import functools

import jax
import jax.numpy as jnp
from jax import lax
from jax.experimental import pallas as pl
from jax.experimental.pallas import tpu as pltpu
from jax.sharding import PartitionSpec as P

relax = 1.0
tv_weight = 0.2
smooth_sq = 0.01

NX, NY = 4, 8
BX, BY = NX // 2, NY // 2
QUAD, SLOTS, FAR = 4, 8, 2
MATS_AT_ONCE = 4
W = 256
LANES = 128
VMEM_LIMIT = 32 * 1024 * 1024


def device_of(y, x):
    return (y % NY) * NX + x % NX


PLACES = [(qy, qx) for qy in range(2) for qx in range(2)]
BLOCKS = [(by, bx) for by in range(BY) for bx in range(BX)]


def exchange(value, level):
    slabs = lax.axis_size("gz")

    def member(slab, block, place):
        shift = slab % 2 + level - 1
        y, x = 2 * block[0] + place[0] + shift, 2 * block[1] + place[1] + shift
        return device_of(y, x) * slabs + slab

    groups = [
        [member(slab, block, place) for place in PLACES] for slab in range(slabs) for block in BLOCKS
    ]
    return lax.all_to_all(
        value, ("xy", "gz"), split_axis=0, concat_axis=0, axis_index_groups=groups, tiled=True
    )


def swap_far(value):
    moves = [(device_of(y, x), device_of(y + BY, x)) for y in range(NY) for x in range(NX)]
    return lax.ppermute(value, "xy", moves)


def split3(value):
    high = value.astype(jnp.bfloat16)
    rest = value - high.astype(jnp.float32)
    mid = rest.astype(jnp.bfloat16)
    low = (rest - mid.astype(jnp.float32)).astype(jnp.bfloat16)
    return [high, mid, low]


def with_ones(value):
    ones = jnp.ones((16, value.shape[1]), jnp.bfloat16)
    return jnp.concatenate(split3(value) + [ones], axis=0)


def shifted(device, core):
    return ((device >> 2) + NY - core) & (NY - 1), ((device & (NX - 1)) + NX - core) & (NX - 1)


def near_far(owner, me, core):
    (y, x), (my_y, my_x) = shifted(owner, core), shifted(me, core)
    near_y = (((y + 1) >> 1) + (my_y >> 1)) & 1
    near_x = (((x + 1) >> 1) + (my_x >> 1)) & 1
    place = ((y + 1) & 1) * 2 + ((x + 1) & 1)
    return near_y * 2 + near_x, place * FAR + (y >> 2)


def join3(product, rows):
    return product[2 * rows : 3 * rows] + product[rows : 2 * rows] + product[:rows]


def fetch_all(pairs, sems):
    copies = [pltpu.make_async_copy(src, dst, sems.at[i]) for i, (src, dst) in enumerate(pairs)]
    for copy in copies:
        copy.start()
    return copies


def pinned(value, space):
    return pltpu.with_memory_space_constraint(value, space)


ANY = pl.BlockSpec(memory_space=pl.ANY)
SMEM = pl.BlockSpec(memory_space=pltpu.SMEM)
VMEM = pl.BlockSpec(memory_space=pltpu.VMEM)
PARAMS = pltpu.CompilerParams(vmem_limit_bytes=VMEM_LIMIT)


def small_scratch(lists, owners, starts):
    return [pltpu.SMEM(a.shape, jnp.int32) for a in (lists, owners, starts)]


def fetch_mats(mats_hbm, mats, sems):
    return fetch_all(
        [
            (mats_hbm.at[0, pl.ds(k, MATS_AT_ONCE)], mats.at[pl.ds(k, MATS_AT_ONCE)])
            for k in range(0, mats.shape[0], MATS_AT_ONCE)
        ],
        sems,
    )


def wait_mats(copies, k):
    if k % MATS_AT_ONCE == 0:
        copies[k // MATS_AT_ONCE].wait()


def mats_scratch(mats, others):
    return [
        pltpu.VMEM(mats.shape[1:], jnp.bfloat16),
        pltpu.SemaphoreType.DMA((others,)),
        pltpu.SemaphoreType.DMA((mats.shape[1] // MATS_AT_ONCE,)),
    ]


def project_kernel(
    me_ref, lists_hbm, owners_hbm, starts_hbm, vol_hbm, mats_hbm,
    out_ref, first_ref, last_ref, lists, owners, starts, wide, mats, sems, mat_sems,
):
    rows, cols = vol_hbm.shape
    count = mats.shape[0]
    copies = fetch_all(
        [
            (lists_hbm, lists),
            (owners_hbm, owners),
            (starts_hbm, starts),
            (vol_hbm, wide.at[:, pl.ds(0, cols)]),
        ],
        sems,
    )
    mat_copies = fetch_mats(mats_hbm, mats, mat_sems)
    wide[:, cols:] = jnp.zeros((rows, LANES), jnp.float32)
    out_ref[...] = jnp.zeros(out_ref.shape, jnp.float32)
    for copy in copies:
        copy.wait()
    first_ref[...] = wide[:1, :cols]
    last_ref[...] = wide[rows - 1 :, :cols]
    me, core = me_ref[0], me_ref[1]
    for k in range(count):
        start = starts[0, k]
        near, far = near_far(owners[0, lists[k, me]], me, core)
        base = pl.multiple_of(start & -LANES, LANES)
        window = wide[:, pl.ds(base, W + LANES)]
        window = pltpu.roll(window, (W + LANES) - (start & (LANES - 1)), 1)[:, :W]
        wait_mats(mat_copies, k)
        product = jnp.dot(with_ones(window), mats[k], preferred_element_type=jnp.float32)
        out_ref[near, pl.ds(pl.multiple_of(far * rows, 8), rows), :] = join3(product, rows)
        out_ref[near, pl.ds(SLOTS * rows + far, 1), :] = product[3 * rows : 3 * rows + 1]


def project(me, lists, owners, starts, volume, mats):
    rows, cols = volume.shape
    operands = [pinned(a, pltpu.HBM) for a in (lists, owners, starts, volume, mats)]
    return pl.pallas_call(
        project_kernel,
        out_shape=[
            pltpu.VMEM((QUAD, SLOTS * rows + 8, W), jnp.float32),
            pltpu.VMEM((1, cols), jnp.float32),
            pltpu.VMEM((1, cols), jnp.float32),
        ],
        in_specs=[SMEM] + [ANY] * 5,
        out_specs=[VMEM] * 3,
        scratch_shapes=small_scratch(lists, owners, starts)
        + [pltpu.VMEM((rows, cols + LANES), jnp.float32)]
        + mats_scratch(mats, 4),
        compiler_params=PARAMS,
    )(me, *operands)


def sum_quad(ref):
    return ref[0] + ref[1] + ref[2] + ref[3]


def gather_near_kernel(rows, in_ref, out_ref):
    total = sum_quad(in_ref)
    for place in range(QUAD):
        at = place * FAR
        out_ref[place, : FAR * rows] = total[at * rows : (at + FAR) * rows]
        sums = total[SLOTS * rows + at : SLOTS * rows + at + FAR]
        out_ref[place, FAR * rows : FAR * rows + FAR] = sums
        out_ref[place, FAR * rows + FAR :] = jnp.zeros((8 - FAR, W), jnp.float32)


def gather_near(arrived):
    rows = (arrived.shape[1] - 8) // SLOTS
    return pl.pallas_call(
        functools.partial(gather_near_kernel, rows),
        out_shape=pltpu.VMEM((QUAD, FAR * rows + 8, W), jnp.float32),
        in_specs=[VMEM],
        out_specs=VMEM,
        compiler_params=PARAMS,
    )(pinned(arrived, pltpu.VMEM))


def my_half(me_ref, rows):
    return pl.ds(pl.multiple_of((shifted(me_ref[0], me_ref[1])[0] >> 2) * rows, 8), rows)


def gather_far_kernel(me_ref, in_ref, measured_ref, out_ref):
    rows = measured_ref.shape[0]
    total = sum_quad(in_ref)
    out_ref[: FAR * rows] = -total[: FAR * rows]
    out_ref[FAR * rows :] = total[FAR * rows :]
    mine = my_half(me_ref, rows)
    out_ref[mine, :] = out_ref[mine, :] + measured_ref[...]


def gather_far(me, arrived, measured):
    return pl.pallas_call(
        gather_far_kernel,
        out_shape=pltpu.VMEM(arrived.shape[1:], jnp.float32),
        in_specs=[SMEM, VMEM, VMEM],
        out_specs=VMEM,
        compiler_params=PARAMS,
    )(me, pinned(arrived, pltpu.VMEM), pinned(measured, pltpu.VMEM))


def spread_far_kernel(me_ref, own_ref, came_ref, out_ref, mine_ref):
    rows = mine_ref.shape[0]
    both = own_ref[...] + came_ref[...]
    for half in range(FAR):
        at = FAR * rows + half
        value = both[half * rows : (half + 1) * rows] / both[at : at + 1]
        for place in range(QUAD):
            out_ref[place, half * rows : (half + 1) * rows] = value
    mine_ref[...] = out_ref[0, my_half(me_ref, rows), :]


def spread_far(me, own, came):
    rows = (own.shape[0] - 8) // FAR
    return pl.pallas_call(
        spread_far_kernel,
        out_shape=[
            pltpu.VMEM((QUAD, FAR * rows, W), jnp.float32),
            jax.ShapeDtypeStruct((rows, W), jnp.float32),
        ],
        in_specs=[SMEM, VMEM, VMEM],
        out_specs=[VMEM, VMEM],
        compiler_params=PARAMS,
    )(me, pinned(own, pltpu.VMEM), pinned(came, pltpu.VMEM))


def spread_near_kernel(column_ref, first_in, last_in, out_hbm, first_ref, last_ref, sems):
    copies = fetch_all([(column_ref, out_hbm.at[place]) for place in range(QUAD)], sems)
    first_ref[...] = first_in[...]
    last_ref[...] = last_in[...]
    for copy in copies:
        copy.wait()


def spread_near(column, first, last):
    face = jax.ShapeDtypeStruct(first.shape, jnp.float32)
    return pl.pallas_call(
        spread_near_kernel,
        out_shape=[pltpu.HBM((QUAD,) + column.shape, jnp.float32), face, face],
        in_specs=[VMEM] * 3,
        out_specs=[ANY, VMEM, VMEM],
        scratch_shapes=[pltpu.SemaphoreType.DMA((QUAD,))],
        compiler_params=PARAMS,
    )(*(pinned(a, pltpu.VMEM) for a in (column, first, last)))


def back_kernel(
    me_ref, lists_hbm, owners_hbm, starts_hbm, mats_hbm, base_ref, got_ref, out_ref,
    lists, owners, starts, total, mats, sems, mat_sems,
):
    rows, cols = base_ref.shape
    count = mats.shape[0]
    copies = fetch_all([(lists_hbm, lists), (owners_hbm, owners), (starts_hbm, starts)], sems)
    mat_copies = fetch_mats(mats_hbm, mats, mat_sems)
    total[...] = jnp.zeros(total.shape, jnp.float32)
    for copy in copies:
        copy.wait()
    me, core = me_ref[0], me_ref[1]
    for k in range(count):
        start = starts[0, k]
        near, far = near_far(owners[0, lists[k, me]], me, core)
        base = pl.multiple_of(start & -LANES, LANES)
        wait_mats(mat_copies, k)
        product = lax.dot_general(
            with_ones(got_ref[near, far]),
            mats[k],
            (((1,), (1,)), ((), ())),
            preferred_element_type=jnp.float32,
        )
        value = jnp.concatenate([join3(product, rows), product[3 * rows : 3 * rows + 8]], axis=0)
        value = jnp.concatenate([value, jnp.zeros((rows + 8, LANES), jnp.float32)], axis=1)
        total[:, pl.ds(base, W + LANES)] += pltpu.roll(value, start & (LANES - 1), 1)
    column = jnp.maximum(total[rows : rows + 1, :cols], 1.0)
    out_ref[...] = base_ref[...] + relax * (total[:rows, :cols] / column)


def back_project(me, lists, owners, starts, base, mats, got):
    rows, cols = base.shape
    operands = [pinned(a, pltpu.HBM) for a in (lists, owners, starts, mats)]
    operands += [pinned(a, pltpu.VMEM) for a in (base, got)]
    return pl.pallas_call(
        back_kernel,
        out_shape=jax.ShapeDtypeStruct((rows, cols), jnp.float32),
        in_specs=[SMEM] + [ANY] * 4 + [VMEM] * 2,
        out_specs=VMEM,
        scratch_shapes=small_scratch(lists, owners, starts)
        + [pltpu.VMEM((rows + 8, cols + LANES), jnp.float32)]
        + mats_scratch(mats, 3),
        compiler_params=PARAMS,
    )(me, *operands)


def with_faces(volume, first, last):
    count = lax.axis_size("gz")
    up = [(i, i + 1) for i in range(count - 1)]
    down = [(i + 1, i) for i in range(count - 1)]
    return jnp.concatenate(
        [lax.ppermute(last, "gz", up), volume, lax.ppermute(first, "gz", down)], axis=0
    )


def total_variation(padded):
    diffs = padded[1:] - padded[:-1]
    slopes = diffs / jnp.sqrt(diffs * diffs + smooth_sq)
    return slopes[:-1] - slopes[1:]


def per_device(volume, sinogram, ray_mats, offsets, ray_lists, owner_map):
    rows = volume.shape[0]
    core = lax.axis_index("gz") % 2
    device = lax.axis_index("xy")
    me = jnp.stack([device, core]).astype(jnp.int32)
    plan = (me, ray_lists.T, owner_map.reshape(1, -1), offsets)
    outgoing, first, last = project(*plan, volume, ray_mats)
    part = gather_far(me, exchange(gather_near(exchange(outgoing, 1)), 2), sinogram)
    spread, weighted = spread_far(me, part, swap_far(part))
    column = exchange(spread, 2).reshape(SLOTS, rows, W)
    spread, first, last = spread_near(column, first, last)
    base = volume - tv_weight * total_variation(with_faces(volume, first, last))
    got = exchange(spread, 1)
    new_volume = back_project(*plan, base, ray_mats, got)
    return (new_volume, weighted)


def solution(mesh):
    in_specs = (P("gz", "xy"), P("gz", "xy"), P("xy", None, None, None), P("xy", None), P(), P())
    out_specs = (P("gz", "xy"), P("gz", "xy"))
    return jax.shard_map(
        per_device, mesh=mesh, in_specs=in_specs, out_specs=out_specs, check_vma=False
    )
```

time: 115 us -> 107 us (0.930)
  the two profiles are of different devices: /device:TPU:1 before, /device:TPU:2 now
where the time goes in v10:
time: 107 us
  blocking collectives  52.2 us (49%)
  waiting for transfers between devices  24.8 us (23%)
  starting transfers between devices  15.9 us (15%)
  Pallas kernels  11.8 us (11%)
  other arithmetic  1.25 us (1%)
    all_to_all x3, blocking collectives, exchange(): lax.all_to_all(value, ('xy', 'gz'), split_axis=0, concat_axis=0, axis_ind...  52.2 us
    all_to_all x1, waiting for transfers between devices, exchange(): lax.all_to_all(value, ('xy', 'gz'), split_axis=0, concat_axis=0, axis_ind...  13.8 us
    ppermute x1, waiting for transfers between devices, swap_far(): return lax.ppermute(value, 'xy', moves)  10.2 us
    all_to_all x1, starting transfers between devices, exchange(): lax.all_to_all(value, ('xy', 'gz'), split_axis=0, concat_axis=0, axis_ind...  7.42 us
    pallas_call x1, Pallas kernels, back_project(): pl.pallas_call(back_kernel, out_shape=jax.ShapeDtypeStruct((rows, cols),...  4.44 us
    ppermute x1, starting transfers between devices, swap_far(): return lax.ppermute(value, 'xy', moves)  4.13 us
    pallas_call x1, Pallas kernels, project(): pl.pallas_call(project_kernel, out_shape=[pltpu.VMEM((QUAD, SLOTS * rows...  3.69 us
    ppermute x1, starting transfers between devices, with_faces(): lax.ppermute(last, 'gz', up)  3.03 us
  transfers between devices with their start and end apart: 4, of which 3 were waited for; matrix products, arithmetic and copies ran while one was open for 1% of the time, Pallas kernels for 0%

profile of v10, /device:TPU:2, one launch (start us, length us, event | category | flops | bytes accessed | tf_op | source)
XLA Modules:
  0.0 106.7 jit_solution(15094956660090735563)
XLA Ops:
  0.6 0.1 pad_add_fusion.me_ref
  0.7 3.7 %shard_map.77 = (f32[4,776,256]{2,1,0:T(8,128)S(1)}, f32[1,1024]{1,0:T(1,128)S(1)}, f32[1,1024]{1,0:T(1,128)S(1)}) custom-call(s32[2]{0:T(128)S(1)} %pad_add_fusion.me_ref, s32[16,32]{1,0:T(8,128)} %bitcast.6, s32[1,32]{1,0:T(1,128)} %bitcast.8, s32[1,16]{1,0:T(1,128)} %starts_hbm.3, f32[96,1024]{1,0:T(8,128)} %vol_hbm.1, bf16[1,16,256,256]{3,2,1,0:T(8,128)(2,1)} %mats_hbm.3), custom_call_target="tpu_custom_call" | custom-call | tf_op jit(solution)/shard_map/pallas_call | solution.py:163
  4.4 28.6 %all_to_all.20.in_ref = f32[4,776,256]{2,1,0:T(8,128)S(1)} all-to-all(f32[4,776,256]{2,1,0:T(8,128)S(1)} %get-tuple-element.10), channel_id=1, replica_groups={{0,16,64,80},{32,48,96,112},{128,144,192,208},{160,176,224,240},{256,27..., dimensions={0} | all-to-all | bytes 6356992 | tf_op jit(solution)/shard_map/all_to_all | solution.py:42
  33.0 0.0 copy-start
  33.1 0.1 shard_map.78
  33.2 11.9 %all_to_all.21.in_ref = f32[4,200,256]{2,1,0:T(8,128)S(1)} all-to-all(f32[4,200,256]{2,1,0:T(8,128)S(1)} %shard_map.78), channel_id=1, replica_groups={{80,96,144,160},{112,64,176,128},{208,224,272,288},{240,192,304,256},{3..., dimensions={0} | all-to-all | bytes 1638400 | tf_op jit(solution)/shard_map/all_to_all | solution.py:42
  45.1 0.0 copy-done
  45.1 0.6 shard_map.79.own_ref
  45.7 4.1 %collective-permute-start = (f32[200,256]{1,0:T(8,128)S(1)}, f32[200,256]{1,0:T(8,128)S(1)}, u32[]{:S(2)}, u32[]{:S(2)}) collective-permute-start(f32[200,256]{1,0:T(8,128)S(1)} %shard_map.79.own_ref), channel_id=1, source_target_pairs={{0,256},{16,272},{32,288},{48,304},{64,320},{80,336},{96,352},{112... | collective-permute-start | bytes 614408 | tf_op jit(solution)/shard_map/ppermute | solution.py:49
  49.8 10.2 %collective-permute-done.came_ref = f32[200,256]{1,0:T(8,128)S(1)} collective-permute-done((f32[200,256]{1,0:T(8,128)S(1)}, f32[200,256]{1,0:T(8,128)S(1)}, u32[]{:S(2)}, u32[]{:S(2)}) %collective-permute-start) | collective-permute-done | bytes 204832 | tf_op jit(solution)/shard_map/ppermute | solution.py:49
  60.1 1.3 %shard_map.80 = (f32[4,192,256]{2,1,0:T(8,128)S(1)}, f32[96,256]{1,0:T(8,128)}) custom-call(s32[2]{0:T(128)S(1)} %pad_add_fusion.me_ref, f32[200,256]{1,0:T(8,128)S(1)} %shard_map.79.own_ref, f32[200,256]{1,0:T(8,128)S(1)} %collective-permute-done.came_ref), custom_call_target="tpu_custom_call" | custom-call | tf_op jit(solution)/shard_map/pallas_call | solution.py:240
  61.3 11.7 %all_to_all.22 = f32[4,192,256]{2,1,0:T(8,128)S(1)} all-to-all(f32[4,192,256]{2,1,0:T(8,128)S(1)} %get-tuple-element.11), channel_id=1, replica_groups={{80,96,144,160},{112,64,176,128},{208,224,272,288},{240,192,304,256},{3..., dimensions={0} | all-to-all | bytes 1572864 | tf_op jit(solution)/shard_map/all_to_all | solution.py:42
  73.0 1.7 %shard_map.81 = (f32[4,8,96,256]{3,2,1,0:T(8,128)}, f32[1,1024]{1,0:T(1,128)S(1)}, f32[1,1024]{1,0:T(1,128)S(1)}) custom-call(f32[8,96,256]{2,1,0:T(8,128)S(1)} %bitcast.5, f32[1,1024]{1,0:T(1,128)S(1)} %get-tuple-element.12.first_in, f32[1,1024]{1,0:T(1,128)S(1)} %get-tuple-element.13.last_in), custom_call_target="tpu_custom_call" | custom-call | tf_op jit(solution)/shard_map/pallas_call | solution.py:262
  74.7 0.0 copy-start.1
  74.7 7.4 %all-to-all-start.3 = ((f32[4,8,96,256]{3,2,1,0:T(8,128)}), f32[4,8,96,256]{3,2,1,0:T(8,128)S(1)}, u32[]{:S(2)}, u32[]{:S(2)}) async-start(f32[4,8,96,256]{3,2,1,0:T(8,128)} %get-tuple-element.16), calls=%async_computation.3 | async-start | bytes 6291456 | tf_op jit(solution)/shard_map/all_to_all | solution.py:42
  82.2 1.3 %collective-permute-start.1 = (f32[1,1024]{1,0:T(1,128)S(1)}, f32[1,1024]{1,0:T(1,128)S(1)}, u32[]{:S(2)}, u32[]{:S(2)}) collective-permute-start(f32[1,1024]{1,0:T(1,128)S(1)} %get-tuple-element.14), channel_id=1, source_target_pairs={{1,0},{2,1},{3,2},{4,3},{5,4},{6,5},{7,6},{8,7},{9,8},{10,9},{11,1... | collective-permute-start | bytes 12296 | tf_op jit(solution)/shard_map/ppermute | solution.py:323
  83.5 3.0 %collective-permute-start.2 = (f32[1,1024]{1,0:T(1,128)S(1)}, f32[1,1024]{1,0:T(1,128)S(1)}, u32[]{:S(2)}, u32[]{:S(2)}) collective-permute-start(f32[1,1024]{1,0:T(1,128)S(1)} %get-tuple-element.15), channel_id=1, source_target_pairs={{0,1},{1,2},{2,3},{3,4},{4,5},{5,6},{6,7},{7,8},{8,9},{9,10},{10,1... | collective-permute-start | bytes 12296 | tf_op jit(solution)/shard_map/ppermute | solution.py:323
  86.5 0.0 collective-permute-done.1
  86.5 0.8 collective-permute-done.2
  87.3 0.0 copy-done.1
  87.3 0.1 rsqrt_multiply_fusion
  87.4 1.1 fusion.1.base_ref
  88.5 13.8 %all-to-all-done.3.got_ref = f32[4,8,96,256]{3,2,1,0:T(8,128)S(1)} async-done(((f32[4,8,96,256]{3,2,1,0:T(8,128)}), f32[4,8,96,256]{3,2,1,0:T(8,128)S(1)}, u32[]{:S(2)}, u32[]{:S(2)}) %all-to-all-start.3) | async-done | bytes 3145760 | tf_op jit(solution)/shard_map/all_to_all | solution.py:42
  102.3 4.4 %shard_map.82 = f32[96,1024]{1,0:T(8,128)} custom-call(s32[2]{0:T(128)S(1)} %pad_add_fusion.me_ref, s32[16,32]{1,0:T(8,128)} %bitcast.7, s32[1,32]{1,0:T(1,128)} %bitcast.9, s32[1,16]{1,0:T(1,128)} %starts_hbm.3, bf16[1,16,256,256]{3,2,1,0:T(8,128)(2,1)} %mats_hbm.3, f32[96,1024]{1,0:T(8,128)S(1)} %fusion.1.base_ref, ...), custom_call_target="tpu_custom_call" | custom-call | tf_op jit(solution)/shard_map/pallas_call | solution.py:306
Async XLA Ops:
  33.0 12.1 %copy-start = (f32[96,256]{1,0:T(8,128)S(1)}, f32[96,256]{1,0:T(8,128)}, u32[]{:S(2)}) copy-start(f32[96,256]{1,0:T(8,128)} %measured_ref.1) | copy-start | bytes 294916
  45.7 14.4 %collective-permute-start = (f32[200,256]{1,0:T(8,128)S(1)}, f32[200,256]{1,0:T(8,128)S(1)}, u32[]{:S(2)}, u32[]{:S(2)}) collective-permute-start(f32[200,256]{1,0:T(8,128)S(1)} %shard_map.79.own_ref), channel_id=1, source_target_pairs={{0,256},{16,272},{32,288},{48,304},{64,320},{80,336},{96,352},{112... | collective-permute-start | bytes 614408 | tf_op jit(solution)/shard_map/ppermute | solution.py:49
  74.7 12.6 %copy-start.1 = (f32[96,1024]{1,0:T(8,128)S(1)}, f32[96,1024]{1,0:T(8,128)}, u32[]{:S(2)}) copy-start(f32[96,1024]{1,0:T(8,128)} %vol_hbm.1) | copy-start | bytes 1179652
  74.7 27.5 %all-to-all-start.3 = ((f32[4,8,96,256]{3,2,1,0:T(8,128)}), f32[4,8,96,256]{3,2,1,0:T(8,128)S(1)}, u32[]{:S(2)}, u32[]{:S(2)}) async-start(f32[4,8,96,256]{3,2,1,0:T(8,128)} %get-tuple-element.16), calls=%async_computation.3 | async-start | bytes 6291456 | tf_op jit(solution)/shard_map/all_to_all | solution.py:42
  82.2 4.3 %collective-permute-start.1 = (f32[1,1024]{1,0:T(1,128)S(1)}, f32[1,1024]{1,0:T(1,128)S(1)}, u32[]{:S(2)}, u32[]{:S(2)}) collective-permute-start(f32[1,1024]{1,0:T(1,128)S(1)} %get-tuple-element.14), channel_id=1, source_target_pairs={{1,0},{2,1},{3,2},{4,3},{5,4},{6,5},{7,6},{8,7},{9,8},{10,9},{11,1... | collective-permute-start | bytes 12296 | tf_op jit(solution)/shard_map/ppermute | solution.py:323
  83.5 3.8 %collective-permute-start.2 = (f32[1,1024]{1,0:T(1,128)S(1)}, f32[1,1024]{1,0:T(1,128)S(1)}, u32[]{:S(2)}, u32[]{:S(2)}) collective-permute-start(f32[1,1024]{1,0:T(1,128)S(1)} %get-tuple-element.15), channel_id=1, source_target_pairs={{0,1},{1,2},{2,3},{3,4},{4,5},{5,6},{6,7},{7,8},{8,9},{9,10},{10,1... | collective-permute-start | bytes 12296 | tf_op jit(solution)/shard_map/ppermute | solution.py:323

commit v11 on v10

--- a/solution.py
+++ b/solution.py
@@ -14,7 +14,6 @@
 NX, NY = 4, 8
 BX, BY = NX // 2, NY // 2
 QUAD, SLOTS, FAR = 4, 8, 2
-MATS_AT_ONCE = 4
 W = 256
 LANES = 128
 VMEM_LIMIT = 32 * 1024 * 1024
@@ -100,25 +99,27 @@
 
 
 def fetch_mats(mats_hbm, mats, sems):
+    size = mats.shape[0] // sems.shape[0]
     return fetch_all(
         [
-            (mats_hbm.at[0, pl.ds(k, MATS_AT_ONCE)], mats.at[pl.ds(k, MATS_AT_ONCE)])
-            for k in range(0, mats.shape[0], MATS_AT_ONCE)
+            (mats_hbm.at[0, pl.ds(k, size)], mats.at[pl.ds(k, size)])
+            for k in range(0, mats.shape[0], size)
         ],
         sems,
     )
 
 
-def wait_mats(copies, k):
-    if k % MATS_AT_ONCE == 0:
-        copies[k // MATS_AT_ONCE].wait()
-
-
-def mats_scratch(mats, others):
+def wait_mats(copies, k, count):
+    size = count // len(copies)
+    if k % size == 0:
+        copies[k // size].wait()
+
+
+def mats_scratch(mats, others, pieces):
     return [
         pltpu.VMEM(mats.shape[1:], jnp.bfloat16),
         pltpu.SemaphoreType.DMA((others,)),
-        pltpu.SemaphoreType.DMA((mats.shape[1] // MATS_AT_ONCE,)),
+        pltpu.SemaphoreType.DMA((pieces,)),
     ]
 
 
@@ -151,7 +152,7 @@
         base = pl.multiple_of(start & -LANES, LANES)
         window = wide[:, pl.ds(base, W + LANES)]
         window = pltpu.roll(window, (W + LANES) - (start & (LANES - 1)), 1)[:, :W]
-        wait_mats(mat_copies, k)
+        wait_mats(mat_copies, k, count)
         product = jnp.dot(with_ones(window), mats[k], preferred_element_type=jnp.float32)
         out_ref[near, pl.ds(pl.multiple_of(far * rows, 8), rows), :] = join3(product, rows)
         out_ref[near, pl.ds(SLOTS * rows + far, 1), :] = product[3 * rows : 3 * rows + 1]
@@ -171,7 +172,7 @@
         out_specs=[VMEM] * 3,
         scratch_shapes=small_scratch(lists, owners, starts)
         + [pltpu.VMEM((rows, cols + LANES), jnp.float32)]
-        + mats_scratch(mats, 4),
+        + mats_scratch(mats, 4, 1),
         compiler_params=PARAMS,
     )(me, *operands)
 
@@ -285,7 +286,7 @@
         start = starts[0, k]
         near, far = near_far(owners[0, lists[k, me]], me, core)
         base = pl.multiple_of(start & -LANES, LANES)
-        wait_mats(mat_copies, k)
+        wait_mats(mat_copies, k, count)
         product = lax.dot_general(
             with_ones(got_ref[near, far]),
             mats[k],
@@ -310,7 +311,7 @@
         out_specs=VMEM,
         scratch_shapes=small_scratch(lists, owners, starts)
         + [pltpu.VMEM((rows + 8, cols + LANES), jnp.float32)]
-        + mats_scratch(mats, 3),
+        + mats_scratch(mats, 3, 2),
         compiler_params=PARAMS,
     )(me, *operands)
 

time: 107 us -> 106 us (level)
  no operation moved by 1% of the time
where the time goes in v11:
time: 106 us
  blocking collectives  52.2 us (49%)
  waiting for transfers between devices  24.8 us (23%)
  starting transfers between devices  15.9 us (15%)
  Pallas kernels  11 us (10%)
  other arithmetic  1.25 us (1%)
    all_to_all x3, blocking collectives, exchange(): lax.all_to_all(value, ('xy', 'gz'), split_axis=0, concat_axis=0, axis_ind...  52.2 us
    all_to_all x1, waiting for transfers between devices, exchange(): lax.all_to_all(value, ('xy', 'gz'), split_axis=0, concat_axis=0, axis_ind...  13.8 us
    ppermute x1, waiting for transfers between devices, swap_far(): return lax.ppermute(value, 'xy', moves)  10.2 us
    all_to_all x1, starting transfers between devices, exchange(): lax.all_to_all(value, ('xy', 'gz'), split_axis=0, concat_axis=0, axis_ind...  7.42 us
    ppermute x1, starting transfers between devices, swap_far(): return lax.ppermute(value, 'xy', moves)  4.14 us
    pallas_call x1, Pallas kernels, back_project(): pl.pallas_call(back_kernel, out_shape=jax.ShapeDtypeStruct((rows, cols),...  4 us
    pallas_call x1, Pallas kernels, project(): pl.pallas_call(project_kernel, out_shape=[pltpu.VMEM((QUAD, SLOTS * rows...  3.35 us
    ppermute x1, starting transfers between devices, with_faces(): lax.ppermute(last, 'gz', up)  3.03 us
  transfers between devices with their start and end apart: 4, of which 3 were waited for; matrix products, arithmetic and copies ran while one was open for 1% of the time, Pallas kernels for 0%

profile of v11, /device:TPU:2, one launch (start us, length us, event | category | flops | bytes accessed | tf_op | source)
XLA Modules:
  0.0 105.9 jit_solution(13589115416644099000)
XLA Ops:
  0.6 0.1 pad_add_fusion.me_ref
  0.7 3.3 %shard_map.77 = (f32[4,776,256]{2,1,0:T(8,128)S(1)}, f32[1,1024]{1,0:T(1,128)S(1)}, f32[1,1024]{1,0:T(1,128)S(1)}) custom-call(s32[2]{0:T(128)S(1)} %pad_add_fusion.me_ref, s32[16,32]{1,0:T(8,128)} %bitcast.6, s32[1,32]{1,0:T(1,128)} %bitcast.8, s32[1,16]{1,0:T(1,128)} %starts_hbm.3, f32[96,1024]{1,0:T(8,128)} %vol_hbm.1, bf16[1,16,256,256]{3,2,1,0:T(8,128)(2,1)} %mats_hbm.3), custom_call_target="tpu_custom_call" | custom-call | tf_op jit(solution)/shard_map/pallas_call | solution.py:164
  4.1 28.6 %all_to_all.20.in_ref = f32[4,776,256]{2,1,0:T(8,128)S(1)} all-to-all(f32[4,776,256]{2,1,0:T(8,128)S(1)} %get-tuple-element.10), channel_id=1, replica_groups={{0,16,64,80},{32,48,96,112},{128,144,192,208},{160,176,224,240},{256,27..., dimensions={0} | all-to-all | bytes 6356992 | tf_op jit(solution)/shard_map/all_to_all | solution.py:41
  32.7 0.0 copy-start
  32.7 0.1 shard_map.78
  32.8 11.9 %all_to_all.21.in_ref = f32[4,200,256]{2,1,0:T(8,128)S(1)} all-to-all(f32[4,200,256]{2,1,0:T(8,128)S(1)} %shard_map.78), channel_id=1, replica_groups={{80,96,144,160},{112,64,176,128},{208,224,272,288},{240,192,304,256},{3..., dimensions={0} | all-to-all | bytes 1638400 | tf_op jit(solution)/shard_map/all_to_all | solution.py:41
  44.7 0.0 copy-done
  44.8 0.6 shard_map.79.own_ref
  45.4 4.1 %collective-permute-start = (f32[200,256]{1,0:T(8,128)S(1)}, f32[200,256]{1,0:T(8,128)S(1)}, u32[]{:S(2)}, u32[]{:S(2)}) collective-permute-start(f32[200,256]{1,0:T(8,128)S(1)} %shard_map.79.own_ref), channel_id=1, source_target_pairs={{0,256},{16,272},{32,288},{48,304},{64,320},{80,336},{96,352},{112... | collective-permute-start | bytes 614408 | tf_op jit(solution)/shard_map/ppermute | solution.py:48
  49.5 10.2 %collective-permute-done.came_ref = f32[200,256]{1,0:T(8,128)S(1)} collective-permute-done((f32[200,256]{1,0:T(8,128)S(1)}, f32[200,256]{1,0:T(8,128)S(1)}, u32[]{:S(2)}, u32[]{:S(2)}) %collective-permute-start) | collective-permute-done | bytes 204832 | tf_op jit(solution)/shard_map/ppermute | solution.py:48
  59.7 1.3 %shard_map.80 = (f32[4,192,256]{2,1,0:T(8,128)S(1)}, f32[96,256]{1,0:T(8,128)}) custom-call(s32[2]{0:T(128)S(1)} %pad_add_fusion.me_ref, f32[200,256]{1,0:T(8,128)S(1)} %shard_map.79.own_ref, f32[200,256]{1,0:T(8,128)S(1)} %collective-permute-done.came_ref), custom_call_target="tpu_custom_call" | custom-call | tf_op jit(solution)/shard_map/pallas_call | solution.py:241
  61.0 11.7 %all_to_all.22 = f32[4,192,256]{2,1,0:T(8,128)S(1)} all-to-all(f32[4,192,256]{2,1,0:T(8,128)S(1)} %get-tuple-element.11), channel_id=1, replica_groups={{80,96,144,160},{112,64,176,128},{208,224,272,288},{240,192,304,256},{3..., dimensions={0} | all-to-all | bytes 1572864 | tf_op jit(solution)/shard_map/all_to_all | solution.py:41
  72.7 1.7 %shard_map.81 = (f32[4,8,96,256]{3,2,1,0:T(8,128)}, f32[1,1024]{1,0:T(1,128)S(1)}, f32[1,1024]{1,0:T(1,128)S(1)}) custom-call(f32[8,96,256]{2,1,0:T(8,128)S(1)} %bitcast.5, f32[1,1024]{1,0:T(1,128)S(1)} %get-tuple-element.12.first_in, f32[1,1024]{1,0:T(1,128)S(1)} %get-tuple-element.13.last_in), custom_call_target="tpu_custom_call" | custom-call | tf_op jit(solution)/shard_map/pallas_call | solution.py:263
  74.4 0.0 copy-start.1
  74.4 7.4 %all-to-all-start.3 = ((f32[4,8,96,256]{3,2,1,0:T(8,128)}), f32[4,8,96,256]{3,2,1,0:T(8,128)S(1)}, u32[]{:S(2)}, u32[]{:S(2)}) async-start(f32[4,8,96,256]{3,2,1,0:T(8,128)} %get-tuple-element.16), calls=%async_computation.3 | async-start | bytes 6291456 | tf_op jit(solution)/shard_map/all_to_all | solution.py:41
  81.8 1.3 %collective-permute-start.1 = (f32[1,1024]{1,0:T(1,128)S(1)}, f32[1,1024]{1,0:T(1,128)S(1)}, u32[]{:S(2)}, u32[]{:S(2)}) collective-permute-start(f32[1,1024]{1,0:T(1,128)S(1)} %get-tuple-element.14), channel_id=1, source_target_pairs={{1,0},{2,1},{3,2},{4,3},{5,4},{6,5},{7,6},{8,7},{9,8},{10,9},{11,1... | collective-permute-start | bytes 12296 | tf_op jit(solution)/shard_map/ppermute | solution.py:324
  83.1 3.0 %collective-permute-start.2 = (f32[1,1024]{1,0:T(1,128)S(1)}, f32[1,1024]{1,0:T(1,128)S(1)}, u32[]{:S(2)}, u32[]{:S(2)}) collective-permute-start(f32[1,1024]{1,0:T(1,128)S(1)} %get-tuple-element.15), channel_id=1, source_target_pairs={{0,1},{1,2},{2,3},{3,4},{4,5},{5,6},{6,7},{7,8},{8,9},{9,10},{10,1... | collective-permute-start | bytes 12296 | tf_op jit(solution)/shard_map/ppermute | solution.py:324
  86.1 0.0 collective-permute-done.1
  86.1 0.8 collective-permute-done.2
  86.9 0.0 copy-done.1
  86.9 0.1 rsqrt_multiply_fusion
  87.1 1.1 %fusion.1.base_ref = f32[96,1024]{1,0:T(8,128)S(1)} fusion(f32[96,1024]{1,0:T(8,128)} %vol_hbm.1, f32[97,1024]{1,0:T(8,128)S(1)} %rsqrt_multiply_fusion), kind=kLoop, calls=%fused_computation.4 | loop fusion | flops 294912 | bytes 1572864 | tf_op jit(solution)/shard_map/sub | solution.py:345
  88.1 13.8 %all-to-all-done.3.got_ref = f32[4,8,96,256]{3,2,1,0:T(8,128)S(1)} async-done(((f32[4,8,96,256]{3,2,1,0:T(8,128)}), f32[4,8,96,256]{3,2,1,0:T(8,128)S(1)}, u32[]{:S(2)}, u32[]{:S(2)}) %all-to-all-start.3) | async-done | bytes 3145760 | tf_op jit(solution)/shard_map/all_to_all | solution.py:41
  101.9 4.0 %shard_map.82 = f32[96,1024]{1,0:T(8,128)} custom-call(s32[2]{0:T(128)S(1)} %pad_add_fusion.me_ref, s32[16,32]{1,0:T(8,128)} %bitcast.7, s32[1,32]{1,0:T(1,128)} %bitcast.9, s32[1,16]{1,0:T(1,128)} %starts_hbm.3, bf16[1,16,256,256]{3,2,1,0:T(8,128)(2,1)} %mats_hbm.3, f32[96,1024]{1,0:T(8,128)S(1)} %fusion.1.base_ref, ...), custom_call_target="tpu_custom_call" | custom-call | tf_op jit(solution)/shard_map/pallas_call | solution.py:307
Async XLA Ops:
  32.7 12.1 %copy-start = (f32[96,256]{1,0:T(8,128)S(1)}, f32[96,256]{1,0:T(8,128)}, u32[]{:S(2)}) copy-start(f32[96,256]{1,0:T(8,128)} %measured_ref.1) | copy-start | bytes 294916
  45.4 14.4 %collective-permute-start = (f32[200,256]{1,0:T(8,128)S(1)}, f32[200,256]{1,0:T(8,128)S(1)}, u32[]{:S(2)}, u32[]{:S(2)}) collective-permute-start(f32[200,256]{1,0:T(8,128)S(1)} %shard_map.79.own_ref), channel_id=1, source_target_pairs={{0,256},{16,272},{32,288},{48,304},{64,320},{80,336},{96,352},{112... | collective-permute-start | bytes 614408 | tf_op jit(solution)/shard_map/ppermute | solution.py:48
  74.4 12.6 %copy-start.1 = (f32[96,1024]{1,0:T(8,128)S(1)}, f32[96,1024]{1,0:T(8,128)}, u32[]{:S(2)}) copy-start(f32[96,1024]{1,0:T(8,128)} %vol_hbm.1) | copy-start | bytes 1179652
  74.4 27.5 %all-to-all-start.3 = ((f32[4,8,96,256]{3,2,1,0:T(8,128)}), f32[4,8,96,256]{3,2,1,0:T(8,128)S(1)}, u32[]{:S(2)}, u32[]{:S(2)}) async-start(f32[4,8,96,256]{3,2,1,0:T(8,128)} %get-tuple-element.16), calls=%async_computation.3 | async-start | bytes 6291456 | tf_op jit(solution)/shard_map/all_to_all | solution.py:41
  81.8 4.3 %collective-permute-start.1 = (f32[1,1024]{1,0:T(1,128)S(1)}, f32[1,1024]{1,0:T(1,128)S(1)}, u32[]{:S(2)}, u32[]{:S(2)}) collective-permute-start(f32[1,1024]{1,0:T(1,128)S(1)} %get-tuple-element.14), channel_id=1, source_target_pairs={{1,0},{2,1},{3,2},{4,3},{5,4},{6,5},{7,6},{8,7},{9,8},{10,9},{11,1... | collective-permute-start | bytes 12296 | tf_op jit(solution)/shard_map/ppermute | solution.py:324
  83.1 3.8 %collective-permute-start.2 = (f32[1,1024]{1,0:T(1,128)S(1)}, f32[1,1024]{1,0:T(1,128)S(1)}, u32[]{:S(2)}, u32[]{:S(2)}) collective-permute-start(f32[1,1024]{1,0:T(1,128)S(1)} %get-tuple-element.15), channel_id=1, source_target_pairs={{0,1},{1,2},{2,3},{3,4},{4,5},{5,6},{6,7},{7,8},{8,9},{9,10},{10,1... | collective-permute-start | bytes 12296 | tf_op jit(solution)/shard_map/ppermute | solution.py:324

commit v12 on v11

--- a/solution.py
+++ b/solution.py
@@ -43,9 +43,19 @@
     )
 
 
+def far_partner(y):
+    return ((3 if y % 4 in (0, 3) else 7) - y) % NY
+
+
 def swap_far(value):
-    moves = [(device_of(y, x), device_of(y + BY, x)) for y in range(NY) for x in range(NX)]
-    return lax.ppermute(value, "xy", moves)
+    slabs = lax.axis_size("gz")
+    moves = [
+        (device_of(y + z % 2, x) * slabs + z, device_of(far_partner(y) + z % 2, x) * slabs + z)
+        for y in range(NY)
+        for x in range(NX)
+        for z in range(slabs)
+    ]
+    return lax.ppermute(value, ("xy", "gz"), moves)
 
 
 def split3(value):
@@ -67,10 +77,13 @@
 
 def near_far(owner, me, core):
     (y, x), (my_y, my_x) = shifted(owner, core), shifted(me, core)
-    near_y = (((y + 1) >> 1) + (my_y >> 1)) & 1
+    inner = ((y + 1) >> 1) & 1
+    near_y = inner ^ ((my_y >> 1) & 1)
+    upper = (y >> 2) ^ (inner & (y >> 1) & 1)
+    far_side = (((my_y & 6) + near_y + NY - 1) & (NY - 1)) >> 2
     near_x = (((x + 1) >> 1) + (my_x >> 1)) & 1
-    place = ((y + 1) & 1) * 2 + ((x + 1) & 1)
-    return near_y * 2 + near_x, place * FAR + (y >> 2)
+    place = (upper ^ far_side) * 2 + ((x + 1) & 1)
+    return near_y * 2 + near_x, place * FAR + (y & 1)
 
 
 def join3(product, rows):
@@ -203,7 +216,7 @@
 
 
 def my_half(me_ref, rows):
-    return pl.ds(pl.multiple_of((shifted(me_ref[0], me_ref[1])[0] >> 2) * rows, 8), rows)
+    return pl.ds(pl.multiple_of((shifted(me_ref[0], me_ref[1])[0] & 1) * rows, 8), rows)
 
 
 def gather_far_kernel(me_ref, in_ref, measured_ref, out_ref):

time: 106 us -> 104 us (0.981)
  waiting for transfers between devices: 24.8 us -> 22.2 us
  blocking collectives: 52.2 us -> 53.6 us
  starting transfers between devices: 15.9 us -> 14.8 us
    ppermute x1, waiting for transfers between devices: 10.2 us -> 7.61 us  [swap_far(): return lax.ppermute(value, ('xy', 'gz'), moves)]
    all_to_all x3, blocking collectives: 52.2 us -> 53.6 us  [exchange(): lax.all_to_all(value, ('xy', 'gz'), split_axis=0, concat_axis=0, axis_ind...]
where the time goes in v12:
time: 104 us
  blocking collectives  53.6 us (52%)
  waiting for transfers between devices  22.2 us (21%)
  starting transfers between devices  14.8 us (14%)
  Pallas kernels  11 us (11%)
  other arithmetic  1.25 us (1%)
    all_to_all x3, blocking collectives, exchange(): lax.all_to_all(value, ('xy', 'gz'), split_axis=0, concat_axis=0, axis_ind...  53.6 us
    all_to_all x1, waiting for transfers between devices, exchange(): lax.all_to_all(value, ('xy', 'gz'), split_axis=0, concat_axis=0, axis_ind...  13.8 us
    ppermute x1, waiting for transfers between devices, swap_far(): return lax.ppermute(value, ('xy', 'gz'), moves)  7.61 us
    all_to_all x1, starting transfers between devices, exchange(): lax.all_to_all(value, ('xy', 'gz'), split_axis=0, concat_axis=0, axis_ind...  6.41 us
    ppermute x1, starting transfers between devices, swap_far(): return lax.ppermute(value, ('xy', 'gz'), moves)  4.03 us
    pallas_call x1, Pallas kernels, back_project(): pl.pallas_call(back_kernel, out_shape=jax.ShapeDtypeStruct((rows, cols),...  4 us
    pallas_call x1, Pallas kernels, project(): pl.pallas_call(project_kernel, out_shape=[pltpu.VMEM((QUAD, SLOTS * rows...  3.34 us
    ppermute x1, starting transfers between devices, with_faces(): lax.ppermute(last, 'gz', up)  3.03 us
  transfers between devices with their start and end apart: 4, of which 3 were waited for; matrix products, arithmetic and copies ran while one was open for 1% of the time, Pallas kernels for 0%

profile of v12, /device:TPU:2, one launch (start us, length us, event | category | flops | bytes accessed | tf_op | source)
XLA Modules:
  0.0 103.5 jit_solution(1465646261312850364)
XLA Ops:
  0.6 0.1 pad_add_fusion.me_ref
  0.7 3.3 %shard_map.77 = (f32[4,776,256]{2,1,0:T(8,128)S(1)}, f32[1,1024]{1,0:T(1,128)S(1)}, f32[1,1024]{1,0:T(1,128)S(1)}) custom-call(s32[2]{0:T(128)S(1)} %pad_add_fusion.me_ref, s32[16,32]{1,0:T(8,128)} %bitcast.6, s32[1,32]{1,0:T(1,128)} %bitcast.8, s32[1,16]{1,0:T(1,128)} %starts_hbm.3, f32[96,1024]{1,0:T(8,128)} %vol_hbm.1, bf16[1,16,256,256]{3,2,1,0:T(8,128)(2,1)} %mats_hbm.3), custom_call_target="tpu_custom_call" | custom-call | tf_op jit(solution)/shard_map/pallas_call | solution.py:177
  4.1 28.6 %all_to_all.20.in_ref = f32[4,776,256]{2,1,0:T(8,128)S(1)} all-to-all(f32[4,776,256]{2,1,0:T(8,128)S(1)} %get-tuple-element.10), channel_id=1, replica_groups={{0,16,64,80},{32,48,96,112},{128,144,192,208},{160,176,224,240},{256,27..., dimensions={0} | all-to-all | bytes 6356992 | tf_op jit(solution)/shard_map/all_to_all | solution.py:41
  32.7 0.0 copy-start
  32.7 0.1 shard_map.78
  32.9 11.9 %all_to_all.21.in_ref = f32[4,200,256]{2,1,0:T(8,128)S(1)} all-to-all(f32[4,200,256]{2,1,0:T(8,128)S(1)} %shard_map.78), channel_id=1, replica_groups={{80,96,144,160},{112,64,176,128},{208,224,272,288},{240,192,304,256},{3..., dimensions={0} | all-to-all | bytes 1638400 | tf_op jit(solution)/shard_map/all_to_all | solution.py:41
  44.8 0.0 copy-done
  44.8 0.6 shard_map.79.own_ref
  45.4 4.0 %collective-permute-start = (f32[200,256]{1,0:T(8,128)S(1)}, f32[200,256]{1,0:T(8,128)S(1)}, u32[]{:S(2)}, u32[]{:S(2)}) collective-permute-start(f32[200,256]{1,0:T(8,128)S(1)} %shard_map.79.own_ref), channel_id=1, source_target_pairs={{0,192},{65,257},{2,194},{67,259},{4,196},{69,261},{6,198},{71,263... | collective-permute-start | bytes 614408 | tf_op jit(solution)/shard_map/ppermute | solution.py:58
  49.4 7.6 %collective-permute-done.came_ref = f32[200,256]{1,0:T(8,128)S(1)} collective-permute-done((f32[200,256]{1,0:T(8,128)S(1)}, f32[200,256]{1,0:T(8,128)S(1)}, u32[]{:S(2)}, u32[]{:S(2)}) %collective-permute-start) | collective-permute-done | bytes 204832 | tf_op jit(solution)/shard_map/ppermute | solution.py:58
  57.0 1.3 %shard_map.80 = (f32[4,192,256]{2,1,0:T(8,128)S(1)}, f32[96,256]{1,0:T(8,128)}) custom-call(s32[2]{0:T(128)S(1)} %pad_add_fusion.me_ref, f32[200,256]{1,0:T(8,128)S(1)} %shard_map.79.own_ref, f32[200,256]{1,0:T(8,128)S(1)} %collective-permute-done.came_ref), custom_call_target="tpu_custom_call" | custom-call | tf_op jit(solution)/shard_map/pallas_call | solution.py:254
  58.3 13.0 %all_to_all.22 = f32[4,192,256]{2,1,0:T(8,128)S(1)} all-to-all(f32[4,192,256]{2,1,0:T(8,128)S(1)} %get-tuple-element.11), channel_id=1, replica_groups={{80,96,144,160},{112,64,176,128},{208,224,272,288},{240,192,304,256},{3..., dimensions={0} | all-to-all | bytes 1572864 | tf_op jit(solution)/shard_map/all_to_all | solution.py:41
  71.3 1.7 %shard_map.81 = (f32[4,8,96,256]{3,2,1,0:T(8,128)}, f32[1,1024]{1,0:T(1,128)S(1)}, f32[1,1024]{1,0:T(1,128)S(1)}) custom-call(f32[8,96,256]{2,1,0:T(8,128)S(1)} %bitcast.5, f32[1,1024]{1,0:T(1,128)S(1)} %get-tuple-element.12.first_in, f32[1,1024]{1,0:T(1,128)S(1)} %get-tuple-element.13.last_in), custom_call_target="tpu_custom_call" | custom-call | tf_op jit(solution)/shard_map/pallas_call | solution.py:276
  73.0 0.0 copy-start.1
  73.0 6.4 %all-to-all-start.3 = ((f32[4,8,96,256]{3,2,1,0:T(8,128)}), f32[4,8,96,256]{3,2,1,0:T(8,128)S(1)}, u32[]{:S(2)}, u32[]{:S(2)}) async-start(f32[4,8,96,256]{3,2,1,0:T(8,128)} %get-tuple-element.16), calls=%async_computation.3 | async-start | bytes 6291456 | tf_op jit(solution)/shard_map/all_to_all | solution.py:41
  79.4 1.3 %collective-permute-start.1 = (f32[1,1024]{1,0:T(1,128)S(1)}, f32[1,1024]{1,0:T(1,128)S(1)}, u32[]{:S(2)}, u32[]{:S(2)}) collective-permute-start(f32[1,1024]{1,0:T(1,128)S(1)} %get-tuple-element.14), channel_id=1, source_target_pairs={{1,0},{2,1},{3,2},{4,3},{5,4},{6,5},{7,6},{8,7},{9,8},{10,9},{11,1... | collective-permute-start | bytes 12296 | tf_op jit(solution)/shard_map/ppermute | solution.py:337
  80.7 3.0 %collective-permute-start.2 = (f32[1,1024]{1,0:T(1,128)S(1)}, f32[1,1024]{1,0:T(1,128)S(1)}, u32[]{:S(2)}, u32[]{:S(2)}) collective-permute-start(f32[1,1024]{1,0:T(1,128)S(1)} %get-tuple-element.15), channel_id=1, source_target_pairs={{0,1},{1,2},{2,3},{3,4},{4,5},{5,6},{6,7},{7,8},{8,9},{9,10},{10,1... | collective-permute-start | bytes 12296 | tf_op jit(solution)/shard_map/ppermute | solution.py:337
  83.7 0.0 collective-permute-done.1
  83.7 0.8 collective-permute-done.2
  84.5 0.0 copy-done.1
  84.5 0.1 rsqrt_multiply_fusion
  84.6 1.1 %fusion.1.base_ref = f32[96,1024]{1,0:T(8,128)S(1)} fusion(f32[96,1024]{1,0:T(8,128)} %vol_hbm.1, f32[97,1024]{1,0:T(8,128)S(1)} %rsqrt_multiply_fusion), kind=kLoop, calls=%fused_computation.4 | loop fusion | flops 294912 | bytes 1572864 | tf_op jit(solution)/shard_map/sub | solution.py:358
  85.7 13.8 %all-to-all-done.3.got_ref = f32[4,8,96,256]{3,2,1,0:T(8,128)S(1)} async-done(((f32[4,8,96,256]{3,2,1,0:T(8,128)}), f32[4,8,96,256]{3,2,1,0:T(8,128)S(1)}, u32[]{:S(2)}, u32[]{:S(2)}) %all-to-all-start.3) | async-done | bytes 3145760 | tf_op jit(solution)/shard_map/all_to_all | solution.py:41
  99.5 4.0 %shard_map.82 = f32[96,1024]{1,0:T(8,128)} custom-call(s32[2]{0:T(128)S(1)} %pad_add_fusion.me_ref, s32[16,32]{1,0:T(8,128)} %bitcast.7, s32[1,32]{1,0:T(1,128)} %bitcast.9, s32[1,16]{1,0:T(1,128)} %starts_hbm.3, bf16[1,16,256,256]{3,2,1,0:T(8,128)(2,1)} %mats_hbm.3, f32[96,1024]{1,0:T(8,128)S(1)} %fusion.1.base_ref, ...), custom_call_target="tpu_custom_call" | custom-call | tf_op jit(solution)/shard_map/pallas_call | solution.py:320
Async XLA Ops:
  32.7 12.1 %copy-start = (f32[96,256]{1,0:T(8,128)S(1)}, f32[96,256]{1,0:T(8,128)}, u32[]{:S(2)}) copy-start(f32[96,256]{1,0:T(8,128)} %measured_ref.1) | copy-start | bytes 294916
  45.4 11.6 %collective-permute-start = (f32[200,256]{1,0:T(8,128)S(1)}, f32[200,256]{1,0:T(8,128)S(1)}, u32[]{:S(2)}, u32[]{:S(2)}) collective-permute-start(f32[200,256]{1,0:T(8,128)S(1)} %shard_map.79.own_ref), channel_id=1, source_target_pairs={{0,192},{65,257},{2,194},{67,259},{4,196},{69,261},{6,198},{71,263... | collective-permute-start | bytes 614408 | tf_op jit(solution)/shard_map/ppermute | solution.py:58
  73.0 11.6 %copy-start.1 = (f32[96,1024]{1,0:T(8,128)S(1)}, f32[96,1024]{1,0:T(8,128)}, u32[]{:S(2)}) copy-start(f32[96,1024]{1,0:T(8,128)} %vol_hbm.1) | copy-start | bytes 1179652
  73.0 26.5 %all-to-all-start.3 = ((f32[4,8,96,256]{3,2,1,0:T(8,128)}), f32[4,8,96,256]{3,2,1,0:T(8,128)S(1)}, u32[]{:S(2)}, u32[]{:S(2)}) async-start(f32[4,8,96,256]{3,2,1,0:T(8,128)} %get-tuple-element.16), calls=%async_computation.3 | async-start | bytes 6291456 | tf_op jit(solution)/shard_map/all_to_all | solution.py:41
  79.4 4.3 %collective-permute-start.1 = (f32[1,1024]{1,0:T(1,128)S(1)}, f32[1,1024]{1,0:T(1,128)S(1)}, u32[]{:S(2)}, u32[]{:S(2)}) collective-permute-start(f32[1,1024]{1,0:T(1,128)S(1)} %get-tuple-element.14), channel_id=1, source_target_pairs={{1,0},{2,1},{3,2},{4,3},{5,4},{6,5},{7,6},{8,7},{9,8},{10,9},{11,1... | collective-permute-start | bytes 12296 | tf_op jit(solution)/shard_map/ppermute | solution.py:337
  80.7 3.8 %collective-permute-start.2 = (f32[1,1024]{1,0:T(1,128)S(1)}, f32[1,1024]{1,0:T(1,128)S(1)}, u32[]{:S(2)}, u32[]{:S(2)}) collective-permute-start(f32[1,1024]{1,0:T(1,128)S(1)} %get-tuple-element.15), channel_id=1, source_target_pairs={{0,1},{1,2},{2,3},{3,4},{4,5},{5,6},{6,7},{7,8},{8,9},{9,10},{10,1... | collective-permute-start | bytes 12296 | tf_op jit(solution)/shard_map/ppermute | solution.py:337

commit v13 on v12

--- a/solution.py
+++ b/solution.py
@@ -238,49 +238,55 @@
     )(me, pinned(arrived, pltpu.VMEM), pinned(measured, pltpu.VMEM))
 
 
-def spread_far_kernel(me_ref, own_ref, came_ref, out_ref, mine_ref):
-    rows = mine_ref.shape[0]
+def spread_far_kernel(own_ref, came_ref, out_ref):
+    rows = out_ref.shape[1] // FAR
     both = own_ref[...] + came_ref[...]
     for half in range(FAR):
         at = FAR * rows + half
         value = both[half * rows : (half + 1) * rows] / both[at : at + 1]
         for place in range(QUAD):
             out_ref[place, half * rows : (half + 1) * rows] = value
-    mine_ref[...] = out_ref[0, my_half(me_ref, rows), :]
-
-
-def spread_far(me, own, came):
+
+
+def spread_far(own, came):
     rows = (own.shape[0] - 8) // FAR
     return pl.pallas_call(
         spread_far_kernel,
-        out_shape=[
-            pltpu.VMEM((QUAD, FAR * rows, W), jnp.float32),
-            jax.ShapeDtypeStruct((rows, W), jnp.float32),
-        ],
-        in_specs=[SMEM, VMEM, VMEM],
-        out_specs=[VMEM, VMEM],
-        compiler_params=PARAMS,
-    )(me, pinned(own, pltpu.VMEM), pinned(came, pltpu.VMEM))
-
-
-def spread_near_kernel(column_ref, first_in, last_in, out_hbm, first_ref, last_ref, sems):
-    copies = fetch_all([(column_ref, out_hbm.at[place]) for place in range(QUAD)], sems)
+        out_shape=pltpu.VMEM((QUAD, FAR * rows, W), jnp.float32),
+        in_specs=[VMEM, VMEM],
+        out_specs=VMEM,
+        compiler_params=PARAMS,
+    )(pinned(own, pltpu.VMEM), pinned(came, pltpu.VMEM))
+
+
+def spread_near_kernel(
+    me_ref, column_ref, far_ref, first_in, last_in, out_hbm, mine_hbm, first_ref, last_ref, sems
+):
+    mine = far_ref.at[0, my_half(me_ref, mine_hbm.shape[0])]
+    copies = fetch_all(
+        [(column_ref, out_hbm.at[place]) for place in range(QUAD)] + [(mine, mine_hbm)], sems
+    )
     first_ref[...] = first_in[...]
     last_ref[...] = last_in[...]
     for copy in copies:
         copy.wait()
 
 
-def spread_near(column, first, last):
+def spread_near(me, column, far, first, last):
     face = jax.ShapeDtypeStruct(first.shape, jnp.float32)
     return pl.pallas_call(
         spread_near_kernel,
-        out_shape=[pltpu.HBM((QUAD,) + column.shape, jnp.float32), face, face],
-        in_specs=[VMEM] * 3,
-        out_specs=[ANY, VMEM, VMEM],
-        scratch_shapes=[pltpu.SemaphoreType.DMA((QUAD,))],
-        compiler_params=PARAMS,
-    )(*(pinned(a, pltpu.VMEM) for a in (column, first, last)))
+        out_shape=[
+            pltpu.HBM((QUAD,) + column.shape, jnp.float32),
+            pltpu.HBM(column.shape[1:], jnp.float32),
+            face,
+            face,
+        ],
+        in_specs=[SMEM] + [VMEM] * 4,
+        out_specs=[ANY, ANY, VMEM, VMEM],
+        scratch_shapes=[pltpu.SemaphoreType.DMA((QUAD + 1,))],
+        compiler_params=PARAMS,
+    )(me, *(pinned(a, pltpu.VMEM) for a in (column, far, first, last)))
 
 
 def back_kernel(
@@ -352,9 +358,9 @@
     plan = (me, ray_lists.T, owner_map.reshape(1, -1), offsets)
     outgoing, first, last = project(*plan, volume, ray_mats)
     part = gather_far(me, exchange(gather_near(exchange(outgoing, 1)), 2), sinogram)
-    spread, weighted = spread_far(me, part, swap_far(part))
-    column = exchange(spread, 2).reshape(SLOTS, rows, W)
-    spread, first, last = spread_near(column, first, last)
+    far = spread_far(part, swap_far(part))
+    column = exchange(far, 2).reshape(SLOTS, rows, W)
+    spread, weighted, first, last = spread_near(me, column, far, first, last)
     base = volume - tv_weight * total_variation(with_faces(volume, first, last))
     got = exchange(spread, 1)
     new_volume = back_project(*plan, base, ray_mats, got)

time: 104 us -> 103 us (level)
    pallas_call x1, Pallas kernels: 1.27 us -> 0.07 us  [spread_far(): pl.pallas_call(spread_far_kernel, out_shape=pltpu.VMEM((QUAD, FAR * rows,...]
where the time goes in v13:
time: 103 us
  blocking collectives  53.6 us (52%)
  waiting for transfers between devices  22.2 us (22%)
  starting transfers between devices  14.7 us (14%)
  Pallas kernels  10.4 us (10%)
  other arithmetic  1.25 us (1%)
    all_to_all x3, blocking collectives, exchange(): lax.all_to_all(value, ('xy', 'gz'), split_axis=0, concat_axis=0, axis_ind...  53.6 us
    all_to_all x1, waiting for transfers between devices, exchange(): lax.all_to_all(value, ('xy', 'gz'), split_axis=0, concat_axis=0, axis_ind...  13.8 us
    ppermute x1, waiting for transfers between devices, swap_far(): return lax.ppermute(value, ('xy', 'gz'), moves)  7.6 us
    all_to_all x1, starting transfers between devices, exchange(): lax.all_to_all(value, ('xy', 'gz'), split_axis=0, concat_axis=0, axis_ind...  6.4 us
    ppermute x1, starting transfers between devices, swap_far(): return lax.ppermute(value, ('xy', 'gz'), moves)  4.03 us
    pallas_call x1, Pallas kernels, back_project(): pl.pallas_call(back_kernel, out_shape=jax.ShapeDtypeStruct((rows, cols),...  4.01 us
    pallas_call x1, Pallas kernels, project(): pl.pallas_call(project_kernel, out_shape=[pltpu.VMEM((QUAD, SLOTS * rows...  3.36 us
    ppermute x1, starting transfers between devices, with_faces(): lax.ppermute(last, 'gz', up)  3.03 us
  transfers between devices with their start and end apart: 4, of which 3 were waited for; matrix products, arithmetic and copies ran while one was open for 1% of the time, Pallas kernels for 0%

profile of v13, /device:TPU:2, one launch (start us, length us, event | category | flops | bytes accessed | tf_op | source)
XLA Modules:
  0.0 102.9 jit_solution(15125010377894738845)
XLA Ops:
  0.6 0.1 pad_add_fusion.me_ref
  0.7 3.4 %shard_map.77 = (f32[4,776,256]{2,1,0:T(8,128)S(1)}, f32[1,1024]{1,0:T(1,128)S(1)}, f32[1,1024]{1,0:T(1,128)S(1)}) custom-call(s32[2]{0:T(128)S(1)} %pad_add_fusion.me_ref, s32[16,32]{1,0:T(8,128)} %bitcast.6, s32[1,32]{1,0:T(1,128)} %bitcast.8, s32[1,16]{1,0:T(1,128)} %starts_hbm.3, f32[96,1024]{1,0:T(8,128)} %vol_hbm.1, bf16[1,16,256,256]{3,2,1,0:T(8,128)(2,1)} %mats_hbm.3), custom_call_target="tpu_custom_call" | custom-call | tf_op jit(solution)/shard_map/pallas_call | solution.py:177
  4.1 28.6 %all_to_all.20.in_ref = f32[4,776,256]{2,1,0:T(8,128)S(1)} all-to-all(f32[4,776,256]{2,1,0:T(8,128)S(1)} %get-tuple-element.9), channel_id=1, replica_groups={{0,16,64,80},{32,48,96,112},{128,144,192,208},{160,176,224,240},{256,27..., dimensions={0} | all-to-all | bytes 6356992 | tf_op jit(solution)/shard_map/all_to_all | solution.py:41
  32.7 0.0 copy-start
  32.7 0.1 shard_map.78
  32.9 11.9 %all_to_all.21.in_ref = f32[4,200,256]{2,1,0:T(8,128)S(1)} all-to-all(f32[4,200,256]{2,1,0:T(8,128)S(1)} %shard_map.78), channel_id=1, replica_groups={{80,96,144,160},{112,64,176,128},{208,224,272,288},{240,192,304,256},{3..., dimensions={0} | all-to-all | bytes 1638400 | tf_op jit(solution)/shard_map/all_to_all | solution.py:41
  44.8 0.0 copy-done
  44.8 0.6 shard_map.79.own_ref
  45.4 4.0 %collective-permute-start = (f32[200,256]{1,0:T(8,128)S(1)}, f32[200,256]{1,0:T(8,128)S(1)}, u32[]{:S(2)}, u32[]{:S(2)}) collective-permute-start(f32[200,256]{1,0:T(8,128)S(1)} %shard_map.79.own_ref), channel_id=1, source_target_pairs={{0,192},{65,257},{2,194},{67,259},{4,196},{69,261},{6,198},{71,263... | collective-permute-start | bytes 614408 | tf_op jit(solution)/shard_map/ppermute | solution.py:58
  49.4 7.6 %collective-permute-done.came_ref = f32[200,256]{1,0:T(8,128)S(1)} collective-permute-done((f32[200,256]{1,0:T(8,128)S(1)}, f32[200,256]{1,0:T(8,128)S(1)}, u32[]{:S(2)}, u32[]{:S(2)}) %collective-permute-start) | collective-permute-done | bytes 204832 | tf_op jit(solution)/shard_map/ppermute | solution.py:58
  57.0 0.1 shard_map.80.far_ref
  57.1 13.0 %all_to_all.22 = f32[4,192,256]{2,1,0:T(8,128)S(1)} all-to-all(f32[4,192,256]{2,1,0:T(8,128)S(1)} %shard_map.80.far_ref), channel_id=1, replica_groups={{80,96,144,160},{112,64,176,128},{208,224,272,288},{240,192,304,256},{3..., dimensions={0} | all-to-all | bytes 1572864 | tf_op jit(solution)/shard_map/all_to_all | solution.py:41
  70.1 2.3 %shard_map.81 = (f32[4,8,96,256]{3,2,1,0:T(8,128)}, f32[96,256]{1,0:T(8,128)}, f32[1,1024]{1,0:T(1,128)S(1)}, f32[1,1024]{1,0:T(1,128)S(1)}) custom-call(s32[2]{0:T(128)S(1)} %pad_add_fusion.me_ref, f32[8,96,256]{2,1,0:T(8,128)S(1)} %bitcast.5, f32[4,192,256]{2,1,0:T(8,128)S(1)} %shard_map.80.far_ref, f32[1,1024]{1,0:T(1,128)S(1)} %get-tuple-element.10.first_in, ...), custom_call_target="tpu_custom_call" | custom-call | tf_op jit(solution)/shard_map/pallas_call | solution.py:277
  72.4 0.0 copy-start.1
  72.4 6.4 %all-to-all-start.3 = ((f32[4,8,96,256]{3,2,1,0:T(8,128)}), f32[4,8,96,256]{3,2,1,0:T(8,128)S(1)}, u32[]{:S(2)}, u32[]{:S(2)}) async-start(f32[4,8,96,256]{3,2,1,0:T(8,128)} %get-tuple-element.14), calls=%async_computation.3 | async-start | bytes 6291456 | tf_op jit(solution)/shard_map/all_to_all | solution.py:41
  78.8 1.3 %collective-permute-start.1 = (f32[1,1024]{1,0:T(1,128)S(1)}, f32[1,1024]{1,0:T(1,128)S(1)}, u32[]{:S(2)}, u32[]{:S(2)}) collective-permute-start(f32[1,1024]{1,0:T(1,128)S(1)} %get-tuple-element.12), channel_id=1, source_target_pairs={{1,0},{2,1},{3,2},{4,3},{5,4},{6,5},{7,6},{8,7},{9,8},{10,9},{11,1... | collective-permute-start | bytes 12296 | tf_op jit(solution)/shard_map/ppermute | solution.py:343
  80.1 3.0 %collective-permute-start.2 = (f32[1,1024]{1,0:T(1,128)S(1)}, f32[1,1024]{1,0:T(1,128)S(1)}, u32[]{:S(2)}, u32[]{:S(2)}) collective-permute-start(f32[1,1024]{1,0:T(1,128)S(1)} %get-tuple-element.13), channel_id=1, source_target_pairs={{0,1},{1,2},{2,3},{3,4},{4,5},{5,6},{6,7},{7,8},{8,9},{9,10},{10,1... | collective-permute-start | bytes 12296 | tf_op jit(solution)/shard_map/ppermute | solution.py:343
  83.1 0.0 collective-permute-done.1
  83.1 0.8 collective-permute-done.2
  83.9 0.0 copy-done.1
  83.9 0.1 rsqrt_multiply_fusion
  84.0 1.1 %fusion.1.base_ref = f32[96,1024]{1,0:T(8,128)S(1)} fusion(f32[96,1024]{1,0:T(8,128)} %vol_hbm.1, f32[97,1024]{1,0:T(8,128)S(1)} %rsqrt_multiply_fusion), kind=kLoop, calls=%fused_computation.4 | loop fusion | flops 294912 | bytes 1572864 | tf_op jit(solution)/shard_map/sub | solution.py:364
  85.1 13.8 %all-to-all-done.3.got_ref = f32[4,8,96,256]{3,2,1,0:T(8,128)S(1)} async-done(((f32[4,8,96,256]{3,2,1,0:T(8,128)}), f32[4,8,96,256]{3,2,1,0:T(8,128)S(1)}, u32[]{:S(2)}, u32[]{:S(2)}) %all-to-all-start.3) | async-done | bytes 3145760 | tf_op jit(solution)/shard_map/all_to_all | solution.py:41
  98.9 4.0 %shard_map.82 = f32[96,1024]{1,0:T(8,128)} custom-call(s32[2]{0:T(128)S(1)} %pad_add_fusion.me_ref, s32[16,32]{1,0:T(8,128)} %bitcast.7, s32[1,32]{1,0:T(1,128)} %bitcast.9, s32[1,16]{1,0:T(1,128)} %starts_hbm.3, bf16[1,16,256,256]{3,2,1,0:T(8,128)(2,1)} %mats_hbm.3, f32[96,1024]{1,0:T(8,128)S(1)} %fusion.1.base_ref, ...), custom_call_target="tpu_custom_call" | custom-call | tf_op jit(solution)/shard_map/pallas_call | solution.py:326
Async XLA Ops:
  32.7 12.1 %copy-start = (f32[96,256]{1,0:T(8,128)S(1)}, f32[96,256]{1,0:T(8,128)}, u32[]{:S(2)}) copy-start(f32[96,256]{1,0:T(8,128)} %measured_ref.1) | copy-start | bytes 294916
  45.4 11.6 %collective-permute-start = (f32[200,256]{1,0:T(8,128)S(1)}, f32[200,256]{1,0:T(8,128)S(1)}, u32[]{:S(2)}, u32[]{:S(2)}) collective-permute-start(f32[200,256]{1,0:T(8,128)S(1)} %shard_map.79.own_ref), channel_id=1, source_target_pairs={{0,192},{65,257},{2,194},{67,259},{4,196},{69,261},{6,198},{71,263... | collective-permute-start | bytes 614408 | tf_op jit(solution)/shard_map/ppermute | solution.py:58
  72.4 11.6 %copy-start.1 = (f32[96,1024]{1,0:T(8,128)S(1)}, f32[96,1024]{1,0:T(8,128)}, u32[]{:S(2)}) copy-start(f32[96,1024]{1,0:T(8,128)} %vol_hbm.1) | copy-start | bytes 1179652
  72.4 26.5 %all-to-all-start.3 = ((f32[4,8,96,256]{3,2,1,0:T(8,128)}), f32[4,8,96,256]{3,2,1,0:T(8,128)S(1)}, u32[]{:S(2)}, u32[]{:S(2)}) async-start(f32[4,8,96,256]{3,2,1,0:T(8,128)} %get-tuple-element.14), calls=%async_computation.3 | async-start | bytes 6291456 | tf_op jit(solution)/shard_map/all_to_all | solution.py:41
  78.8 4.3 %collective-permute-start.1 = (f32[1,1024]{1,0:T(1,128)S(1)}, f32[1,1024]{1,0:T(1,128)S(1)}, u32[]{:S(2)}, u32[]{:S(2)}) collective-permute-start(f32[1,1024]{1,0:T(1,128)S(1)} %get-tuple-element.12), channel_id=1, source_target_pairs={{1,0},{2,1},{3,2},{4,3},{5,4},{6,5},{7,6},{8,7},{9,8},{10,9},{11,1... | collective-permute-start | bytes 12296 | tf_op jit(solution)/shard_map/ppermute | solution.py:343
  80.1 3.8 %collective-permute-start.2 = (f32[1,1024]{1,0:T(1,128)S(1)}, f32[1,1024]{1,0:T(1,128)S(1)}, u32[]{:S(2)}, u32[]{:S(2)}) collective-permute-start(f32[1,1024]{1,0:T(1,128)S(1)} %get-tuple-element.13), channel_id=1, source_target_pairs={{0,1},{1,2},{2,3},{3,4},{4,5},{5,6},{6,7},{7,8},{8,9},{9,10},{10,1... | collective-permute-start | bytes 12296 | tf_op jit(solution)/shard_map/ppermute | solution.py:343

commit v14 on v13

--- a/solution.py
+++ b/solution.py
@@ -243,7 +243,7 @@
     both = own_ref[...] + came_ref[...]
     for half in range(FAR):
         at = FAR * rows + half
-        value = both[half * rows : (half + 1) * rows] / both[at : at + 1]
+        value = both[half * rows : (half + 1) * rows] * (1.0 / both[at : at + 1])
         for place in range(QUAD):
             out_ref[place, half * rows : (half + 1) * rows] = value
 
@@ -315,8 +315,8 @@
         value = jnp.concatenate([join3(product, rows), product[3 * rows : 3 * rows + 8]], axis=0)
         value = jnp.concatenate([value, jnp.zeros((rows + 8, LANES), jnp.float32)], axis=1)
         total[:, pl.ds(base, W + LANES)] += pltpu.roll(value, start & (LANES - 1), 1)
-    column = jnp.maximum(total[rows : rows + 1, :cols], 1.0)
-    out_ref[...] = base_ref[...] + relax * (total[:rows, :cols] / column)
+    scale = relax / jnp.maximum(total[rows : rows + 1, :cols], 1.0)
+    out_ref[...] = base_ref[...] + total[:rows, :cols] * scale
 
 
 def back_project(me, lists, owners, starts, base, mats, got):

time: 103 us -> 103 us (level)
  no operation moved by 1% of the time
where the time goes in v14:
time: 103 us
  blocking collectives  53.6 us (52%)
  waiting for transfers between devices  22.2 us (22%)
  starting transfers between devices  14.8 us (14%)
  Pallas kernels  10.4 us (10%)
  other arithmetic  1.25 us (1%)
    all_to_all x3, blocking collectives, exchange(): lax.all_to_all(value, ('xy', 'gz'), split_axis=0, concat_axis=0, axis_ind...  53.6 us
    all_to_all x1, waiting for transfers between devices, exchange(): lax.all_to_all(value, ('xy', 'gz'), split_axis=0, concat_axis=0, axis_ind...  13.8 us
    ppermute x1, waiting for transfers between devices, swap_far(): return lax.ppermute(value, ('xy', 'gz'), moves)  7.6 us
    all_to_all x1, starting transfers between devices, exchange(): lax.all_to_all(value, ('xy', 'gz'), split_axis=0, concat_axis=0, axis_ind...  6.41 us
    ppermute x1, starting transfers between devices, swap_far(): return lax.ppermute(value, ('xy', 'gz'), moves)  4.04 us
    pallas_call x1, Pallas kernels, back_project(): pl.pallas_call(back_kernel, out_shape=jax.ShapeDtypeStruct((rows, cols),...  4.01 us
    pallas_call x1, Pallas kernels, project(): pl.pallas_call(project_kernel, out_shape=[pltpu.VMEM((QUAD, SLOTS * rows...  3.34 us
    ppermute x1, starting transfers between devices, with_faces(): lax.ppermute(last, 'gz', up)  3.03 us
  transfers between devices with their start and end apart: 4, of which 3 were waited for; matrix products, arithmetic and copies ran while one was open for 1% of the time, Pallas kernels for 0%

profile of v14, /device:TPU:2, one launch (start us, length us, event | category | flops | bytes accessed | tf_op | source)
XLA Modules:
  0.0 102.9 jit_solution(17917817477912998432)
XLA Ops:
  0.6 0.1 pad_add_fusion.me_ref
  0.7 3.3 %shard_map.77 = (f32[4,776,256]{2,1,0:T(8,128)S(1)}, f32[1,1024]{1,0:T(1,128)S(1)}, f32[1,1024]{1,0:T(1,128)S(1)}) custom-call(s32[2]{0:T(128)S(1)} %pad_add_fusion.me_ref, s32[16,32]{1,0:T(8,128)} %bitcast.6, s32[1,32]{1,0:T(1,128)} %bitcast.8, s32[1,16]{1,0:T(1,128)} %starts_hbm.3, f32[96,1024]{1,0:T(8,128)} %vol_hbm.1, bf16[1,16,256,256]{3,2,1,0:T(8,128)(2,1)} %mats_hbm.3), custom_call_target="tpu_custom_call" | custom-call | tf_op jit(solution)/shard_map/pallas_call | solution.py:177
  4.1 28.7 %all_to_all.20.in_ref = f32[4,776,256]{2,1,0:T(8,128)S(1)} all-to-all(f32[4,776,256]{2,1,0:T(8,128)S(1)} %get-tuple-element.9), channel_id=1, replica_groups={{0,16,64,80},{32,48,96,112},{128,144,192,208},{160,176,224,240},{256,27..., dimensions={0} | all-to-all | bytes 6356992 | tf_op jit(solution)/shard_map/all_to_all | solution.py:41
  32.7 0.0 copy-start
  32.7 0.1 shard_map.78
  32.9 11.9 %all_to_all.21.in_ref = f32[4,200,256]{2,1,0:T(8,128)S(1)} all-to-all(f32[4,200,256]{2,1,0:T(8,128)S(1)} %shard_map.78), channel_id=1, replica_groups={{80,96,144,160},{112,64,176,128},{208,224,272,288},{240,192,304,256},{3..., dimensions={0} | all-to-all | bytes 1638400 | tf_op jit(solution)/shard_map/all_to_all | solution.py:41
  44.8 0.0 copy-done
  44.8 0.6 shard_map.79.own_ref
  45.4 4.0 %collective-permute-start = (f32[200,256]{1,0:T(8,128)S(1)}, f32[200,256]{1,0:T(8,128)S(1)}, u32[]{:S(2)}, u32[]{:S(2)}) collective-permute-start(f32[200,256]{1,0:T(8,128)S(1)} %shard_map.79.own_ref), channel_id=1, source_target_pairs={{0,192},{65,257},{2,194},{67,259},{4,196},{69,261},{6,198},{71,263... | collective-permute-start | bytes 614408 | tf_op jit(solution)/shard_map/ppermute | solution.py:58
  49.4 7.6 %collective-permute-done.came_ref = f32[200,256]{1,0:T(8,128)S(1)} collective-permute-done((f32[200,256]{1,0:T(8,128)S(1)}, f32[200,256]{1,0:T(8,128)S(1)}, u32[]{:S(2)}, u32[]{:S(2)}) %collective-permute-start) | collective-permute-done | bytes 204832 | tf_op jit(solution)/shard_map/ppermute | solution.py:58
  57.0 0.1 shard_map.80.far_ref
  57.1 13.0 %all_to_all.22 = f32[4,192,256]{2,1,0:T(8,128)S(1)} all-to-all(f32[4,192,256]{2,1,0:T(8,128)S(1)} %shard_map.80.far_ref), channel_id=1, replica_groups={{80,96,144,160},{112,64,176,128},{208,224,272,288},{240,192,304,256},{3..., dimensions={0} | all-to-all | bytes 1572864 | tf_op jit(solution)/shard_map/all_to_all | solution.py:41
  70.1 2.3 %shard_map.81 = (f32[4,8,96,256]{3,2,1,0:T(8,128)}, f32[96,256]{1,0:T(8,128)}, f32[1,1024]{1,0:T(1,128)S(1)}, f32[1,1024]{1,0:T(1,128)S(1)}) custom-call(s32[2]{0:T(128)S(1)} %pad_add_fusion.me_ref, f32[8,96,256]{2,1,0:T(8,128)S(1)} %bitcast.5, f32[4,192,256]{2,1,0:T(8,128)S(1)} %shard_map.80.far_ref, f32[1,1024]{1,0:T(1,128)S(1)} %get-tuple-element.10.first_in, ...), custom_call_target="tpu_custom_call" | custom-call | tf_op jit(solution)/shard_map/pallas_call | solution.py:277
  72.4 0.0 copy-start.1
  72.4 6.4 %all-to-all-start.3 = ((f32[4,8,96,256]{3,2,1,0:T(8,128)}), f32[4,8,96,256]{3,2,1,0:T(8,128)S(1)}, u32[]{:S(2)}, u32[]{:S(2)}) async-start(f32[4,8,96,256]{3,2,1,0:T(8,128)} %get-tuple-element.14), calls=%async_computation.3 | async-start | bytes 6291456 | tf_op jit(solution)/shard_map/all_to_all | solution.py:41
  78.8 1.3 %collective-permute-start.1 = (f32[1,1024]{1,0:T(1,128)S(1)}, f32[1,1024]{1,0:T(1,128)S(1)}, u32[]{:S(2)}, u32[]{:S(2)}) collective-permute-start(f32[1,1024]{1,0:T(1,128)S(1)} %get-tuple-element.12), channel_id=1, source_target_pairs={{1,0},{2,1},{3,2},{4,3},{5,4},{6,5},{7,6},{8,7},{9,8},{10,9},{11,1... | collective-permute-start | bytes 12296 | tf_op jit(solution)/shard_map/ppermute | solution.py:343
  80.1 3.0 %collective-permute-start.2 = (f32[1,1024]{1,0:T(1,128)S(1)}, f32[1,1024]{1,0:T(1,128)S(1)}, u32[]{:S(2)}, u32[]{:S(2)}) collective-permute-start(f32[1,1024]{1,0:T(1,128)S(1)} %get-tuple-element.13), channel_id=1, source_target_pairs={{0,1},{1,2},{2,3},{3,4},{4,5},{5,6},{6,7},{7,8},{8,9},{9,10},{10,1... | collective-permute-start | bytes 12296 | tf_op jit(solution)/shard_map/ppermute | solution.py:343
  83.1 0.0 collective-permute-done.1
  83.1 0.8 collective-permute-done.2
  83.9 0.0 copy-done.1
  83.9 0.1 rsqrt_multiply_fusion
  84.0 1.1 %fusion.1.base_ref = f32[96,1024]{1,0:T(8,128)S(1)} fusion(f32[96,1024]{1,0:T(8,128)} %vol_hbm.1, f32[97,1024]{1,0:T(8,128)S(1)} %rsqrt_multiply_fusion), kind=kLoop, calls=%fused_computation.4 | loop fusion | flops 294912 | bytes 1572864 | tf_op jit(solution)/shard_map/sub | solution.py:364
  85.1 13.8 %all-to-all-done.3.got_ref = f32[4,8,96,256]{3,2,1,0:T(8,128)S(1)} async-done(((f32[4,8,96,256]{3,2,1,0:T(8,128)}), f32[4,8,96,256]{3,2,1,0:T(8,128)S(1)}, u32[]{:S(2)}, u32[]{:S(2)}) %all-to-all-start.3) | async-done | bytes 3145760 | tf_op jit(solution)/shard_map/all_to_all | solution.py:41
  98.9 4.0 %shard_map.82 = f32[96,1024]{1,0:T(8,128)} custom-call(s32[2]{0:T(128)S(1)} %pad_add_fusion.me_ref, s32[16,32]{1,0:T(8,128)} %bitcast.7, s32[1,32]{1,0:T(1,128)} %bitcast.9, s32[1,16]{1,0:T(1,128)} %starts_hbm.3, bf16[1,16,256,256]{3,2,1,0:T(8,128)(2,1)} %mats_hbm.3, f32[96,1024]{1,0:T(8,128)S(1)} %fusion.1.base_ref, ...), custom_call_target="tpu_custom_call" | custom-call | tf_op jit(solution)/shard_map/pallas_call | solution.py:326
Async XLA Ops:
  32.7 12.1 %copy-start = (f32[96,256]{1,0:T(8,128)S(1)}, f32[96,256]{1,0:T(8,128)}, u32[]{:S(2)}) copy-start(f32[96,256]{1,0:T(8,128)} %measured_ref.1) | copy-start | bytes 294916
  45.4 11.6 %collective-permute-start = (f32[200,256]{1,0:T(8,128)S(1)}, f32[200,256]{1,0:T(8,128)S(1)}, u32[]{:S(2)}, u32[]{:S(2)}) collective-permute-start(f32[200,256]{1,0:T(8,128)S(1)} %shard_map.79.own_ref), channel_id=1, source_target_pairs={{0,192},{65,257},{2,194},{67,259},{4,196},{69,261},{6,198},{71,263... | collective-permute-start | bytes 614408 | tf_op jit(solution)/shard_map/ppermute | solution.py:58
  72.4 11.6 %copy-start.1 = (f32[96,1024]{1,0:T(8,128)S(1)}, f32[96,1024]{1,0:T(8,128)}, u32[]{:S(2)}) copy-start(f32[96,1024]{1,0:T(8,128)} %vol_hbm.1) | copy-start | bytes 1179652
  72.4 26.5 %all-to-all-start.3 = ((f32[4,8,96,256]{3,2,1,0:T(8,128)}), f32[4,8,96,256]{3,2,1,0:T(8,128)S(1)}, u32[]{:S(2)}, u32[]{:S(2)}) async-start(f32[4,8,96,256]{3,2,1,0:T(8,128)} %get-tuple-element.14), calls=%async_computation.3 | async-start | bytes 6291456 | tf_op jit(solution)/shard_map/all_to_all | solution.py:41
  78.8 4.3 %collective-permute-start.1 = (f32[1,1024]{1,0:T(1,128)S(1)}, f32[1,1024]{1,0:T(1,128)S(1)}, u32[]{:S(2)}, u32[]{:S(2)}) collective-permute-start(f32[1,1024]{1,0:T(1,128)S(1)} %get-tuple-element.12), channel_id=1, source_target_pairs={{1,0},{2,1},{3,2},{4,3},{5,4},{6,5},{7,6},{8,7},{9,8},{10,9},{11,1... | collective-permute-start | bytes 12296 | tf_op jit(solution)/shard_map/ppermute | solution.py:343
  80.1 3.8 %collective-permute-start.2 = (f32[1,1024]{1,0:T(1,128)S(1)}, f32[1,1024]{1,0:T(1,128)S(1)}, u32[]{:S(2)}, u32[]{:S(2)}) collective-permute-start(f32[1,1024]{1,0:T(1,128)S(1)} %get-tuple-element.13), channel_id=1, source_target_pairs={{0,1},{1,2},{2,3},{3,4},{4,5},{5,6},{6,7},{7,8},{8,9},{9,10},{10,1... | collective-permute-start | bytes 12296 | tf_op jit(solution)/shard_map/ppermute | solution.py:343
